TPU v7x, 512 devices: a whole 4x8x8 slice. The times are simulated.
512 devices in a mesh: tm: 8 (over x, core), row: 64 (over y, z).
Axes of the slice: x: 4, y: 8, z: 8, core: 2. Of those that a mesh axis runs over, the one named last changes fastest.
Arguments:
- forcing: float32 [8, 2048, 2048], P('tm', 'row'), may hold values from -6 to 6
- rate_class: int32 [2048, 2048], P('row'), may hold values from 0 to 15
- rate_table: float32 [16], replicated, may hold values from 0.95 to 0.999
- row_class: int32 [2048], replicated, may hold values from 0 to 1
- col_class: int32 [2048], replicated, may hold values from 0 to 1
- inverse_offsets: float32 [2, 512, 512], P(None, 'row'), may hold values from -0.25 to 0.25
Outputs:
- covariance_field: float32 [8, 2048, 2048], P('tm', 'row')
- adjoint_field: float32 [8, 2048, 2048], P('tm', 'row')
All inputs are finite; a program needn't handle non-finite values.
Results may differ from a plain program's by a relative error of at most 0.0001.
Values sent between devices are 32-bit elements; how exact they have to be, the bound alone decides.
No kernel may reach another device: no remote copies, remote signals or barrier semaphores. Data moves between devices by JAX's collectives and lax.ppermute only.
A program may use at most 64 MiB of HBM per device.

v0:
```python
import jax
import jax.numpy as jnp
from jax import lax
from jax.sharding import PartitionSpec as P


def carried_in(part, axis, combine, identity, reverse):
    count = lax.axis_size(axis)
    place = lax.axis_index(axis)
    ahead = count - 1 - place if reverse else place
    gathered = jax.tree.map(lambda a: lax.all_gather(a, axis), part)
    state = jax.tree.map(lambda a, e: jnp.zeros_like(a) + jnp.asarray(e, a.dtype), part, identity)

    def one(turn, state):
        source = count - 1 - turn if reverse else turn
        return combine(
            state, jax.tree.map(lambda a: lax.dynamic_index_in_dim(a, source, 0, False), gathered)
        )

    return lax.fori_loop(0, ahead, one, state)


def lookup(labels, table):
    result = jnp.zeros(labels.shape, jnp.float32)
    for table_row in range(table.shape[0]):
        result = jnp.where(labels == table_row, table[table_row], result)
    return result


def rows_forward(forcing, offsets, my_rows):
    steps_here, row_count, grid_size = forcing.shape
    block_size = offsets.shape[1]
    pieces = forcing.reshape(steps_here, row_count, grid_size // block_size, block_size)

    def apply_class(category):
        return jnp.einsum(
            "trbi,ij->tbjr", pieces, offsets[category], precision=lax.Precision.HIGHEST
        )

    result = apply_class(0)
    category = 1
    result = jnp.where((my_rows == category).reshape(1, 1, 1, -1), apply_class(category), result)
    result = result + pieces.transpose(0, 2, 3, 1)
    return result.reshape(steps_here, grid_size, row_count)


def rows_adjoint(spread, offsets, my_rows):
    steps_here, grid_size, row_count = spread.shape
    block_size = offsets.shape[1]
    pieces = spread.reshape(steps_here, grid_size // block_size, block_size, row_count)

    def apply_class(category):
        return jnp.einsum(
            "tbjr,ij->trbi", pieces, offsets[category], precision=lax.Precision.HIGHEST
        )

    result = apply_class(0)
    category = 1
    result = jnp.where((my_rows == category).reshape(1, -1, 1, 1), apply_class(category), result)
    result = result + pieces.transpose(0, 3, 1, 2)
    return result.reshape(steps_here, row_count, grid_size)


def columns_apply(items, offsets, my_cols, adjoint):
    count_items, col_count, grid_size = items.shape
    block_size = offsets.shape[1]
    pieces = items.reshape(count_items, col_count, grid_size // block_size, block_size)
    pattern = "tcbj,ij->tcbi" if adjoint else "tcbi,ij->tcbj"

    def apply_class(category):
        return jnp.einsum(pattern, pieces, offsets[category], precision=lax.Precision.HIGHEST)

    result = apply_class(0)
    category = 1
    result = jnp.where((my_cols == category).reshape(1, -1, 1, 1), apply_class(category), result)
    result = result + pieces
    return result.reshape(count_items, col_count, grid_size)


def to_rows(column_field):
    return lax.all_to_all(column_field, "row", split_axis=2, concat_axis=1, tiled=True)


def affine_join(earlier, latter):
    return (earlier[0] * latter[0], latter[0] * earlier[1] + latter[1])


def forward_link(span, final_state):
    identity_pair = (jnp.ones_like(span), jnp.zeros_like(final_state))
    _, incoming = carried_in((span, final_state), "tm", affine_join, identity_pair, False)
    return incoming


def adjoint_link(span, first_state):
    identity_pair = (jnp.ones_like(span), jnp.zeros_like(first_state))
    _, incoming = carried_in((span, first_state), "tm", affine_join, identity_pair, True)
    return incoming


def chain_powers(decays):
    running = jnp.ones_like(decays)
    running = running * decays
    powers = [running]
    return powers


def forward_full(source, decays, scaled):
    carried = jnp.zeros_like(decays)
    carried = decays * carried + scaled * source[0]
    powers = chain_powers(decays)
    incoming = forward_link(powers[-1], carried)
    return jnp.stack([carried + powers[0] * incoming])


def adjoint_full(source, decays, scaled):
    length = source.shape[0]
    carried = jnp.zeros_like(decays)
    history = [None] * length
    carried = decays * carried + scaled * source[0]
    history[0] = carried
    powers = chain_powers(decays)
    incoming = adjoint_link(powers[-1], carried)
    return jnp.stack([history[0] + powers[length - 1] * incoming])


def per_device(forcing, rate_class, rate_table, row_class, col_class, inverse_offsets):
    row_count = forcing.shape[1]
    offsets = lax.all_gather(inverse_offsets, "row", axis=1, tiled=True)
    first_row = lax.axis_index("row") * row_count
    my_rows = lax.dynamic_slice_in_dim(row_class, first_row, row_count)
    my_cols = lax.dynamic_slice_in_dim(col_class, first_row, row_count)
    row_solved = rows_forward(forcing, offsets, my_rows)
    smoothed = columns_apply(
        lax.all_to_all(row_solved, "row", split_axis=1, concat_axis=2, tiled=True),
        offsets,
        my_cols,
        False,
    )
    decays = lookup(rate_class.T, rate_table)
    scaled = jnp.sqrt(1.0 - decays * decays)
    forward_rows = forward_full(to_rows(smoothed), decays, scaled)
    covariance_field = forward_rows.transpose(0, 2, 1)
    backward = adjoint_full(forward_rows, decays, scaled)
    spread = to_rows(
        columns_apply(
            lax.all_to_all(backward, "row", split_axis=1, concat_axis=2, tiled=True),
            offsets,
            my_cols,
            True,
        )
    )
    adjoint_field = rows_adjoint(spread, offsets, my_rows)
    return (covariance_field, adjoint_field)


def solution(mesh):
    placed = (P("tm", "row", None), P("row", None), P(), P(), P(), P(None, "row", None))
    return jax.shard_map(
        per_device,
        mesh=mesh,
        in_specs=placed,
        out_specs=(P("tm", "row", None), P("tm", "row", None)),
        check_vma=False,
    )
```

profile of v0, /device:TPU:8, one launch (start us, length us, event | category | flops | bytes accessed | tf_op | source)
XLA Modules:
  0.0 432.8 jit_solution(6217265600858629313)
XLA Ops:
  9.8 89.0 %all-gather.8.cloned.1.call-done = f32[2,512,512]{2,1,0:T(8,128)} async-done(((f32[2,8,512]{2,1,0:T(8,128)}), f32[2,512,512]{2,1,0:T(8,128)}) %all-gather.8.cloned.1.call-update) | async-done | bytes 2097168 | tf_op jit(solution)/shard_map/all_gather | solution.py:128
  98.9 2.0 convolution_bitcast_fusion.3
  100.9 2.0 fusion.2
  103.7 9.3 %reduce = f32[2048,32]{1,0:T(8,128)S(1)} reduce(f32[2048,1,32]{2,1,0:T(1,128)S(1)} %bitcast.153, f32[]{:T(128)} %broadcast.129), dimensions={1}, to_apply=%bitcast.132.reduce_sub_computation | reduce | bytes 524292
  113.4 21.7 %all_to_all.60 = f32[64,1,1024]{2,1,0:T(1,128)S(1)} all-to-all(f32[64,1,1024]{2,1,0:T(1,128)S(1)} %reshape.96), channel_id=1, replica_groups=mesh['tm'=8,'row'=64] {'row'}, dimensions={0} | all-to-all | bytes 524288 | tf_op jit(solution)/shard_map/all_to_all | solution.py:134
  136.3 1.8 reshape.97
  138.1 1.7 copy.114
  139.9 2.4 copy.82
  143.4 1.5 fusion.4
  146.2 10.2 %reduce.2 = f32[2048,32]{1,0:T(8,128)} reduce(f32[2048,1,32]{2,1,0:T(1,128)S(1)} %bitcast.154, f32[]{:T(128)} %broadcast.129), dimensions={1}, to_apply=%bitcast.134.reduce_sub_computation | reduce | bytes 524292
  156.4 2.4 reshape.98
  158.8 5.8 %all-to-all-start.1 = ((f32[64,1,1024]{2,1,0:T(1,128)}), f32[64,1,1024]{2,1,0:T(1,128)S(1)}, u32[]{:S(2)}, u32[]{:S(2)}) async-start(f32[64,1,1024]{2,1,0:T(1,128)} %reshape.98), calls=%async_computation.1 | async-start | bytes 524288 | tf_op jit(solution)/shard_map/all_to_all | solution.py:81
  165.6 11.4 %all-to-all-done.1 = f32[64,1,1024]{2,1,0:T(1,128)S(1)} async-done(((f32[64,1,1024]{2,1,0:T(1,128)}), f32[64,1,1024]{2,1,0:T(1,128)S(1)}, u32[]{:S(2)}, u32[]{:S(2)}) %all-to-all-start.1) | async-done | bytes 262176 | tf_op jit(solution)/shard_map/all_to_all | solution.py:81
  178.2 1.8 reshape.99
  180.0 1.7 copy.116
  181.7 2.2 copy.89
  184.5 12.1 %multiply_add_fusion.2 = (f32[2048,32]{0,1:T(8,128)}, f32[2048,32]{0,1:T(8,128)}) fusion(f32[2048,32]{0,1:T(8,128)S(1)} %squeeze.105, f32[]{:T(128)} %bitcast.20, s32[32,2048]{1,0:T(8,128)} %param.11, f32[]{:T(128)} %bitcast.19, f32[]{:T(128)} %bitcast.18, f32[]{:T(128)} %bitcast.17, f32[]{:T(128)} %bitcast.16, f32[]{:T(128)} %bitcast.15, f32[]{:T(128)} %bitcast.14, ...), kind=kLoop, calls=%fused_computation.28 | loop fusion | flops 2424832 | bytes 1048640 | tf_op jit(solution)/shard_map/add | solution.py:109
  197.4 22.9 %all-gather.12.cloned.1.call-done = f32[16384,32]{0,1:T(8,128)} async-done(((f32[2048,32]{0,1:T(8,128)}), f32[16384,32]{0,1:T(8,128)}) %all-gather.12.cloned.1.call-update) | async-done | bytes 2097168 | tf_op jit(solution)/shard_map/all_gather | solution.py:11
  220.3 6.2 %copy.117 = f32[16384,32]{1,0:T(8,128)} copy(f32[16384,32]{0,1:T(8,128)} %all-gather.12.cloned.1.call-done) | data formatting | bytes 4194304 | tf_op jit(solution)/shard_map/while | solution.py:20
  226.5 27.4 %all-gather.10.cloned.1.call-done = f32[16384,32]{0,1:T(8,128)} async-done(((f32[2048,32]{0,1:T(8,128)}), f32[16384,32]{0,1:T(8,128)}) %all-gather.10.cloned.1.call-update) | async-done | bytes 2097168 | tf_op jit(solution)/shard_map/all_gather | solution.py:11
  253.9 6.2 %copy.124 = f32[16384,32]{1,0:T(8,128)} copy(f32[16384,32]{0,1:T(8,128)} %all-gather.10.cloned.1.call-done) | data formatting | bytes 4194304 | tf_op jit(solution)/shard_map/while | solution.py:20
  261.3 2.0 multiply_add_fusion
  263.3 45.4 %all-gather.14.cloned.1.call-done = f32[16384,32]{0,1:T(8,128)} async-done(((f32[2048,32]{0,1:T(8,128)}), f32[16384,32]{0,1:T(8,128)}) %all-gather.14.cloned.1.call-update) | async-done | bytes 2097168 | tf_op jit(solution)/shard_map/all_gather | solution.py:11
  308.6 6.2 %copy.118 = f32[16384,32]{1,0:T(8,128)} copy(f32[16384,32]{0,1:T(8,128)} %all-gather.14.cloned.1.call-done) | data formatting | bytes 4194304 | tf_op jit(solution)/shard_map/while | solution.py:20
  314.9 14.7 %while.27 = (s32[]{:T(128)}, f32[2048,32]{1,0:T(8,128)S(1)}, s32[]{:T(128)}, f32[8,2048,32]{2,1,0:T(8,128)}, f32[8,2048,32]{2,1,0:T(8,128)}, /*index=5*/s32[]{:T(128)}, s32[]{:T(128)}, s32[]{:T(128)}, s32[]{:T(128)}) while((s32[]{:T(128)}, f32[2048,32]{1,0:T(8,128)S(1)}, s32[]{:T(128)}, f32[8,2048,32]{2,1,0:T(8,128)}, ...), condition=%wide.region_3.4_spmd, body=%wide.region_2.3_spmd.sunk | while | flops 131078 | bytes 1048719 | solution.py:20
  314.9 2.1 bitcast_add_fusion.5
  317.1 2.1 bitcast_add_fusion.5
  319.2 2.1 bitcast_add_fusion.5
  321.3 2.1 bitcast_add_fusion.5
  323.4 2.1 bitcast_add_fusion.5
  325.5 2.1 bitcast_add_fusion.5
  327.6 2.1 bitcast_add_fusion.5
  330.7 1.8 add_bitcast_fusion
  332.4 2.1 copy.98
  334.5 10.2 %reduce.4 = f32[2048,32]{1,0:T(8,128)} reduce(f32[2048,1,32]{2,1,0:T(1,128)S(1)} %bitcast.155, f32[]{:T(128)} %broadcast.129), dimensions={1}, to_apply=%bitcast.136.reduce_sub_computation | reduce | bytes 524292
  344.8 1.7 reshape.100
  346.5 25.9 %all_to_all.61 = f32[64,1,1024]{2,1,0:T(1,128)S(1)} all-to-all(f32[64,1,1024]{2,1,0:T(1,128)S(1)} %reshape.100), channel_id=1, replica_groups=mesh['tm'=8,'row'=64] {'row'}, dimensions={0} | all-to-all | bytes 524288 | tf_op jit(solution)/shard_map/all_to_all | solution.py:146
  373.6 1.8 reshape.101
  375.4 1.7 copy.119
  377.1 2.2 copy.100
  380.9 1.9 fusion.3
  384.1 10.2 %reduce.6 = f32[2048,32]{1,0:T(8,128)} reduce(f32[2048,1,32]{2,1,0:T(1,128)S(1)} %bitcast.156, f32[]{:T(128)} %broadcast.129), dimensions={1}, to_apply=%bitcast.138.reduce_sub_computation | reduce | bytes 524292
  394.3 1.7 reshape.102
  396.0 17.6 %all_to_all.62 = f32[64,1,1024]{2,1,0:T(1,128)S(1)} all-to-all(f32[64,1,1024]{2,1,0:T(1,128)S(1)} %reshape.102), channel_id=1, replica_groups=mesh['tm'=8,'row'=64] {'row'}, dimensions={0} | all-to-all | bytes 524288 | tf_op jit(solution)/shard_map/all_to_all | solution.py:81
  414.8 1.8 reshape.103
  416.6 1.7 copy.121
  418.3 2.2 copy.107
  423.3 2.1 fusion.8
  (44 shorter events, 21.7 us)
Async XLA Ops:
  7.2 93.7 %copy-start.3 = (f32[1,32,2048]{2,1,0:T(8,128)S(1)}, f32[1,32,2048]{2,1,0:T(8,128)}, u32[]{:S(2)}) copy-start(f32[1,32,2048]{2,1,0:T(8,128)} %param.10) | copy-start | bytes 786436
  7.2 91.7 %all-gather.8.cloned.1.call-start = ((), (), s32[]{:S(2)}) async-start(), calls=%async_computation.4 | async-start | bytes 2129920 | tf_op jit(solution)/shard_map/all_gather | solution.py:128
  139.9 2.8 copy-start
  146.2 18.7 %copy-start.4 = (f32[16]{0:T(128)S(1)}, f32[16]{0:T(128)}, u32[]{:S(2)}) copy-start(f32[16]{0:T(128)} %param.12) | copy-start | bytes 196
  158.8 18.2 %all-to-all-start.1 = ((f32[64,1,1024]{2,1,0:T(1,128)}), f32[64,1,1024]{2,1,0:T(1,128)S(1)}, u32[]{:S(2)}, u32[]{:S(2)}) async-start(f32[64,1,1024]{2,1,0:T(1,128)} %reshape.98), calls=%async_computation.1 | async-start | bytes 524288 | tf_op jit(solution)/shard_map/all_to_all | solution.py:81
  164.6 55.7 %all-gather.12.cloned.1.call-start = ((), (), s32[]{:S(2)}) async-start(), calls=%async_computation.6 | async-start | bytes 2359296 | tf_op jit(solution)/shard_map/all_gather | solution.py:11
  184.4 42.1 %copy-start.2 = (f32[2048,32]{0,1:T(8,128)}, f32[2048,32]{0,1:T(8,128)S(1)}, u32[]{:S(2)}) copy-start(f32[2048,32]{0,1:T(8,128)S(1)} %squeeze.105) | copy-start | bytes 786436
  196.6 57.3 %all-gather.10.cloned.1.call-start = ((), (), s32[]{:S(2)}) async-start(), calls=%async_computation.5 | async-start | bytes 2359296 | tf_op jit(solution)/shard_map/all_gather | solution.py:11
  197.3 111.3 %all-gather.14.cloned.1.call-start = ((), (), s32[]{:S(2)}) async-start(), calls=%async_computation.7 | async-start | bytes 2359296 | tf_op jit(solution)/shard_map/all_gather | solution.py:11
  260.2 1.0 copy-start.1
Sparse Core Ops, SparseCore 0:
  11.1 87.7 all-gather.7
  196.7 23.5 all-gather.11
  223.0 30.8 all-gather.9
  263.4 45.2 all-gather.13
where the time goes:
time: 440 us; the launch traced here: 433 us
  waiting for transfers between devices  198 us (45%)
  other arithmetic  75.8 us (17%)
  blocking collectives  65.3 us (15%)
  local copies, waits for them, and re-layouts  61.1 us (14%)
  between operations  14.3 us (3%)
  matrix products  12.6 us (3%)
  starting transfers between devices  6.13 us (1%)
    all_gather x3, waiting for transfers between devices, carried_in(): gathered = jax.tree.map(lambda a: lax.all_gather(a, axis), part)  95.7 us
    all_gather x1, waiting for transfers between devices, per_device(): offsets = lax.all_gather(inverse_offsets, 'row', axis=1, tiled=True)  89 us
    unnamed x4, other arithmetic  40 us
    all_to_all x1, blocking collectives, per_device(): lax.all_to_all(backward, 'row', split_axis=1, concat_axis=2, tiled=True)  25.9 us
    all_to_all x1, blocking collectives, per_device(): lax.all_to_all(row_solved, 'row', split_axis=1, concat_axis=2, tiled=True)  21.7 us
    while x5, local copies, waits for them, and re-layouts, carried_in(): return lax.fori_loop(0, ahead, one, state)  20.7 us
    all_to_all x1, blocking collectives, to_rows(): lax.all_to_all(column_field, 'row', split_axis=2, concat_axis=1, tiled=True)  17.6 us
    add x7, other arithmetic, affine_join(): return (earlier[0] * latter[0], latter[0] * earlier[1] + latter[1])  14.6 us
  transfers between devices with their start and end apart: 5, of which 5 were waited for; matrix products, arithmetic and copies ran while one was open for 2% of the time, Pallas kernels for 0%

commit v1 on v0

v1 whole, which is shorter than its diff:
```python
import jax
import jax.numpy as jnp
from jax import lax
from jax.experimental import pallas as pl
from jax.experimental.pallas import tpu as pltpu
from jax.sharding import Mesh
from jax.sharding import PartitionSpec as P

BLOCK = 512
LANES = 128
PIECE = 32
F32 = jnp.float32
BF16 = jnp.bfloat16
ROWS = ("h", "l", "z")
TIME = ("x", "c")
SPREAD = ("x", "l", "z")


def split(values):
    high = values.astype(BF16)
    return high, (values - high.astype(F32)).astype(BF16)


def solve(lines, mask, highs, lows, adjoint):
    dims = (((1,), (1 if adjoint else 0,)), ((), ()))
    total = None
    for k in range(2):
        mine = lines * (mask if k == 0 else 1.0 - mask)
        high, low = split(mine)
        both = jnp.concatenate([high, low], axis=0)
        wide = lax.dot_general(both, highs[k], dims, preferred_element_type=F32)
        part = wide[: lines.shape[0]] + wide[lines.shape[0] :]
        part = part + lax.dot_general(high, lows[k], dims, preferred_element_type=F32)
        total = part if total is None else total + part
    return lines + total


def exchange_lanes(tiles):
    group = lax.broadcasted_iota(jnp.int32, tiles[0].shape, 1) // PIECE
    out = []
    for place in range(4):
        made = None
        for source in range(4):
            turn = ((source - place) % 4) * PIECE
            rolled = pltpu.roll(tiles[source], turn, 1) if turn else tiles[source]
            made = rolled if made is None else jnp.where(group == source, rolled, made)
        out.append(made)
    return out


def rows_kernel(f_ref, mine_ref, other_ref, mask_ref, out_ref, high_ref, low_ref):
    lines = jnp.concatenate(
        [
            f_ref[t, :, b * BLOCK : (b + 1) * BLOCK]
            for t in range(2)
            for b in range(2)
        ],
        axis=0,
    )
    for k, ref in enumerate((mine_ref, other_ref)):
        for s in range(4):
            high, low = split(ref[s])
            high_ref[k, :, s * LANES : (s + 1) * LANES] = high
            low_ref[k, :, s * LANES : (s + 1) * LANES] = low
    solved = solve(
        lines,
        mask_ref[...],
        [high_ref[0], high_ref[1]],
        [low_ref[0], low_ref[1]],
        False,
    )
    for s in range(4):
        turned = solved[:, s * LANES : (s + 1) * LANES].T
        out_ref[s * 16 : (s + 1) * 16] = turned.reshape(16, 8, LANES)


def middle_kernel(
    x_ref, rate_ref, mask_ref, table_ref, high_ref, low_ref, out_ref, a_ref, r_ref
):
    tiles = x_ref[...].reshape(4, 4, 4, 8, LANES)
    made = exchange_lanes([tiles[:, :, i].reshape(128, LANES) for i in range(4)])
    for tb in range(4):
        block = made[tb].reshape(4, 4, 8, LANES)
        for q in range(4):
            a_ref[:, tb, :, q * LANES : (q + 1) * LANES] = block[:, q]
    rates = rate_ref[...].reshape(4, 4, 8, LANES)
    made = exchange_lanes([rates[:, i].reshape(32, LANES) for i in range(4)])
    for b in range(2):
        block = made[b].reshape(4, 8, LANES)
        for q in range(4):
            r_ref[b, :, q * LANES : (q + 1) * LANES] = block[q]
    rate = r_ref[...].reshape(16, BLOCK)
    decays = jnp.zeros_like(rate)
    for k in range(16):
        decays = jnp.where(rate == float(k), table_ref[k], decays)
    scaled = jnp.sqrt(1.0 - decays * decays)

    highs, lows = [high_ref[0], high_ref[1]], [low_ref[0], low_ref[1]]
    mask = mask_ref[...]
    smoothed = solve(a_ref[...].reshape(128, BLOCK), mask, highs, lows, False)
    state, field = None, []
    for t in range(8):
        here = scaled * smoothed[t * 16 : (t + 1) * 16]
        state = here if state is None else decays * state + here
        field.append(state)
    state, back = None, [None] * 8
    for t in range(7, -1, -1):
        here = scaled * field[t]
        state = here if state is None else decays * state + here
        back[t] = state
    adjoint = solve(jnp.concatenate(back, axis=0), mask, highs, lows, True)
    field = jnp.concatenate(field, axis=0)
    for n, value in enumerate((field, adjoint)):
        parts = value.reshape(4, 4, 8, BLOCK)
        for q in range(4):
            tiles = [
                parts[:, tb, :, q * LANES : (q + 1) * LANES].reshape(32, LANES)
                for tb in range(4)
            ]
            made = exchange_lanes(tiles)
            for i in range(4):
                block = made[i].reshape(4, 8, LANES)
                for x in range(4):
                    out_ref[x * 16 + q * 4 + i, n * 8 : (n + 1) * 8, :] = block[x]


def last_kernel(x_ref, mask_ref, high_ref, low_ref, out_ref):
    pieces = [[], []]
    for s in range(4):
        for n in range(2):
            tile = x_ref[s * 16 : (s + 1) * 16, n * 8 : (n + 1) * 8, :]
            pieces[n].append(tile.reshape(LANES, LANES).T)
    field = jnp.concatenate(pieces[0], axis=1)
    lines = jnp.concatenate(pieces[1], axis=1)
    solved = solve(
        lines,
        mask_ref[...],
        [high_ref[0], high_ref[1]],
        [low_ref[0], low_ref[1]],
        True,
    )
    for n, value in enumerate((field, solved)):
        for t in range(2):
            for b in range(2):
                first = (t * 2 + b) * PIECE
                out_ref[t, n, :, b * BLOCK : (b + 1) * BLOCK] = value[
                    first : first + PIECE
                ]


def vmem(count):
    return [pl.BlockSpec(memory_space=pltpu.VMEM)] * count


PARAMS = pltpu.CompilerParams(vmem_limit_bytes=48 * 1024 * 1024)


def swap(values, axis):
    return lax.all_to_all(values, axis, split_axis=0, concat_axis=0, tiled=True)


def spread_out(values, axis):
    count = lax.axis_size(axis)
    return swap(jnp.broadcast_to(values[None], (count,) + values.shape), axis)


def gather_matrices(offsets, x, c):
    rows = offsets.shape[1]
    piece = lax.dynamic_slice(offsets, (c, 0, x * LANES), (1, rows, LANES))[0]
    slab = spread_out(piece, ROWS).reshape(BLOCK, LANES)
    mine = spread_out(slab, "x")
    other = lax.ppermute(mine, "c", [(0, 1), (1, 0)])
    return mine, other


def per_device(forcing, rate_class, rate_table, row_class, col_class, offsets):
    x, c = lax.axis_index("x"), lax.axis_index("c")
    place = lax.axis_index(("l", "z"))
    first_row = lax.axis_index(ROWS) * PIECE
    kind = c.astype(jnp.int32)

    my_rows = lax.dynamic_slice_in_dim(row_class, first_row, PIECE)
    row_mask = jnp.tile((my_rows == kind).astype(F32), 4).reshape(128, 1)
    columns = [c * 1024 + b * BLOCK + x * LANES for b in range(2)]
    my_cols = jnp.concatenate(
        [lax.dynamic_slice_in_dim(col_class, at + place * 8, 8) for at in columns]
    )
    col_mask = jnp.tile((my_cols == kind).astype(F32), 8).reshape(128, 1)

    f = forcing[0]
    f = swap(jnp.stack([f[:, :1024], f[:, 1024:]]), "c")
    rate = [lax.dynamic_slice(rate_class, (0, at), (PIECE, LANES)) for at in columns]
    rate = jnp.concatenate(rate + rate, axis=0).astype(F32).T.reshape(16, 8, LANES)
    rate = swap(rate, ("l", "z"))
    mine, other = gather_matrices(offsets, x, c)

    out, high, low = pl.pallas_call(
        rows_kernel,
        out_shape=(
            jax.ShapeDtypeStruct((64, 8, LANES), F32),
            jax.ShapeDtypeStruct((2, BLOCK, BLOCK), BF16),
            jax.ShapeDtypeStruct((2, BLOCK, BLOCK), BF16),
        ),
        in_specs=vmem(4),
        out_specs=tuple(vmem(3)),
        compiler_params=PARAMS,
        name="rows",
    )(f, mine, other, row_mask)
    out = swap(out, SPREAD)
    out = pl.pallas_call(
        middle_kernel,
        out_shape=jax.ShapeDtypeStruct((64, 16, LANES), F32),
        in_specs=vmem(3) + [pl.BlockSpec(memory_space=pltpu.SMEM)] + vmem(2),
        out_specs=vmem(1)[0],
        scratch_shapes=[
            pltpu.VMEM((4, 4, 8, BLOCK), F32),
            pltpu.VMEM((2, 8, BLOCK), F32),
        ],
        compiler_params=PARAMS,
        name="middle",
    )(out, rate, col_mask, rate_table, high, low)
    out = swap(out, SPREAD)
    out = pl.pallas_call(
        last_kernel,
        out_shape=jax.ShapeDtypeStruct((2, 2, PIECE, 1024), F32),
        in_specs=vmem(4),
        out_specs=vmem(1)[0],
        compiler_params=PARAMS,
        name="last",
    )(out, row_mask, high, low)
    out = swap(out, "c")
    covariance = jnp.concatenate([out[0, 0], out[1, 0]], axis=1)
    adjoint = jnp.concatenate([out[0, 1], out[1, 1]], axis=1)
    return covariance[None], adjoint[None]


def solution(mesh):
    devices = mesh.devices
    tm, row = devices.shape
    fine = Mesh(devices.reshape(tm // 2, 2, row // 16, 2, 8), ("x", "c", "h", "l", "z"))
    field = P(TIME, ROWS, None)
    return jax.shard_map(
        per_device,
        mesh=fine,
        in_specs=(field, P(ROWS, None), P(), P(), P(), P(None, ROWS, None)),
        out_specs=(field, field),
        check_vma=False,
    )
```

time: 440 us -> 123 us (0.28)
  the two profiles are of different devices: /device:TPU:8 before, /device:TPU:1 now
where the time goes in v1:
time: 123 us; the launch traced here: 122 us
  blocking collectives  74.4 us (60%)
  starting transfers between devices  20.4 us (17%)
  waiting for transfers between devices  12.7 us (10%)
  local copies, waits for them, and re-layouts  6.98 us (6%)
  Pallas kernels  4.29 us (3%)
  other arithmetic  2.4 us (2%)
    all_to_all x4, blocking collectives, swap(): return lax.all_to_all(values, axis, split_axis=0, concat_axis=0, tiled=True)  74.4 us
    all_to_all x3, starting transfers between devices, swap(): return lax.all_to_all(values, axis, split_axis=0, concat_axis=0, tiled=True)  13.9 us
    all_to_all x3, waiting for transfers between devices, swap(): return lax.all_to_all(values, axis, split_axis=0, concat_axis=0, tiled=True)  12.7 us
    ppermute x1, starting transfers between devices, gather_matrices(): other = lax.ppermute(mine, 'c', [(0, 1), (1, 0)])  6.53 us
    unnamed x12, local copies, waits for them, and re-layouts  4.31 us
    pallas_call x1, Pallas kernels, per_device(): pl.pallas_call(middle_kernel, out_shape=jax.ShapeDtypeStruct((64, 16, LAN...  2.56 us
  transfers between devices with their start and end apart: 4, of which 2 were waited for; matrix products, arithmetic and copies ran while one was open for 3% of the time, Pallas kernels for 1%

profile of v1, /device:TPU:1, one launch (start us, length us, event | category | flops | bytes accessed | tf_op | source)
XLA Modules:
  0.0 122.0 jit_solution(896955892374269431)
XLA Ops:
  0.6 0.0 copy-start
  0.7 0.7 copy-done
  1.4 29.5 %all_to_all.35 = f32[64,8,128]{2,1,0:T(8,128)S(1)} all-to-all(f32[64,8,128]{2,1,0:T(8,128)S(1)} %broadcast_in_dim.21), channel_id=1, replica_groups=mesh['x'=4,'c'=2,'h'=4,'l'=2,'z'=8] {'h','l','z'}, dimensions={0} | all-to-all | bytes 524288 | tf_op jit(solution)/shard_map/all_to_all | solution.py:159
  30.9 0.1 broadcast_in_dim.23
  31.0 0.0 copy-start.5
  31.0 15.4 %all_to_all.36.mine_ref = f32[4,512,128]{2,1,0:T(8,128)S(1)} all-to-all(f32[4,512,128]{2,1,0:T(8,128)S(1)} %broadcast_in_dim.23), channel_id=1, replica_groups=mesh['x'=4,'c'=2,'h'=4,'l'=2,'z'=8] {'x'}, dimensions={0} | all-to-all | bytes 2097152 | tf_op jit(solution)/shard_map/all_to_all | solution.py:159
  46.4 6.5 %collective-permute-start = (f32[4,512,128]{2,1,0:T(8,128)S(1)}, f32[4,512,128]{2,1,0:T(8,128)S(1)}, u32[]{:S(2)}, u32[]{:S(2)}) collective-permute-start(f32[4,512,128]{2,1,0:T(8,128)S(1)} %all_to_all.36.mine_ref), channel_id=1, source_target_pairs={{0,64},{64,0},{1,65},{65,1},{2,66},{66,2},{3,67},{67,3},{4,68},{68... | collective-permute-start | bytes 3145736 | tf_op jit(solution)/shard_map/ppermute | solution.py:172
  52.9 0.0 copy-done.5
  52.9 0.7 pad_maximum_fusion
  53.7 3.4 %all-to-all-start = ((f32[2,32,1024]{2,1,0:T(8,128)}), f32[2,32,1024]{2,1,0:T(8,128)S(1)}, u32[]{:S(2)}, u32[]{:S(2)}) async-start(f32[2,32,1024]{2,1,0:T(8,128)} %pad_maximum_fusion), calls=%async_computation | async-start | bytes 524288 | tf_op jit(solution)/shard_map/all_to_all | solution.py:159
  57.1 0.7 constant_dynamic-slice_fusion.1
  57.9 0.7 copy.9
  58.6 0.0 all-to-all-done.f_ref
  58.6 4.1 %all-to-all-start.4 = ((f32[16,8,128]{2,1,0:T(8,128)}), f32[16,8,128]{2,1,0:T(8,128)}, u32[]{:S(2)}, u32[]{:S(2)}) async-start(f32[16,8,128]{2,1,0:T(8,128)} %bitcast.6), calls=%async_computation.4 | async-start | bytes 131072 | tf_op jit(solution)/shard_map/all_to_all | solution.py:159
  62.8 0.8 compare_convert_fusion.1
  63.5 0.1 reshape_tile.8.mask_ref
  63.6 0.0 collective-permute-done.other_ref
  63.7 0.0 copy-start.1
  63.7 1.0 copy-done.1
  64.6 0.0 copy-start.2
  64.6 1.2 %copy-done.2 = f32[4,512,128]{2,1,0:T(8,128)S(1)} copy-done((f32[4,512,128]{2,1,0:T(8,128)S(1)}, f32[4,512,128]{2,1,0:T(8,128)}, u32[]{:S(2)}) %copy-start.2) | copy-done | bytes 1048600
  65.9 0.9 rows.1
  66.8 0.0 copy-start.3
  66.8 0.7 copy-done.3
  67.5 2.7 %all-to-all-done.4.rate_ref = f32[16,8,128]{2,1,0:T(8,128)} async-done(((f32[16,8,128]{2,1,0:T(8,128)}), f32[16,8,128]{2,1,0:T(8,128)}, u32[]{:S(2)}, u32[]{:S(2)}) %all-to-all-start.4) | async-done | bytes 65568 | tf_op jit(solution)/shard_map/all_to_all | solution.py:159
  70.2 6.3 %all-to-all-start.3 = ((f32[64,8,128]{2,1,0:T(8,128)}), f32[64,8,128]{2,1,0:T(8,128)S(1)}, u32[]{:S(2)}, u32[]{:S(2)}) async-start(f32[64,8,128]{2,1,0:T(8,128)} %copy-done.3), calls=%async_computation.3 | async-start | bytes 524288 | tf_op jit(solution)/shard_map/all_to_all | solution.py:159
  76.5 0.8 fusion.1
  77.3 0.1 compare_convert_fusion
  77.4 0.1 reshape_tile.9.mask_ref
  77.5 10.0 %all-to-all-done.3.x_ref = f32[64,8,128]{2,1,0:T(8,128)S(1)} async-done(((f32[64,8,128]{2,1,0:T(8,128)}), f32[64,8,128]{2,1,0:T(8,128)S(1)}, u32[]{:S(2)}, u32[]{:S(2)}) %all-to-all-start.3) | async-done | bytes 262176 | tf_op jit(solution)/shard_map/all_to_all | solution.py:159
  87.5 0.0 copy-start.4
  87.5 0.7 copy-done.4
  88.2 2.6 %middle.1 = f32[64,16,128]{2,1,0:T(8,128)S(1)} custom-call(f32[64,8,128]{2,1,0:T(8,128)S(1)} %all-to-all-done.3.x_ref, f32[16,8,128]{2,1,0:T(8,128)} %all-to-all-done.4.rate_ref, f32[128,1]{1,0:T(8,128)S(1)} %reshape_tile.9.mask_ref, f32[16]{0:T(128)S(1)} %copy-done.4, bf16[2,512,512]{2,1,0:T(8,128)(2,1)S(1)} %get-tuple-element.6.high_ref, ...), custom_call_target="tpu_custom_call" | custom-call | tf_op jit(solution)/shard_map/middle/pallas_call | solution.py:210
  90.7 23.0 %all_to_all.37.x_ref = f32[64,16,128]{2,1,0:T(8,128)S(1)} all-to-all(f32[64,16,128]{2,1,0:T(8,128)S(1)} %middle.1), channel_id=1, replica_groups=mesh['x'=4,'c'=2,'h'=4,'l'=2,'z'=8] {'x','l','z'}, dimensions={0} | all-to-all | bytes 1048576 | tf_op jit(solution)/shard_map/all_to_all | solution.py:159
  113.7 0.8 last.1
  114.6 6.6 %all_to_all.38 = f32[2,2,32,1024]{3,2,1,0:T(8,128)S(1)} all-to-all(f32[2,2,32,1024]{3,2,1,0:T(8,128)S(1)} %last.1), channel_id=1, replica_groups=mesh['x'=4,'c'=2,'h'=4,'l'=2,'z'=8] {'c'}, dimensions={0} | all-to-all | bytes 1048576 | tf_op jit(solution)/shard_map/all_to_all | solution.py:159
  121.2 0.8 maximum_bitcast_fusion
  (7 shorter events, 0.1 us)
Async XLA Ops:
  0.6 0.8 copy-start
  31.0 21.9 %copy-start.5 = (f32[1,32,2048]{2,1,0:T(8,128)S(1)}, f32[1,32,2048]{2,1,0:T(8,128)}, u32[]{:S(2)}) copy-start(f32[1,32,2048]{2,1,0:T(8,128)} %param.6) | copy-start | bytes 786436
  46.4 17.3 %collective-permute-start = (f32[4,512,128]{2,1,0:T(8,128)S(1)}, f32[4,512,128]{2,1,0:T(8,128)S(1)}, u32[]{:S(2)}, u32[]{:S(2)}) collective-permute-start(f32[4,512,128]{2,1,0:T(8,128)S(1)} %all_to_all.36.mine_ref), channel_id=1, source_target_pairs={{0,64},{64,0},{1,65},{65,1},{2,66},{66,2},{3,67},{67,3},{4,68},{68... | collective-permute-start | bytes 3145736 | tf_op jit(solution)/shard_map/ppermute | solution.py:172
  53.7 4.9 %all-to-all-start = ((f32[2,32,1024]{2,1,0:T(8,128)}), f32[2,32,1024]{2,1,0:T(8,128)S(1)}, u32[]{:S(2)}, u32[]{:S(2)}) async-start(f32[2,32,1024]{2,1,0:T(8,128)} %pad_maximum_fusion), calls=%async_computation | async-start | bytes 524288 | tf_op jit(solution)/shard_map/all_to_all | solution.py:159
  58.6 11.6 %all-to-all-start.4 = ((f32[16,8,128]{2,1,0:T(8,128)}), f32[16,8,128]{2,1,0:T(8,128)}, u32[]{:S(2)}, u32[]{:S(2)}) async-start(f32[16,8,128]{2,1,0:T(8,128)} %bitcast.6), calls=%async_computation.4 | async-start | bytes 131072 | tf_op jit(solution)/shard_map/all_to_all | solution.py:159
  63.7 1.0 copy-start.1
  64.6 1.2 %copy-start.2 = (f32[4,512,128]{2,1,0:T(8,128)S(1)}, f32[4,512,128]{2,1,0:T(8,128)}, u32[]{:S(2)}) copy-start(f32[4,512,128]{2,1,0:T(8,128)} %copy-done.1) | copy-start | bytes 3145732
  66.8 0.7 copy-start.3
  70.2 17.3 %all-to-all-start.3 = ((f32[64,8,128]{2,1,0:T(8,128)}), f32[64,8,128]{2,1,0:T(8,128)S(1)}, u32[]{:S(2)}, u32[]{:S(2)}) async-start(f32[64,8,128]{2,1,0:T(8,128)} %copy-done.3), calls=%async_computation.3 | async-start | bytes 524288 | tf_op jit(solution)/shard_map/all_to_all | solution.py:159
  87.5 0.7 copy-start.4

commit v2 on v1

v2 whole, which is shorter than its diff:
```python
import jax
import jax.numpy as jnp
from jax import lax
from jax.experimental import pallas as pl
from jax.experimental.pallas import tpu as pltpu
from jax.sharding import Mesh
from jax.sharding import PartitionSpec as P

BLOCK = 512
HALF = 256
LANES = 128
PIECE = 32
F32 = jnp.float32
BF16 = jnp.bfloat16
ROWS = ("h", "l", "z")
TIME = ("u", "v", "c")
NEAR = ("u", "l", "z")
SPREAD = ("u", "v", "l", "z")


def split(values):
    high = values.astype(BF16)
    return high, (values - high.astype(F32)).astype(BF16)


def product(both, high, matrix_high, matrix_low, adjoint):
    dims = (((1,), (1 if adjoint else 0,)), ((), ()))
    count = high.shape[0]
    wide = lax.dot_general(both, matrix_high, dims, preferred_element_type=F32)
    small = lax.dot_general(high, matrix_low, dims, preferred_element_type=F32)
    return wide[:count] + (wide[count:] + small)


def by_half(v, own, far):
    return [jnp.where(v == 0, own, far), jnp.where(v == 0, far, own)]


def solve_forward(lines, mask, halves):
    high, low = split(lines)
    both = jnp.concatenate([high, low], axis=0)
    out = []
    for highs, lows in halves:
        parts = [product(both, high, highs[k], lows[k], False) for k in range(2)]
        out.append(jnp.where(mask, parts[0], parts[1]))
    return out


def solve_adjoint(lines, mask, v, halves):
    total = [None, None]
    order = by_half(v, lines[:, :HALF], lines[:, HALF:])
    for piece, (highs, lows) in zip(order, halves):
        high, low = split(piece)
        both = jnp.concatenate([high, low], axis=0)
        for k in range(2):
            part = product(both, high, highs[k], lows[k], True)
            total[k] = part if total[k] is None else total[k] + part
    return lines + jnp.where(mask, total[0], total[1])


def exchange_lanes(tiles):
    group = lax.broadcasted_iota(jnp.int32, tiles[0].shape, 1) // PIECE
    out = []
    for place in range(4):
        made = None
        for source in range(4):
            turn = ((source - place) % 4) * PIECE
            rolled = pltpu.roll(tiles[source], turn, 1) if turn else tiles[source]
            made = rolled if made is None else jnp.where(group == source, rolled, made)
        out.append(made)
    return out


def class_mask(line, first, count, kind, copies):
    lane = lax.broadcasted_iota(jnp.int32, (count, LANES), 1)
    row = lax.broadcasted_iota(jnp.int32, (count, LANES), 0)
    picked = jnp.where((lane == row + first) & (line == kind), 1.0, 0.0)
    return jnp.concatenate([jnp.sum(picked, axis=1, keepdims=True)] * copies, axis=0) > 0.5


def row_mask(class_ref, kind, copies):
    place = lax.axis_index(ROWS)
    line = class_ref[pl.ds(place // 4, 1), :]
    return class_mask(line, lax.rem(place, 4) * PIECE, PIECE, kind, copies)


def rows_kernel(
    f0, f1, f2, f3, mine_ref, other_ref, rate_ref, class_ref, out_ref, high_ref, low_ref
):
    c, v = lax.axis_index("c"), lax.axis_index("v")
    fields = (f0, f1, f2, f3)

    def columns(ref, b, more, width):
        at = pl.multiple_of(c * 1024 + b * BLOCK + more, width)
        return ref[..., pl.ds(at, width)].reshape(PIECE, width)

    lines = jnp.concatenate(
        [columns(f, b, 0, BLOCK) for f in fields for b in range(2)], axis=0
    )
    same = jnp.concatenate(
        [columns(f, b, v * HALF, HALF) for f in fields for b in range(2)], axis=0
    )
    rate = [columns(rate_ref, b, v * HALF, HALF).astype(F32) for b in range(2)]
    rate = jnp.concatenate(rate + rate, axis=0)
    for k, ref in enumerate((mine_ref, other_ref)):
        high, low = split(ref[...])
        high_ref[k] = high
        low_ref[k] = low
    mask = row_mask(class_ref, c, 8)
    solved = solve_forward(lines, mask, [(high_ref, low_ref)])[0] + same
    for n in range(2):
        at = slice(n * LANES, (n + 1) * LANES)
        for place in range(3):
            tile = rate if place == 2 else solved[place * LANES : (place + 1) * LANES]
            out_ref[n * 16 : (n + 1) * 16, place] = tile[:, at].T.reshape(16, 8, LANES)


def middle_kernel(
    x_ref, near_mine, near_other, class_ref, table_ref, high_ref, low_ref,
    out_ref, far_high, far_low, a_ref, r_ref,
):
    c, v, u = lax.axis_index("c"), lax.axis_index("v"), lax.axis_index("u")
    for k, ref in enumerate((near_mine, near_other)):
        high, low = split(ref[...])
        far_high[k] = high
        far_low[k] = low
    tiles = x_ref[...].reshape(2, 4, 4, 3, 8, LANES)
    made = exchange_lanes([tiles[:, :, i, :2].reshape(128, LANES) for i in range(4)])
    for tb in range(4):
        block = made[tb].reshape(2, 4, 2, 8, LANES)
        for q in range(4):
            a_ref[:, :, tb, :, q * LANES : (q + 1) * LANES] = block[:, q]
    made = exchange_lanes([tiles[0, :, i, 2].reshape(32, LANES) for i in range(4)])
    for b in range(2):
        block = made[b].reshape(4, 8, LANES)
        for q in range(4):
            r_ref[b, :, q * LANES : (q + 1) * LANES] = block[q]
    rate = r_ref[...].reshape(16, BLOCK)
    decays = jnp.zeros_like(rate)
    for k in range(16):
        decays = jnp.where(rate == float(k), table_ref[k], decays)
    scaled = jnp.sqrt(1.0 - decays * decays)

    place = lax.axis_index(("l", "z"))
    marks = []
    for b in range(2):
        line = class_ref[pl.ds(c * 8 + b * 4 + v * 2 + u, 1), :]
        marks.append(class_mask(line, place * 8, 8, c, 1).astype(F32))
    mask = jnp.concatenate(marks * 8, axis=0) > 0.5
    halves = [(high_ref, low_ref), (far_high, far_low)]
    lines = a_ref[...].reshape(128, BLOCK)
    solved = by_half(v, *solve_forward(lines, mask, halves))
    smoothed = (lines + jnp.concatenate(solved, axis=1)).reshape(2, 2, 2, 16, BLOCK)
    state, field = None, []
    for t in range(8):
        far, late, core = t // 4, (t // 2) % 2, t % 2
        pair = smoothed[far]
        pair = jnp.where(v == 0, pair[late], pair[1 - late])
        here = scaled * jnp.where(c == 0, pair[core], pair[1 - core])
        state = here if state is None else decays * state + here
        field.append(state)
    state, back = None, [None] * 8
    for t in range(7, -1, -1):
        here = scaled * field[t]
        state = here if state is None else decays * state + here
        back[t] = state
    adjoint = solve_adjoint(jnp.concatenate(back, axis=0), mask, v, halves)
    field = jnp.concatenate(field, axis=0)
    for n, value in enumerate((field, adjoint)):
        parts = value.reshape(4, 4, 8, BLOCK)
        for q in range(4):
            tiles = [
                parts[:, tb, :, q * LANES : (q + 1) * LANES].reshape(32, LANES)
                for tb in range(4)
            ]
            made = exchange_lanes(tiles)
            for i in range(4):
                block = made[i].reshape(4, 8, LANES)
                for x in range(4):
                    out_ref[x * 16 + q * 4 + i, n * 8 : (n + 1) * 8, :] = block[x]


def last_kernel(
    x_ref, class_ref, high_ref, low_ref, far_high, far_low, out_ref
):
    c, v = lax.axis_index("c"), lax.axis_index("v")
    pieces = [[], []]
    for s in range(4):
        x = (s % 2) * 2 + s // 2
        for n in range(2):
            tile = x_ref[x * 16 : (x + 1) * 16, n * 8 : (n + 1) * 8, :]
            pieces[n].append(tile.reshape(LANES, LANES).T)
    field = jnp.concatenate(pieces[0], axis=1)
    lines = jnp.concatenate(pieces[1], axis=1)
    mask = row_mask(class_ref, c, 4)
    halves = [(high_ref, low_ref), (far_high, far_low)]
    solved = solve_adjoint(lines, mask, v, halves)
    for n, value in enumerate((field, solved)):
        for t in range(2):
            for b in range(2):
                first = (t * 2 + b) * PIECE
                out_ref[t, n, :, b * BLOCK : (b + 1) * BLOCK] = value[
                    first : first + PIECE
                ]


def vmem(count):
    return [pl.BlockSpec(memory_space=pltpu.VMEM)] * count


PARAMS = pltpu.CompilerParams(vmem_limit_bytes=40 * 1024 * 1024)
HALVES = (jax.ShapeDtypeStruct((2, BLOCK, HALF), BF16),) * 2


def swap(values, axis):
    return lax.all_to_all(values, axis, split_axis=0, concat_axis=0, tiled=True)


def to_partners(values):
    core = lax.ppermute(values, "c", [(0, 1), (1, 0)])
    near = lax.ppermute(values, "v", [(0, 1), (1, 0)])
    both = lax.ppermute(values, ("v", "c"), [(k, 3 - k) for k in range(4)])
    return core, near, both


def per_device(forcing, rate_class, rate_table, row_class, col_class, offsets):
    c, v = lax.axis_index("c"), lax.axis_index("v")
    row_lines = row_class.reshape(-1, LANES)
    col_lines = col_class.reshape(-1, LANES)

    fields = (forcing,) + to_partners(forcing)
    rows = offsets.shape[1]
    piece = lax.dynamic_slice(offsets, (c, 0, v * HALF), (1, rows, HALF))
    pieces = jnp.broadcast_to(piece, (BLOCK // rows, rows, HALF))
    mine = swap(pieces, ROWS).reshape(BLOCK, HALF)
    mine, *fields = lax.optimization_barrier((mine,) + fields)
    other, near_mine, near_other = to_partners(mine)

    out, high, low = pl.pallas_call(
        rows_kernel,
        out_shape=(jax.ShapeDtypeStruct((32, 3, 8, LANES), F32),) + HALVES,
        in_specs=vmem(8),
        out_specs=tuple(vmem(3)),
        compiler_params=PARAMS,
        name="rows",
    )(*fields, mine, other, rate_class, row_lines)
    out = swap(out, NEAR)
    out, far_high, far_low = pl.pallas_call(
        middle_kernel,
        out_shape=(jax.ShapeDtypeStruct((64, 16, LANES), F32),) + HALVES,
        in_specs=vmem(4) + [pl.BlockSpec(memory_space=pltpu.SMEM)] + vmem(2),
        out_specs=tuple(vmem(3)),
        scratch_shapes=[
            pltpu.VMEM((2, 2, 4, 8, BLOCK), F32),
            pltpu.VMEM((2, 8, BLOCK), F32),
        ],
        compiler_params=PARAMS,
        name="middle",
    )(out, near_mine, near_other, col_lines, rate_table, high, low)
    out = swap(out, SPREAD)
    out = pl.pallas_call(
        last_kernel,
        out_shape=jax.ShapeDtypeStruct((2, 2, PIECE, 1024), F32),
        in_specs=vmem(6),
        out_specs=vmem(1)[0],
        compiler_params=PARAMS,
        name="last",
    )(out, row_lines, high, low, far_high, far_low)
    out = swap(out, "c")
    covariance = jnp.concatenate([out[0, 0], out[1, 0]], axis=1)
    adjoint = jnp.concatenate([out[0, 1], out[1, 1]], axis=1)
    return covariance[None], adjoint[None]


def solution(mesh):
    devices = mesh.devices
    tm, row = devices.shape
    fine = Mesh(
        devices.reshape(tm // 4, 2, 2, row // 16, 2, 8), ("u", "v", "c", "h", "l", "z")
    )
    field = P(TIME, ROWS, None)
    return jax.shard_map(
        per_device,
        mesh=fine,
        in_specs=(field, P(ROWS, None), P(), P(), P(), P(None, ROWS, None)),
        out_specs=(field, field),
        check_vma=False,
    )
```

time: 123 us -> 122 us (level)
  blocking collectives: 74.4 us -> 32.9 us
  waiting for transfers between devices: 12.7 us -> 36.2 us
  starting transfers between devices: 20.4 us -> 43.9 us
  local copies, waits for them, and re-layouts: 6.98 us -> 2.3 us
  other arithmetic: 2.4 us -> 0.83 us
    all_to_all x4 -> x2, blocking collectives: 74.4 us -> 32.9 us  [swap(): return lax.all_to_all(values, axis, split_axis=0, concat_axis=0, tiled=True)]
    ppermute x1 -> x6, waiting for transfers between devices: 0.01 us -> 36.2 us  [the longest x2 17.6 us: to_partners(): both = lax.ppermute(values, ('v', 'c'), [(k, 3 - k) for k in range(4)])]
    all_to_all x3 -> x2, waiting for transfers between devices: 12.7 us -> 0.01 us  [swap(): return lax.all_to_all(values, axis, split_axis=0, concat_axis=0, tiled=True)]
    all_to_all x3 -> x2, starting transfers between devices: 13.9 us -> 26.2 us  [swap(): return lax.all_to_all(values, axis, split_axis=0, concat_axis=0, tiled=True)]
    ppermute x1 -> x6, starting transfers between devices: 6.53 us -> 17.8 us  [the longest x2 6.27 us: to_partners(): core = lax.ppermute(values, 'c', [(0, 1), (1, 0)])]
    unnamed x12, local copies, waits for them, and re-layouts: 4.31 us -> 1.42 us
    dynamic_slice x2 -> x0, local copies, waits for them, and re-layouts: 1.58 us -> none  [the longest x1 0.84 us: per_device(): lax.dynamic_slice_in_dim(col_class, at + place * 8, 8)]
  transfers between devices with their start and end apart: 4 -> 8, of which waited for: 2 -> 5; matrix products, arithmetic and copies ran while one was open for 3% -> 0% of each run, Pallas kernels for 1% -> 0%
where the time goes in v2:
time: 122 us
  starting transfers between devices  43.9 us (36%)
  waiting for transfers between devices  36.2 us (30%)
  blocking collectives  32.9 us (27%)
  Pallas kernels  4.68 us (4%)
  local copies, waits for them, and re-layouts  2.3 us (2%)
    all_to_all x2, blocking collectives, swap(): return lax.all_to_all(values, axis, split_axis=0, concat_axis=0, tiled=True)  32.9 us
    all_to_all x2, starting transfers between devices, swap(): return lax.all_to_all(values, axis, split_axis=0, concat_axis=0, tiled=True)  26.2 us
    ppermute x2, waiting for transfers between devices, to_partners(): both = lax.ppermute(values, ('v', 'c'), [(k, 3 - k) for k in range(4)])  17.6 us
    ppermute x2, waiting for transfers between devices, to_partners(): near = lax.ppermute(values, 'v', [(0, 1), (1, 0)])  17.1 us
    ppermute x2, starting transfers between devices, to_partners(): core = lax.ppermute(values, 'c', [(0, 1), (1, 0)])  6.27 us
    ppermute x2, starting transfers between devices, to_partners(): both = lax.ppermute(values, ('v', 'c'), [(k, 3 - k) for k in range(4)])  6.13 us
    ppermute x2, starting transfers between devices, to_partners(): near = lax.ppermute(values, 'v', [(0, 1), (1, 0)])  5.35 us
  transfers between devices with their start and end apart: 8, of which 5 were waited for; matrix products, arithmetic and copies ran while one was open for 0% of the time, Pallas kernels for 0%

profile of v2, /device:TPU:1, one launch (start us, length us, event | category | flops | bytes accessed | tf_op | source)
XLA Modules:
  0.0 121.6 jit_solution(18408733004607991810)
XLA Ops:
  0.6 0.0 copy-start
  0.7 0.7 copy-done
  1.4 0.8 broadcast_in_dim.14
  2.2 0.0 copy-start.1
  2.2 0.0 copy-start.2
  2.2 0.0 copy-start.3
  2.2 17.3 %all-to-all-start = ((f32[64,8,256]{2,1,0:T(8,128)}), f32[64,8,256]{2,1,0:T(8,128)S(1)}, u32[]{:S(2)}, u32[]{:S(2)}) async-start(f32[64,8,256]{2,1,0:T(8,128)} %broadcast_in_dim.14), calls=%async_computation | async-start | bytes 1048576 | tf_op jit(solution)/shard_map/all_to_all | solution.py:215
  19.5 0.0 copy-done.1
  19.5 2.9 %collective-permute-start = (f32[1,32,2048]{2,1,0:T(8,128)S(1)}, f32[1,32,2048]{2,1,0:T(8,128)S(1)}, u32[]{:S(2)}, u32[]{:S(2)}) collective-permute-start(f32[1,32,2048]{2,1,0:T(8,128)S(1)} %copy-done.1), channel_id=1, source_target_pairs={{0,64},{64,0},{1,65},{65,1},{2,66},{66,2},{3,67},{67,3},{4,68},{68... | collective-permute-start | bytes 786440 | tf_op jit(solution)/shard_map/ppermute | solution.py:219
  22.4 3.1 %collective-permute-start.1 = (f32[1,32,2048]{2,1,0:T(8,128)S(1)}, f32[1,32,2048]{2,1,0:T(8,128)S(1)}, u32[]{:S(2)}, u32[]{:S(2)}) collective-permute-start(f32[1,32,2048]{2,1,0:T(8,128)S(1)} %copy-done.1), channel_id=1, source_target_pairs={{0,128},{128,0},{1,129},{129,1},{2,130},{130,2},{3,131},{131,3},{4... | collective-permute-start | bytes 786440 | tf_op jit(solution)/shard_map/ppermute | solution.py:220
  25.5 2.3 %collective-permute-start.2 = (f32[1,32,2048]{2,1,0:T(8,128)S(1)}, f32[1,32,2048]{2,1,0:T(8,128)S(1)}, u32[]{:S(2)}, u32[]{:S(2)}) collective-permute-start(f32[1,32,2048]{2,1,0:T(8,128)S(1)} %copy-done.1), channel_id=1, source_target_pairs={{0,192},{64,128},{128,64},{192,0},{1,193},{65,129},{129,65},{193,1... | collective-permute-start | bytes 786440 | tf_op jit(solution)/shard_map/ppermute | solution.py:221
  27.9 0.0 collective-permute-done.f1
  27.9 4.3 %collective-permute-done.1.f2 = f32[1,32,2048]{2,1,0:T(8,128)S(1)} collective-permute-done((f32[1,32,2048]{2,1,0:T(8,128)S(1)}, f32[1,32,2048]{2,1,0:T(8,128)S(1)}, u32[]{:S(2)}, u32[]{:S(2)}) %collective-permute-start.1) | collective-permute-done | bytes 262176 | tf_op jit(solution)/shard_map/ppermute | solution.py:220
  32.2 6.0 %collective-permute-done.2.f3 = f32[1,32,2048]{2,1,0:T(8,128)S(1)} collective-permute-done((f32[1,32,2048]{2,1,0:T(8,128)S(1)}, f32[1,32,2048]{2,1,0:T(8,128)S(1)}, u32[]{:S(2)}, u32[]{:S(2)}) %collective-permute-start.2) | collective-permute-done | bytes 262176 | tf_op jit(solution)/shard_map/ppermute | solution.py:221
  38.2 0.0 all-to-all-done
  38.2 3.4 %collective-permute-start.3 = (f32[512,256]{1,0:T(8,128)S(1)}, f32[512,256]{1,0:T(8,128)S(1)}, u32[]{:S(2)}, u32[]{:S(2)}) collective-permute-start(f32[512,256]{1,0:T(8,128)S(1)} %bitcast.17), channel_id=1, source_target_pairs={{0,64},{64,0},{1,65},{65,1},{2,66},{66,2},{3,67},{67,3},{4,68},{68... | collective-permute-start | bytes 1572872 | tf_op jit(solution)/shard_map/ppermute | solution.py:219
  41.7 1.5 %collective-permute-done.3.other_ref = f32[512,256]{1,0:T(8,128)S(1)} collective-permute-done((f32[512,256]{1,0:T(8,128)S(1)}, f32[512,256]{1,0:T(8,128)S(1)}, u32[]{:S(2)}, u32[]{:S(2)}) %collective-permute-start.3) | collective-permute-done | bytes 524320 | tf_op jit(solution)/shard_map/ppermute | solution.py:219
  43.2 0.0 copy-done.2
  43.2 0.0 copy-done.3
  43.2 1.5 %rows.1 = (f32[32,3,8,128]{3,2,1,0:T(8,128)}, bf16[2,512,256]{2,1,0:T(8,128)(2,1)S(1)}, bf16[2,512,256]{2,1,0:T(8,128)(2,1)S(1)}) custom-call(f32[1,32,2048]{2,1,0:T(8,128)S(1)} %copy-done.1, f32[1,32,2048]{2,1,0:T(8,128)S(1)} %collective-permute-done.f1, f32[1,32,2048]{2,1,0:T(8,128)S(1)} %collective-permute-done.1.f2, ...), custom_call_target="tpu_custom_call" | custom-call | tf_op jit(solution)/shard_map/rows/pallas_call | solution.py:238
  44.6 0.0 copy-start.4
  44.6 8.9 %all-to-all-start.1 = ((f32[32,3,8,128]{3,2,1,0:T(8,128)}), f32[32,3,8,128]{3,2,1,0:T(8,128)S(1)}, u32[]{:S(2)}, u32[]{:S(2)}) async-start(f32[32,3,8,128]{3,2,1,0:T(8,128)} %get-tuple-element.18), calls=%async_computation.1 | async-start | bytes 786432 | tf_op jit(solution)/shard_map/all_to_all | solution.py:215
  53.6 2.2 %collective-permute-start.4 = (f32[512,256]{1,0:T(8,128)S(1)}, f32[512,256]{1,0:T(8,128)S(1)}, u32[]{:S(2)}, u32[]{:S(2)}) collective-permute-start(f32[512,256]{1,0:T(8,128)S(1)} %bitcast.19), channel_id=1, source_target_pairs={{0,128},{128,0},{1,129},{129,1},{2,130},{130,2},{3,131},{131,3},{4... | collective-permute-start | bytes 1572872 | tf_op jit(solution)/shard_map/ppermute | solution.py:220
  55.8 3.8 %collective-permute-start.5 = (f32[512,256]{1,0:T(8,128)S(1)}, f32[512,256]{1,0:T(8,128)S(1)}, u32[]{:S(2)}, u32[]{:S(2)}) collective-permute-start(f32[512,256]{1,0:T(8,128)S(1)} %bitcast.20), channel_id=1, source_target_pairs={{0,192},{64,128},{128,64},{192,0},{1,193},{65,129},{129,65},{193,1... | collective-permute-start | bytes 1572872 | tf_op jit(solution)/shard_map/ppermute | solution.py:221
  59.6 12.7 %collective-permute-done.4.near_mine = f32[512,256]{1,0:T(8,128)S(1)} collective-permute-done((f32[512,256]{1,0:T(8,128)S(1)}, f32[512,256]{1,0:T(8,128)S(1)}, u32[]{:S(2)}, u32[]{:S(2)}) %collective-permute-start.4) | collective-permute-done | bytes 524320 | tf_op jit(solution)/shard_map/ppermute | solution.py:220
  72.4 11.5 %collective-permute-done.5.near_other = f32[512,256]{1,0:T(8,128)S(1)} collective-permute-done((f32[512,256]{1,0:T(8,128)S(1)}, f32[512,256]{1,0:T(8,128)S(1)}, u32[]{:S(2)}, u32[]{:S(2)}) %collective-permute-start.5) | collective-permute-done | bytes 524320 | tf_op jit(solution)/shard_map/ppermute | solution.py:221
  83.9 0.0 all-to-all-done.1.x_ref
  83.9 0.0 copy-start.5
  83.9 0.0 copy-done.4
  83.9 0.6 copy-done.5
  84.6 2.4 %middle.1 = (f32[64,16,128]{2,1,0:T(8,128)S(1)}, bf16[2,512,256]{2,1,0:T(8,128)(2,1)S(1)}, bf16[2,512,256]{2,1,0:T(8,128)(2,1)S(1)}) custom-call(f32[32,3,8,128]{3,2,1,0:T(8,128)S(1)} %all-to-all-done.1.x_ref, f32[512,256]{1,0:T(8,128)S(1)} %collective-permute-done.4.near_mine, f32[512,256]{1,0:T(8,128)S(1)} %collective-permute-done.5.near_other, ...), custom_call_target="tpu_custom_call" | custom-call | tf_op jit(solution)/shard_map/middle/pallas_call | solution.py:247
  87.0 26.6 %all_to_all.20.x_ref = f32[64,16,128]{2,1,0:T(8,128)S(1)} all-to-all(f32[64,16,128]{2,1,0:T(8,128)S(1)} %get-tuple-element.21), channel_id=1, replica_groups=mesh['u'=2,'v'=2,'c'=2,'h'=4,'l'=2,'z'=8] {'u','v','l','z'}, dimensions={0} | all-to-all | bytes 1048576 | tf_op jit(solution)/shard_map/all_to_all | solution.py:215
  113.5 0.8 last.1
  114.4 6.3 %all_to_all.21 = f32[2,2,32,1024]{3,2,1,0:T(8,128)S(1)} all-to-all(f32[2,2,32,1024]{3,2,1,0:T(8,128)S(1)} %last.1), channel_id=1, replica_groups=mesh['u'=2,'v'=2,'c'=2,'h'=4,'l'=2,'z'=8] {'c'}, dimensions={0} | all-to-all | bytes 1048576 | tf_op jit(solution)/shard_map/all_to_all | solution.py:215
  120.8 0.8 maximum_bitcast_fusion
  (2 shorter events, 0.0 us)
Async XLA Ops:
  0.6 0.8 copy-start
  2.2 17.3 %copy-start.1 = (f32[1,32,2048]{2,1,0:T(8,128)S(1)}, f32[1,32,2048]{2,1,0:T(8,128)}, u32[]{:S(2)}) copy-start(f32[1,32,2048]{2,1,0:T(8,128)} %f0) | copy-start | bytes 786436
  2.2 40.9 %copy-start.2 = (s32[32,2048]{1,0:T(8,128)S(1)}, s32[32,2048]{1,0:T(8,128)}, u32[]{:S(2)}) copy-start(s32[32,2048]{1,0:T(8,128)} %rate_ref.1) | copy-start | bytes 786436
  2.2 40.9 %copy-start.3 = (s32[2048]{0:T(1024)S(1)}, s32[2048]{0:T(1024)}, u32[]{:S(2)}) copy-start(s32[2048]{0:T(1024)} %param.9) | copy-start | bytes 24580
  2.2 36.0 %all-to-all-start = ((f32[64,8,256]{2,1,0:T(8,128)}), f32[64,8,256]{2,1,0:T(8,128)S(1)}, u32[]{:S(2)}, u32[]{:S(2)}) async-start(f32[64,8,256]{2,1,0:T(8,128)} %broadcast_in_dim.14), calls=%async_computation | async-start | bytes 1048576 | tf_op jit(solution)/shard_map/all_to_all | solution.py:215
  19.5 8.3 %collective-permute-start = (f32[1,32,2048]{2,1,0:T(8,128)S(1)}, f32[1,32,2048]{2,1,0:T(8,128)S(1)}, u32[]{:S(2)}, u32[]{:S(2)}) collective-permute-start(f32[1,32,2048]{2,1,0:T(8,128)S(1)} %copy-done.1), channel_id=1, source_target_pairs={{0,64},{64,0},{1,65},{65,1},{2,66},{66,2},{3,67},{67,3},{4,68},{68... | collective-permute-start | bytes 786440 | tf_op jit(solution)/shard_map/ppermute | solution.py:219
  22.4 9.8 %collective-permute-start.1 = (f32[1,32,2048]{2,1,0:T(8,128)S(1)}, f32[1,32,2048]{2,1,0:T(8,128)S(1)}, u32[]{:S(2)}, u32[]{:S(2)}) collective-permute-start(f32[1,32,2048]{2,1,0:T(8,128)S(1)} %copy-done.1), channel_id=1, source_target_pairs={{0,128},{128,0},{1,129},{129,1},{2,130},{130,2},{3,131},{131,3},{4... | collective-permute-start | bytes 786440 | tf_op jit(solution)/shard_map/ppermute | solution.py:220
  25.5 12.7 %collective-permute-start.2 = (f32[1,32,2048]{2,1,0:T(8,128)S(1)}, f32[1,32,2048]{2,1,0:T(8,128)S(1)}, u32[]{:S(2)}, u32[]{:S(2)}) collective-permute-start(f32[1,32,2048]{2,1,0:T(8,128)S(1)} %copy-done.1), channel_id=1, source_target_pairs={{0,192},{64,128},{128,64},{192,0},{1,193},{65,129},{129,65},{193,1... | collective-permute-start | bytes 786440 | tf_op jit(solution)/shard_map/ppermute | solution.py:221
  38.2 4.9 %collective-permute-start.3 = (f32[512,256]{1,0:T(8,128)S(1)}, f32[512,256]{1,0:T(8,128)S(1)}, u32[]{:S(2)}, u32[]{:S(2)}) collective-permute-start(f32[512,256]{1,0:T(8,128)S(1)} %bitcast.17), channel_id=1, source_target_pairs={{0,64},{64,0},{1,65},{65,1},{2,66},{66,2},{3,67},{67,3},{4,68},{68... | collective-permute-start | bytes 1572872 | tf_op jit(solution)/shard_map/ppermute | solution.py:219
  44.6 39.3 %copy-start.4 = (s32[2048]{0:T(1024)S(1)}, s32[2048]{0:T(1024)}, u32[]{:S(2)}) copy-start(s32[2048]{0:T(1024)} %param.10) | copy-start | bytes 24580
  44.6 39.3 %all-to-all-start.1 = ((f32[32,3,8,128]{3,2,1,0:T(8,128)}), f32[32,3,8,128]{3,2,1,0:T(8,128)S(1)}, u32[]{:S(2)}, u32[]{:S(2)}) async-start(f32[32,3,8,128]{3,2,1,0:T(8,128)} %get-tuple-element.18), calls=%async_computation.1 | async-start | bytes 786432 | tf_op jit(solution)/shard_map/all_to_all | solution.py:215
  53.6 18.8 %collective-permute-start.4 = (f32[512,256]{1,0:T(8,128)S(1)}, f32[512,256]{1,0:T(8,128)S(1)}, u32[]{:S(2)}, u32[]{:S(2)}) collective-permute-start(f32[512,256]{1,0:T(8,128)S(1)} %bitcast.19), channel_id=1, source_target_pairs={{0,128},{128,0},{1,129},{129,1},{2,130},{130,2},{3,131},{131,3},{4... | collective-permute-start | bytes 1572872 | tf_op jit(solution)/shard_map/ppermute | solution.py:220
  55.8 28.1 %collective-permute-start.5 = (f32[512,256]{1,0:T(8,128)S(1)}, f32[512,256]{1,0:T(8,128)S(1)}, u32[]{:S(2)}, u32[]{:S(2)}) collective-permute-start(f32[512,256]{1,0:T(8,128)S(1)} %bitcast.20), channel_id=1, source_target_pairs={{0,192},{64,128},{128,64},{192,0},{1,193},{65,129},{129,65},{193,1... | collective-permute-start | bytes 1572872 | tf_op jit(solution)/shard_map/ppermute | solution.py:221
  83.9 0.7 copy-start.5

commit v3 on v2

--- a/solution.py
+++ b/solution.py
@@ -84,23 +84,27 @@
 
 
 def rows_kernel(
-    f0, f1, f2, f3, mine_ref, other_ref, rate_ref, class_ref, out_ref, high_ref, low_ref
+    f0, f1, f2, f3, mine_ref, other_ref, rate_ref, class_ref, table_ref,
+    out_ref, high_ref, low_ref,
 ):
     c, v = lax.axis_index("c"), lax.axis_index("v")
     fields = (f0, f1, f2, f3)
 
-    def columns(ref, b, more, width):
-        at = pl.multiple_of(c * 1024 + b * BLOCK + more, width)
+    def columns(ref, at, width):
+        at = pl.multiple_of(at, width)
         return ref[..., pl.ds(at, width)].reshape(PIECE, width)
 
     lines = jnp.concatenate(
-        [columns(f, b, 0, BLOCK) for f in fields for b in range(2)], axis=0
+        [columns(f, b * BLOCK, BLOCK) for f in fields for b in range(2)], axis=0
     )
-    same = jnp.concatenate(
-        [columns(f, b, v * HALF, HALF) for f in fields for b in range(2)], axis=0
-    )
-    rate = [columns(rate_ref, b, v * HALF, HALF).astype(F32) for b in range(2)]
-    rate = jnp.concatenate(rate + rate, axis=0)
+    at = [b * BLOCK + v * HALF for b in range(2)]
+    same = jnp.concatenate([columns(f, a, HALF) for f in fields for a in at], axis=0)
+    rate = [columns(rate_ref, c * 1024 + a, HALF) for a in at]
+    rate = jnp.concatenate(rate, axis=0)
+    decays = jnp.zeros(rate.shape, F32)
+    for k in range(16):
+        decays = jnp.where(rate == k, table_ref[k], decays)
+    decays = jnp.concatenate([decays, decays], axis=0)
     for k, ref in enumerate((mine_ref, other_ref)):
         high, low = split(ref[...])
         high_ref[k] = high
@@ -110,12 +114,12 @@
     for n in range(2):
         at = slice(n * LANES, (n + 1) * LANES)
         for place in range(3):
-            tile = rate if place == 2 else solved[place * LANES : (place + 1) * LANES]
+            tile = decays if place == 2 else solved[place * LANES : (place + 1) * LANES]
             out_ref[n * 16 : (n + 1) * 16, place] = tile[:, at].T.reshape(16, 8, LANES)
 
 
 def middle_kernel(
-    x_ref, near_mine, near_other, class_ref, table_ref, high_ref, low_ref,
+    x_ref, near_mine, near_other, class_ref, high_ref, low_ref,
     out_ref, far_high, far_low, a_ref, r_ref,
 ):
     c, v, u = lax.axis_index("c"), lax.axis_index("v"), lax.axis_index("u")
@@ -134,10 +138,7 @@
         block = made[b].reshape(4, 8, LANES)
         for q in range(4):
             r_ref[b, :, q * LANES : (q + 1) * LANES] = block[q]
-    rate = r_ref[...].reshape(16, BLOCK)
-    decays = jnp.zeros_like(rate)
-    for k in range(16):
-        decays = jnp.where(rate == float(k), table_ref[k], decays)
+    decays = r_ref[...].reshape(16, BLOCK)
     scaled = jnp.sqrt(1.0 - decays * decays)
 
     place = lax.axis_index(("l", "z"))
@@ -180,7 +181,7 @@
 
 
 def last_kernel(
-    x_ref, class_ref, high_ref, low_ref, far_high, far_low, out_ref
+    x_ref, class_ref, high_ref, low_ref, far_high, far_low, keep_ref, send_ref
 ):
     c, v = lax.axis_index("c"), lax.axis_index("v")
     pieces = [[], []]
@@ -195,12 +196,19 @@
     halves = [(high_ref, low_ref), (far_high, far_low)]
     solved = solve_adjoint(lines, mask, v, halves)
     for n, value in enumerate((field, solved)):
-        for t in range(2):
+        times = value[: 2 * PIECE], value[2 * PIECE :]
+        for ref, first in ((keep_ref, 0), (send_ref, 1)):
+            chosen = jnp.where(c == first, times[0], times[1])
             for b in range(2):
-                first = (t * 2 + b) * PIECE
-                out_ref[t, n, :, b * BLOCK : (b + 1) * BLOCK] = value[
-                    first : first + PIECE
-                ]
+                lines = chosen[b * PIECE : (b + 1) * PIECE]
+                ref[n, :, b * BLOCK : (b + 1) * BLOCK] = lines
+
+
+def join_kernel(keep_ref, got_ref, field_ref, adjoint_ref):
+    c = lax.axis_index("c")
+    for n, ref in enumerate((field_ref, adjoint_ref)):
+        for part, place in ((keep_ref, c), (got_ref, 1 - c)):
+            ref[0, :, pl.ds(pl.multiple_of(place * 1024, 1024), 1024)] = part[n]
 
 
 def vmem(count):
@@ -215,11 +223,8 @@
     return lax.all_to_all(values, axis, split_axis=0, concat_axis=0, tiled=True)
 
 
-def to_partners(values):
-    core = lax.ppermute(values, "c", [(0, 1), (1, 0)])
-    near = lax.ppermute(values, "v", [(0, 1), (1, 0)])
-    both = lax.ppermute(values, ("v", "c"), [(k, 3 - k) for k in range(4)])
-    return core, near, both
+CORE = [(0, 1), (1, 0)]
+BOTH = [(k, 3 - k) for k in range(4)]
 
 
 def per_device(forcing, rate_class, rate_table, row_class, col_class, offsets):
@@ -227,27 +232,39 @@
     row_lines = row_class.reshape(-1, LANES)
     col_lines = col_class.reshape(-1, LANES)
 
-    fields = (forcing,) + to_partners(forcing)
     rows = offsets.shape[1]
     piece = lax.dynamic_slice(offsets, (c, 0, v * HALF), (1, rows, HALF))
     pieces = jnp.broadcast_to(piece, (BLOCK // rows, rows, HALF))
     mine = swap(pieces, ROWS).reshape(BLOCK, HALF)
+
+    field = lax.dynamic_slice(forcing[0], (0, c * 1024), (PIECE, 1024))
+    cross = lax.dynamic_slice(forcing[0], (0, (1 - c) * 1024), (PIECE, 1024))
+    fields = (
+        field,
+        lax.ppermute(cross, "c", CORE),
+        lax.ppermute(field, "v", CORE),
+        lax.ppermute(cross, ("v", "c"), BOTH),
+    )
     mine, *fields = lax.optimization_barrier((mine,) + fields)
-    other, near_mine, near_other = to_partners(mine)
-
+    other = lax.ppermute(mine, "c", CORE)
+    near_mine = lax.ppermute(mine, "v", CORE)
+    near_other = lax.ppermute(near_mine, "c", CORE)
+
+    smem = pl.BlockSpec(memory_space=pltpu.SMEM)
     out, high, low = pl.pallas_call(
         rows_kernel,
         out_shape=(jax.ShapeDtypeStruct((32, 3, 8, LANES), F32),) + HALVES,
-        in_specs=vmem(8),
+        in_specs=vmem(8) + [smem],
         out_specs=tuple(vmem(3)),
         compiler_params=PARAMS,
         name="rows",
-    )(*fields, mine, other, rate_class, row_lines)
+    )(*fields, mine, other, rate_class, row_lines, rate_table)
     out = swap(out, NEAR)
+    out, near_mine, near_other = lax.optimization_barrier((out, near_mine, near_other))
     out, far_high, far_low = pl.pallas_call(
         middle_kernel,
         out_shape=(jax.ShapeDtypeStruct((64, 16, LANES), F32),) + HALVES,
-        in_specs=vmem(4) + [pl.BlockSpec(memory_space=pltpu.SMEM)] + vmem(2),
+        in_specs=vmem(6),
         out_specs=tuple(vmem(3)),
         scratch_shapes=[
             pltpu.VMEM((2, 2, 4, 8, BLOCK), F32),
@@ -255,20 +272,25 @@
         ],
         compiler_params=PARAMS,
         name="middle",
-    )(out, near_mine, near_other, col_lines, rate_table, high, low)
+    )(out, near_mine, near_other, col_lines, high, low)
     out = swap(out, SPREAD)
-    out = pl.pallas_call(
+    keep, send = pl.pallas_call(
         last_kernel,
-        out_shape=jax.ShapeDtypeStruct((2, 2, PIECE, 1024), F32),
+        out_shape=(jax.ShapeDtypeStruct((2, PIECE, 1024), F32),) * 2,
         in_specs=vmem(6),
-        out_specs=vmem(1)[0],
+        out_specs=tuple(vmem(2)),
         compiler_params=PARAMS,
         name="last",
     )(out, row_lines, high, low, far_high, far_low)
-    out = swap(out, "c")
-    covariance = jnp.concatenate([out[0, 0], out[1, 0]], axis=1)
-    adjoint = jnp.concatenate([out[0, 1], out[1, 1]], axis=1)
-    return covariance[None], adjoint[None]
+    got = lax.ppermute(send, "c", CORE)
+    return pl.pallas_call(
+        join_kernel,
+        out_shape=(jax.ShapeDtypeStruct(forcing.shape, F32),) * 2,
+        in_specs=vmem(2),
+        out_specs=tuple(vmem(2)),
+        compiler_params=PARAMS,
+        name="join",
+    )(keep, got)
 
 
 def solution(mesh):

time: 122 us -> 100 us (0.82)
  waiting for transfers between devices: 36.2 us -> 19 us
  blocking collectives: 32.9 us -> 24.3 us
  starting transfers between devices: 43.9 us -> 48.6 us
    ppermute x6 -> x7, waiting for transfers between devices: 36.2 us -> 10.9 us  [the longest x1 4.1 us: per_device(): lax.ppermute(field, 'v', CORE)]
    all_to_all x2 -> x1, blocking collectives: 32.9 us -> 24.3 us  [swap(): return lax.all_to_all(values, axis, split_axis=0, concat_axis=0, tiled=True)]
    all_to_all x2, waiting for transfers between devices: 0.01 us -> 8.03 us  [swap(): return lax.all_to_all(values, axis, split_axis=0, concat_axis=0, tiled=True)]
    ppermute x6 -> x7, starting transfers between devices: 17.8 us -> 24.7 us  [the longest x1 5.91 us: per_device(): other = lax.ppermute(mine, 'c', CORE)]
    all_to_all x2, starting transfers between devices: 26.2 us -> 23.9 us  [swap(): return lax.all_to_all(values, axis, split_axis=0, concat_axis=0, tiled=True)]
  transfers between devices with their start and end apart: 8 -> 9, of which waited for: 5 -> 7; matrix products, arithmetic and copies ran while one was open for 0% -> 0% of each run, Pallas kernels for 0% -> 2%
where the time goes in v3:
time: 100 us; the launch traced here: 99.8 us
  starting transfers between devices  48.6 us (49%)
  blocking collectives  24.3 us (24%)
  waiting for transfers between devices  19 us (19%)
  Pallas kernels  5.54 us (6%)
  local copies, waits for them, and re-layouts  1.63 us (2%)
    all_to_all x1, blocking collectives, swap(): return lax.all_to_all(values, axis, split_axis=0, concat_axis=0, tiled=True)  24.3 us
    all_to_all x2, starting transfers between devices, swap(): return lax.all_to_all(values, axis, split_axis=0, concat_axis=0, tiled=True)  23.9 us
    all_to_all x2, waiting for transfers between devices, swap(): return lax.all_to_all(values, axis, split_axis=0, concat_axis=0, tiled=True)  8.03 us
    ppermute x1, starting transfers between devices, per_device(): other = lax.ppermute(mine, 'c', CORE)  5.91 us
    ppermute x1, starting transfers between devices, per_device(): got = lax.ppermute(send, 'c', CORE)  4.69 us
    ppermute x1, waiting for transfers between devices, per_device(): lax.ppermute(field, 'v', CORE)  4.1 us
    ppermute x1, starting transfers between devices, per_device(): lax.ppermute(cross, ('v', 'c'), BOTH)  4.09 us
    ppermute x1, waiting for transfers between devices, per_device(): near_mine = lax.ppermute(mine, 'v', CORE)  3.99 us
  transfers between devices with their start and end apart: 9, of which 7 were waited for; matrix products, arithmetic and copies ran while one was open for 0% of the time, Pallas kernels for 2%

profile of v3, /device:TPU:1, one launch (start us, length us, event | category | flops | bytes accessed | tf_op | source)
XLA Modules:
  0.0 99.8 jit_solution(6955735542209684928)
XLA Ops:
  0.6 0.0 copy-start
  0.7 0.7 copy-done
  1.4 0.8 broadcast_in_dim.8
  2.2 0.0 copy-start.5
  2.2 17.3 %all-to-all-start = ((f32[64,8,256]{2,1,0:T(8,128)}), f32[64,8,256]{2,1,0:T(8,128)S(1)}, u32[]{:S(2)}, u32[]{:S(2)}) async-start(f32[64,8,256]{2,1,0:T(8,128)} %broadcast_in_dim.8), calls=%async_computation | async-start | bytes 1048576 | tf_op jit(solution)/shard_map/all_to_all | solution.py:223
  19.5 0.0 copy-done.5
  19.5 0.0 copy-start.1
  19.5 0.0 copy-start.2
  19.6 4.1 %collective-permute-start.2 = (f32[32,1024]{1,0:T(8,128)S(1)}, f32[32,1024]{1,0:T(8,128)S(1)}, u32[]{:S(2)}, u32[]{:S(2)}) collective-permute-start(f32[32,1024]{1,0:T(8,128)S(1)} %get-tuple-element.34), channel_id=1, source_target_pairs={{0,192},{64,128},{128,64},{192,0},{1,193},{65,129},{129,65},{193,1... | collective-permute-start | bytes 393224 | tf_op jit(solution)/shard_map/ppermute | solution.py:246
  23.7 1.9 %collective-permute-start = (f32[32,1024]{1,0:T(8,128)S(1)}, f32[32,1024]{1,0:T(8,128)S(1)}, u32[]{:S(2)}, u32[]{:S(2)}) collective-permute-start(f32[32,1024]{1,0:T(8,128)S(1)} %get-tuple-element.34), channel_id=1, source_target_pairs={{0,64},{64,0},{1,65},{65,1},{2,66},{66,2},{3,67},{67,3},{4,68},{68... | collective-permute-start | bytes 393224 | tf_op jit(solution)/shard_map/ppermute | solution.py:244
  25.6 2.2 %collective-permute-start.1 = (f32[32,1024]{1,0:T(8,128)S(1)}, f32[32,1024]{1,0:T(8,128)S(1)}, u32[]{:S(2)}, u32[]{:S(2)}) collective-permute-start(f32[32,1024]{1,0:T(8,128)S(1)} %get-tuple-element.18.f0), channel_id=1, source_target_pairs={{0,128},{128,0},{1,129},{129,1},{2,130},{130,2},{3,131},{131,3},{4... | collective-permute-start | bytes 393224 | tf_op jit(solution)/shard_map/ppermute | solution.py:245
  27.8 0.2 collective-permute-done.2.f3
  28.0 0.0 collective-permute-done.f1
  28.0 4.1 %collective-permute-done.1.f2 = f32[32,1024]{1,0:T(8,128)S(1)} collective-permute-done((f32[32,1024]{1,0:T(8,128)S(1)}, f32[32,1024]{1,0:T(8,128)S(1)}, u32[]{:S(2)}, u32[]{:S(2)}) %collective-permute-start.1) | collective-permute-done | bytes 131104 | tf_op jit(solution)/shard_map/ppermute | solution.py:245
  32.1 3.8 %all-to-all-done = f32[64,8,256]{2,1,0:T(8,128)S(1)} async-done(((f32[64,8,256]{2,1,0:T(8,128)}), f32[64,8,256]{2,1,0:T(8,128)S(1)}, u32[]{:S(2)}, u32[]{:S(2)}) %all-to-all-start) | async-done | bytes 524320 | tf_op jit(solution)/shard_map/all_to_all | solution.py:223
  35.9 0.0 copy-start.4
  35.9 5.9 %collective-permute-start.3 = (f32[512,256]{1,0:T(8,128)S(1)}, f32[512,256]{1,0:T(8,128)S(1)}, u32[]{:S(2)}, u32[]{:S(2)}) collective-permute-start(f32[512,256]{1,0:T(8,128)S(1)} %bitcast.9), channel_id=1, source_target_pairs={{0,64},{64,0},{1,65},{65,1},{2,66},{66,2},{3,67},{67,3},{4,68},{68... | collective-permute-start | bytes 1572872 | tf_op jit(solution)/shard_map/ppermute | solution.py:249
  41.8 3.1 %collective-permute-start.4 = (f32[512,256]{1,0:T(8,128)S(1)}, f32[512,256]{1,0:T(8,128)S(1)}, u32[]{:S(2)}, u32[]{:S(2)}) collective-permute-start(f32[512,256]{1,0:T(8,128)S(1)} %bitcast.10), channel_id=1, source_target_pairs={{0,128},{128,0},{1,129},{129,1},{2,130},{130,2},{3,131},{131,3},{4... | collective-permute-start | bytes 1572872 | tf_op jit(solution)/shard_map/ppermute | solution.py:250
  44.9 0.0 collective-permute-done.3.other_ref
  44.9 0.0 copy-done.1
  44.9 0.0 copy-done.2
  44.9 0.0 copy-done.4
  44.9 2.0 %rows.1 = (f32[32,3,8,128]{3,2,1,0:T(8,128)}, bf16[2,512,256]{2,1,0:T(8,128)(2,1)S(1)}, bf16[2,512,256]{2,1,0:T(8,128)(2,1)S(1)}) custom-call(f32[32,1024]{1,0:T(8,128)S(1)} %get-tuple-element.18.f0, f32[32,1024]{1,0:T(8,128)S(1)} %collective-permute-done.f1, f32[32,1024]{1,0:T(8,128)S(1)} %collective-permute-done.1.f2, ...), custom_call_target="tpu_custom_call" | custom-call | tf_op jit(solution)/shard_map/rows/pallas_call | solution.py:254
  47.0 0.0 copy-start.3
  47.0 6.6 %all-to-all-start.1 = ((f32[32,3,8,128]{3,2,1,0:T(8,128)}), f32[32,3,8,128]{3,2,1,0:T(8,128)S(1)}, u32[]{:S(2)}, u32[]{:S(2)}) async-start(f32[32,3,8,128]{3,2,1,0:T(8,128)} %get-tuple-element.23), calls=%async_computation.1 | async-start | bytes 786432 | tf_op jit(solution)/shard_map/all_to_all | solution.py:223
  53.6 4.0 %collective-permute-done.4.near_mine = f32[512,256]{1,0:T(8,128)S(1)} collective-permute-done((f32[512,256]{1,0:T(8,128)S(1)}, f32[512,256]{1,0:T(8,128)S(1)}, u32[]{:S(2)}, u32[]{:S(2)}) %collective-permute-start.4) | collective-permute-done | bytes 524320 | tf_op jit(solution)/shard_map/ppermute | solution.py:250
  57.6 2.8 %collective-permute-start.5 = (f32[512,256]{1,0:T(8,128)S(1)}, f32[512,256]{1,0:T(8,128)S(1)}, u32[]{:S(2)}, u32[]{:S(2)}) collective-permute-start(f32[512,256]{1,0:T(8,128)S(1)} %collective-permute-done.4.near_mine), channel_id=1, source_target_pairs={{0,64},{64,0},{1,65},{65,1},{2,66},{66,2},{3,67},{67,3},{4,68},{68... | collective-permute-start | bytes 1572872 | tf_op jit(solution)/shard_map/ppermute | solution.py:251
  60.4 1.5 %collective-permute-done.5.near_other = f32[512,256]{1,0:T(8,128)S(1)} collective-permute-done((f32[512,256]{1,0:T(8,128)S(1)}, f32[512,256]{1,0:T(8,128)S(1)}, u32[]{:S(2)}, u32[]{:S(2)}) %collective-permute-start.5) | collective-permute-done | bytes 524320 | tf_op jit(solution)/shard_map/ppermute | solution.py:251
  62.0 4.2 %all-to-all-done.1.x_ref = f32[32,3,8,128]{3,2,1,0:T(8,128)S(1)} async-done(((f32[32,3,8,128]{3,2,1,0:T(8,128)}), f32[32,3,8,128]{3,2,1,0:T(8,128)S(1)}, u32[]{:S(2)}, u32[]{:S(2)}) %all-to-all-start.1) | async-done | bytes 393248 | tf_op jit(solution)/shard_map/all_to_all | solution.py:223
  66.2 0.0 copy-done.3
  66.2 1.8 %middle.1 = (f32[64,16,128]{2,1,0:T(8,128)S(1)}, bf16[2,512,256]{2,1,0:T(8,128)(2,1)S(1)}, bf16[2,512,256]{2,1,0:T(8,128)(2,1)S(1)}) custom-call(f32[32,3,8,128]{3,2,1,0:T(8,128)S(1)} %all-to-all-done.1.x_ref, f32[512,256]{1,0:T(8,128)S(1)} %collective-permute-done.4.near_mine, f32[512,256]{1,0:T(8,128)S(1)} %collective-permute-done.5.near_other, ...), custom_call_target="tpu_custom_call" | custom-call | tf_op jit(solution)/shard_map/middle/pallas_call | solution.py:264
  68.0 24.3 %all_to_all.15.x_ref = f32[64,16,128]{2,1,0:T(8,128)S(1)} all-to-all(f32[64,16,128]{2,1,0:T(8,128)S(1)} %get-tuple-element.29), channel_id=1, replica_groups=mesh['u'=2,'v'=2,'c'=2,'h'=4,'l'=2,'z'=8] {'u','v','l','z'}, dimensions={0} | all-to-all | bytes 1048576 | tf_op jit(solution)/shard_map/all_to_all | solution.py:223
  92.3 0.8 last.1
  93.2 4.7 %collective-permute-start.6 = (f32[2,32,1024]{2,1,0:T(8,128)S(1)}, f32[2,32,1024]{2,1,0:T(8,128)S(1)}, u32[]{:S(2)}, u32[]{:S(2)}) collective-permute-start(f32[2,32,1024]{2,1,0:T(8,128)S(1)} %get-tuple-element.33), channel_id=1, source_target_pairs={{0,64},{64,0},{1,65},{65,1},{2,66},{66,2},{3,67},{67,3},{4,68},{68... | collective-permute-start | bytes 786440 | tf_op jit(solution)/shard_map/ppermute | solution.py:285
  97.9 1.1 %collective-permute-done.6.got_ref = f32[2,32,1024]{2,1,0:T(8,128)S(1)} collective-permute-done((f32[2,32,1024]{2,1,0:T(8,128)S(1)}, f32[2,32,1024]{2,1,0:T(8,128)S(1)}, u32[]{:S(2)}, u32[]{:S(2)}) %collective-permute-start.6) | collective-permute-done | bytes 262176 | tf_op jit(solution)/shard_map/ppermute | solution.py:285
  99.0 0.8 join.1
  (2 shorter events, 0.0 us)
Async XLA Ops:
  0.6 0.8 copy-start
  2.2 17.3 %copy-start.5 = (f32[1,32,2048]{2,1,0:T(8,128)S(1)}, f32[1,32,2048]{2,1,0:T(8,128)}, u32[]{:S(2)}) copy-start(f32[1,32,2048]{2,1,0:T(8,128)} %param.6) | copy-start | bytes 786436
  2.2 33.6 %all-to-all-start = ((f32[64,8,256]{2,1,0:T(8,128)}), f32[64,8,256]{2,1,0:T(8,128)S(1)}, u32[]{:S(2)}, u32[]{:S(2)}) async-start(f32[64,8,256]{2,1,0:T(8,128)} %broadcast_in_dim.8), calls=%async_computation | async-start | bytes 1048576 | tf_op jit(solution)/shard_map/all_to_all | solution.py:223
  19.5 25.4 %copy-start.1 = (s32[32,2048]{1,0:T(8,128)S(1)}, s32[32,2048]{1,0:T(8,128)}, u32[]{:S(2)}) copy-start(s32[32,2048]{1,0:T(8,128)} %rate_ref.1) | copy-start | bytes 786436
  19.5 25.4 %copy-start.2 = (s32[2048]{0:T(1024)S(1)}, s32[2048]{0:T(1024)}, u32[]{:S(2)}) copy-start(s32[2048]{0:T(1024)} %param.9) | copy-start | bytes 24580
  19.6 8.4 %collective-permute-start.2 = (f32[32,1024]{1,0:T(8,128)S(1)}, f32[32,1024]{1,0:T(8,128)S(1)}, u32[]{:S(2)}, u32[]{:S(2)}) collective-permute-start(f32[32,1024]{1,0:T(8,128)S(1)} %get-tuple-element.34), channel_id=1, source_target_pairs={{0,192},{64,128},{128,64},{192,0},{1,193},{65,129},{129,65},{193,1... | collective-permute-start | bytes 393224 | tf_op jit(solution)/shard_map/ppermute | solution.py:246
  23.7 4.3 %collective-permute-start = (f32[32,1024]{1,0:T(8,128)S(1)}, f32[32,1024]{1,0:T(8,128)S(1)}, u32[]{:S(2)}, u32[]{:S(2)}) collective-permute-start(f32[32,1024]{1,0:T(8,128)S(1)} %get-tuple-element.34), channel_id=1, source_target_pairs={{0,64},{64,0},{1,65},{65,1},{2,66},{66,2},{3,67},{67,3},{4,68},{68... | collective-permute-start | bytes 393224 | tf_op jit(solution)/shard_map/ppermute | solution.py:244
  25.6 6.5 %collective-permute-start.1 = (f32[32,1024]{1,0:T(8,128)S(1)}, f32[32,1024]{1,0:T(8,128)S(1)}, u32[]{:S(2)}, u32[]{:S(2)}) collective-permute-start(f32[32,1024]{1,0:T(8,128)S(1)} %get-tuple-element.18.f0), channel_id=1, source_target_pairs={{0,128},{128,0},{1,129},{129,1},{2,130},{130,2},{3,131},{131,3},{4... | collective-permute-start | bytes 393224 | tf_op jit(solution)/shard_map/ppermute | solution.py:245
  35.9 9.1 %copy-start.4 = (f32[16]{0:T(128)S(1)}, f32[16]{0:T(128)}, u32[]{:S(2)}) copy-start(f32[16]{0:T(128)} %table_ref.1) | copy-start | bytes 196
  35.9 9.0 %collective-permute-start.3 = (f32[512,256]{1,0:T(8,128)S(1)}, f32[512,256]{1,0:T(8,128)S(1)}, u32[]{:S(2)}, u32[]{:S(2)}) collective-permute-start(f32[512,256]{1,0:T(8,128)S(1)} %bitcast.9), channel_id=1, source_target_pairs={{0,64},{64,0},{1,65},{65,1},{2,66},{66,2},{3,67},{67,3},{4,68},{68... | collective-permute-start | bytes 1572872 | tf_op jit(solution)/shard_map/ppermute | solution.py:249
  41.8 15.8 %collective-permute-start.4 = (f32[512,256]{1,0:T(8,128)S(1)}, f32[512,256]{1,0:T(8,128)S(1)}, u32[]{:S(2)}, u32[]{:S(2)}) collective-permute-start(f32[512,256]{1,0:T(8,128)S(1)} %bitcast.10), channel_id=1, source_target_pairs={{0,128},{128,0},{1,129},{129,1},{2,130},{130,2},{3,131},{131,3},{4... | collective-permute-start | bytes 1572872 | tf_op jit(solution)/shard_map/ppermute | solution.py:250
  47.0 19.2 %copy-start.3 = (s32[2048]{0:T(1024)S(1)}, s32[2048]{0:T(1024)}, u32[]{:S(2)}) copy-start(s32[2048]{0:T(1024)} %param.10) | copy-start | bytes 24580
  47.0 19.2 %all-to-all-start.1 = ((f32[32,3,8,128]{3,2,1,0:T(8,128)}), f32[32,3,8,128]{3,2,1,0:T(8,128)S(1)}, u32[]{:S(2)}, u32[]{:S(2)}) async-start(f32[32,3,8,128]{3,2,1,0:T(8,128)} %get-tuple-element.23), calls=%async_computation.1 | async-start | bytes 786432 | tf_op jit(solution)/shard_map/all_to_all | solution.py:223
  57.6 4.4 %collective-permute-start.5 = (f32[512,256]{1,0:T(8,128)S(1)}, f32[512,256]{1,0:T(8,128)S(1)}, u32[]{:S(2)}, u32[]{:S(2)}) collective-permute-start(f32[512,256]{1,0:T(8,128)S(1)} %collective-permute-done.4.near_mine), channel_id=1, source_target_pairs={{0,64},{64,0},{1,65},{65,1},{2,66},{66,2},{3,67},{67,3},{4,68},{68... | collective-permute-start | bytes 1572872 | tf_op jit(solution)/shard_map/ppermute | solution.py:251
  93.2 5.8 %collective-permute-start.6 = (f32[2,32,1024]{2,1,0:T(8,128)S(1)}, f32[2,32,1024]{2,1,0:T(8,128)S(1)}, u32[]{:S(2)}, u32[]{:S(2)}) collective-permute-start(f32[2,32,1024]{2,1,0:T(8,128)S(1)} %get-tuple-element.33), channel_id=1, source_target_pairs={{0,64},{64,0},{1,65},{65,1},{2,66},{66,2},{3,67},{67,3},{4,68},{68... | collective-permute-start | bytes 786440 | tf_op jit(solution)/shard_map/ppermute | solution.py:285

commit v4 on v2

v4 whole, which is shorter than its diff:
```python
import jax
import jax.numpy as jnp
from jax import lax
from jax.experimental import pallas as pl
from jax.experimental.pallas import tpu as pltpu
from jax.sharding import Mesh
from jax.sharding import PartitionSpec as P

BLOCK = 512
LANES = 128
PIECE = 32
F32 = jnp.float32
BF16 = jnp.bfloat16
ROWS = ("h", "l", "z")
TIME = ("u", "v", "c")
NEAR = ("u", "l", "z")
SPREAD = ("u", "v", "c", "l", "z")


def split(values):
    high = values.astype(BF16)
    return high, (values - high.astype(F32)).astype(BF16)


def product(both, high, low, adjoint):
    dims = (((1,), (1 if adjoint else 0,)), ((), ()))
    count = both.shape[0] // 2
    wide = lax.dot_general(both, high, dims, preferred_element_type=F32)
    small = lax.dot_general(both[:count], low, dims, preferred_element_type=F32)
    return wide[:count] + (wide[count:] + small)


def own_first(lines, v, c):
    quarters = [lines[:, k * LANES : (k + 1) * LANES] for k in range(4)]
    quarters = [jnp.where(v == 0, quarters[k], quarters[(k + 2) % 4]) for k in range(4)]
    quarters = [jnp.where(c == 0, quarters[k], quarters[k ^ 1]) for k in range(4)]
    return jnp.concatenate(quarters, axis=1)


def matrix(own_ref, rest_ref, k):
    return jnp.concatenate([own_ref[:, k * LANES : (k + 1) * LANES], rest_ref[k]], axis=1)


def solve(lines, mask, matrices, adjoint):
    own_high, own_low, rest_high, rest_low = matrices
    both = jnp.concatenate(split(lines), axis=0)
    parts = []
    for k in range(2):
        high, low = matrix(own_high, rest_high, k), matrix(own_low, rest_low, k)
        parts.append(product(both, high, low, adjoint))
    return jnp.where(mask, parts[0], parts[1])


def exchange_lanes(tiles):
    group = lax.broadcasted_iota(jnp.int32, tiles[0].shape, 1) // PIECE
    out = []
    for place in range(4):
        made = None
        for source in range(4):
            turn = ((source - place) % 4) * PIECE
            rolled = pltpu.roll(tiles[source], turn, 1) if turn else tiles[source]
            made = rolled if made is None else jnp.where(group == source, rolled, made)
        out.append(made)
    return out


def class_marks(line, first, count):
    lane = lax.broadcasted_iota(jnp.int32, (count, LANES), 1)
    row = lax.broadcasted_iota(jnp.int32, (count, LANES), 0)
    picked = jnp.where((lane == row + first) & (line == 0), 1.0, 0.0)
    return jnp.sum(picked, axis=1, keepdims=True)


def row_mask(class_ref, copies):
    place = lax.axis_index(ROWS)
    line = class_ref[pl.ds(place // 4, 1), :]
    marks = class_marks(line, lax.rem(place, 4) * PIECE, PIECE)
    return jnp.concatenate([marks] * copies, axis=0) > 0.5


def lines_kernel(f0, f1, f2, f3, rate_ref, table_ref, both_ref, same_ref, decays_ref):
    quarter = lax.axis_index("v") * 2 + lax.axis_index("c")
    fields = ((f0, f1), (f2, f3))
    at = [pl.multiple_of(b * BLOCK + quarter * LANES, LANES) for b in range(4)]
    for far in range(2):
        for pair in range(2):
            for core in range(2):
                for b in range(2):
                    ref, block = fields[far][core], pair * 2 + b
                    first = (((far * 2 + pair) * 2 + core) * 2 + b) * PIECE
                    rows = pl.ds(first, PIECE)
                    lines = ref[0, :, block * BLOCK : (block + 1) * BLOCK]
                    high, low = split(lines)
                    both_ref[rows, :] = high
                    both_ref[pl.ds(512 + first, PIECE), :] = low
                    same_ref[rows, :] = ref[0, :, pl.ds(at[block], LANES)]
    for pair in range(2):
        rate = [rate_ref[:, pl.ds(at[pair * 2 + b], LANES)] for b in range(2)]
        rate = jnp.concatenate(rate, axis=0)
        decays = jnp.zeros(rate.shape, F32)
        for k in range(16):
            decays = jnp.where(rate == k, table_ref[k], decays)
        decays = jnp.concatenate([decays, decays], axis=0).T.reshape(16, 8, LANES)
        decays_ref[pair * 16 : (pair + 1) * 16] = decays


def rows_kernel(
    both_ref, same_ref, decays_ref, m_ref, class_ref, out_ref, high_ref, low_ref
):
    for k in range(2):
        high, low = split(m_ref[:, k].reshape(BLOCK, LANES))
        high_ref[:, k * LANES : (k + 1) * LANES] = high
        low_ref[:, k * LANES : (k + 1) * LANES] = low
    solved = product(both_ref[...], high_ref[...], low_ref[...], False)
    solved = jnp.where(row_mask(class_ref, 16), solved[:, :LANES], solved[:, LANES:])
    solved = solved + same_ref[...]
    for pair in range(2):
        at = slice(pair * 16, (pair + 1) * 16)
        for far in range(2):
            first = (far * 2 + pair) * LANES
            turned = solved[first : first + LANES].T
            out_ref[at, far] = turned.reshape(16, 8, LANES)
        out_ref[at, 2] = decays_ref[at]


def rest_kernel(m1, m2, m3, high_ref, low_ref):
    for n, ref in enumerate((m1, m2, m3)):
        for k in range(2):
            high, low = split(ref[:, k].reshape(BLOCK, LANES))
            high_ref[k, :, n * LANES : (n + 1) * LANES] = high
            low_ref[k, :, n * LANES : (n + 1) * LANES] = low


def middle_kernel(x_ref, class_ref, h0, l0, h1, l1, out_ref, a_ref, r_ref):
    c, v, u = lax.axis_index("c"), lax.axis_index("v"), lax.axis_index("u")
    tiles = x_ref[...].reshape(2, 4, 4, 3, 8, LANES)
    made = exchange_lanes([tiles[:, :, i, :2].reshape(128, LANES) for i in range(4)])
    for tb in range(4):
        block = made[tb].reshape(2, 4, 2, 8, LANES)
        for q in range(4):
            a_ref[:, :, tb, :, q * LANES : (q + 1) * LANES] = block[:, q]
    made = exchange_lanes([tiles[0, :, i, 2].reshape(32, LANES) for i in range(4)])
    for b in range(2):
        block = made[b].reshape(4, 8, LANES)
        for q in range(4):
            r_ref[b, :, q * LANES : (q + 1) * LANES] = block[q]
    decays = r_ref[...].reshape(16, BLOCK)
    scaled = jnp.sqrt(1.0 - decays * decays)

    place = lax.axis_index(("l", "z"))
    marks = []
    for b in range(2):
        line = class_ref[pl.ds((u * 2 + b) * 4 + v * 2 + c, 1), :]
        marks.append(class_marks(line, place * 8, 8))
    mask = jnp.concatenate(marks * 8, axis=0) > 0.5
    matrices = (h0, l0, h1, l1)
    lines = a_ref[...].reshape(128, BLOCK)
    smoothed = lines + own_first(solve(lines, mask, matrices, False), v, c)
    smoothed = smoothed.reshape(2, 2, 2, 16, BLOCK)
    state, field = None, []
    for t in range(8):
        far, late, core = t // 4, (t // 2) % 2, t % 2
        pair = smoothed[far]
        pair = jnp.where(v == 0, pair[late], pair[1 - late])
        here = scaled * jnp.where(c == 0, pair[core], pair[1 - core])
        state = here if state is None else decays * state + here
        field.append(state)
    state, back = None, [None] * 8
    for t in range(7, -1, -1):
        here = scaled * field[t]
        state = here if state is None else decays * state + here
        back[t] = state
    back = jnp.concatenate(back, axis=0)
    adjoint = back + solve(own_first(back, v, c), mask, matrices, True)
    field = jnp.concatenate(field, axis=0).reshape(4, 4, 8, BLOCK)
    adjoint = adjoint.reshape(4, 4, 8, BLOCK)
    for core in range(2):
        for q in range(4):
            lanes = slice(q * LANES, (q + 1) * LANES)
            tiles = [
                value[:, core * 2 + b, :, lanes].reshape(32, LANES)
                for value in (field, adjoint)
                for b in range(2)
            ]
            made = exchange_lanes(tiles)
            for i in range(4):
                block = made[i].reshape(4, 8, LANES)
                for x in range(4):
                    out_ref[(x * 2 + core) * 16 + q * 4 + i] = block[x]


def last_kernel(x_ref, class_ref, h0, l0, h1, l1, field_ref, adjoint_ref):
    c, v = lax.axis_index("c"), lax.axis_index("v")
    lines = []
    for u in range(2):
        pieces = []
        for k in range(4):
            first = (u * 4 + k) * 16
            turned = x_ref[first : first + 16].reshape(LANES, LANES).T
            for b in range(2):
                at = (u * 2 + b) * BLOCK + k * LANES
                field_ref[0, :, at : at + LANES] = turned[b * PIECE : (b + 1) * PIECE]
            pieces.append(turned[2 * PIECE :])
        lines.append(jnp.concatenate(pieces, axis=1))
    lines = jnp.concatenate(lines, axis=0)
    mask = row_mask(class_ref, 4)
    solved = lines + solve(own_first(lines, v, c), mask, (h0, l0, h1, l1), True)
    for b in range(4):
        piece = solved[b * PIECE : (b + 1) * PIECE]
        adjoint_ref[0, :, b * BLOCK : (b + 1) * BLOCK] = piece


def call(kernel, name, shapes, operands, smem=(), scratch=()):
    vmem = pl.BlockSpec(memory_space=pltpu.VMEM)
    places = [
        pl.BlockSpec(memory_space=pltpu.SMEM) if k in smem else vmem
        for k in range(len(operands))
    ]
    return pl.pallas_call(
        kernel,
        out_shape=tuple(jax.ShapeDtypeStruct(*shape) for shape in shapes),
        in_specs=places,
        out_specs=(vmem,) * len(shapes),
        scratch_shapes=[pltpu.VMEM(shape, F32) for shape in scratch],
        compiler_params=pltpu.CompilerParams(vmem_limit_bytes=40 * 1024 * 1024),
        name=name,
    )(*operands)


def swap(values, axis):
    return lax.all_to_all(values, axis, split_axis=0, concat_axis=0, tiled=True)


def partners(values):
    other = [(0, 1), (1, 0)]
    near = lax.ppermute(values, "v", other)
    core = lax.ppermute(values, "c", other)
    return core, near, lax.ppermute(near, "c", other)


def per_device(forcing, rate_class, rate_table, row_class, col_class, offsets):
    row_lines = row_class.reshape(-1, LANES)
    col_lines = col_class.reshape(-1, LANES)

    quarter = lax.axis_index("v") * 2 + lax.axis_index("c")
    rows = offsets.shape[1]
    piece = lax.dynamic_slice(offsets, (0, 0, quarter * LANES), (2, rows, LANES))
    piece = piece.reshape(2 * rows, LANES)
    own = swap(jnp.broadcast_to(piece, (BLOCK // rows, 2 * rows, LANES)), ROWS)

    shapes = (((1024, BLOCK), BF16), ((512, LANES), F32), ((32, 8, LANES), F32))
    operands = (forcing,) + partners(forcing) + (rate_class, rate_table)
    lines = call(lines_kernel, "lines", shapes, operands, smem=(5,))
    own, *lines = lax.optimization_barrier((own,) + lines)
    own = own.reshape(-1, 2, rows, LANES)
    rest = partners(own)

    shapes = (((32, 3, 8, LANES), F32),) + (((BLOCK, 256), BF16),) * 2
    operands = (*lines, own, row_lines)
    out, *own = call(rows_kernel, "rows", shapes, operands)
    out = swap(out, NEAR)
    shapes = (((2, BLOCK, 384), BF16),) * 2
    rest = call(rest_kernel, "rest", shapes, rest)
    out, *rest = lax.optimization_barrier((out,) + rest)
    matrices = (*own, *rest)
    (out,) = call(
        middle_kernel,
        "middle",
        (((128, 8, LANES), F32),),
        (out, col_lines) + matrices,
        scratch=((2, 2, 4, 8, BLOCK), (2, 8, BLOCK)),
    )
    out = swap(out, SPREAD)
    shapes = ((forcing.shape, F32),) * 2
    return call(last_kernel, "last", shapes, (out, row_lines) + matrices)


def solution(mesh):
    devices = mesh.devices
    tm, row = devices.shape
    fine = Mesh(
        devices.reshape(tm // 4, 2, 2, row // 16, 2, 8), ("u", "v", "c", "h", "l", "z")
    )
    field = P(TIME, ROWS, None)
    return jax.shard_map(
        per_device,
        mesh=fine,
        in_specs=(field, P(ROWS, None), P(), P(), P(), P(None, ROWS, None)),
        out_specs=(field, field),
        check_vma=False,
    )
```

time: 122 us -> 92.6 us (0.76)
  waiting for transfers between devices: 36.2 us -> 9.54 us
  blocking collectives: 32.9 us -> 29 us
  starting transfers between devices: 43.9 us -> 45.2 us
  Pallas kernels: 4.68 us -> 5.94 us
    ppermute x6, waiting for transfers between devices: 36.2 us -> 5.47 us  [the longest x2 2.99 us: partners(): return (core, near, lax.ppermute(near, 'c', other))]
    all_to_all x2, waiting for transfers between devices: 0.01 us -> 4.07 us  [swap(): return lax.all_to_all(values, axis, split_axis=0, concat_axis=0, tiled=True)]
    all_to_all x2 -> x1, blocking collectives: 32.9 us -> 29 us  [swap(): return lax.all_to_all(values, axis, split_axis=0, concat_axis=0, tiled=True)]
    ppermute x6, starting transfers between devices: 17.8 us -> 19.7 us  [the longest x2 7.76 us: partners(): core = lax.ppermute(values, 'c', other)]
    pallas_call x3 -> x5, Pallas kernels: 4.68 us -> 5.94 us  [call(): pl.pallas_call(kernel, out_shape=tuple((jax.ShapeDtypeStruct(*shape) for...]
  transfers between devices with their start and end apart: 8 -> 8, of which waited for: 5 -> 5; matrix products, arithmetic and copies ran while one was open for 0% -> 0% of each run, Pallas kernels for 0% -> 3%
where the time goes in v4:
time: 92.6 us; the launch traced here: 92.1 us
  starting transfers between devices  45.2 us (49%)
  blocking collectives  29 us (31%)
  waiting for transfers between devices  9.54 us (10%)
  Pallas kernels  5.94 us (6%)
  local copies, waits for them, and re-layouts  1.62 us (2%)
    all_to_all x1, blocking collectives, swap(): return lax.all_to_all(values, axis, split_axis=0, concat_axis=0, tiled=True)  29 us
    all_to_all x2, starting transfers between devices, swap(): return lax.all_to_all(values, axis, split_axis=0, concat_axis=0, tiled=True)  25.5 us
    ppermute x2, starting transfers between devices, partners(): core = lax.ppermute(values, 'c', other)  7.76 us
    ppermute x2, starting transfers between devices, partners(): near = lax.ppermute(values, 'v', other)  6.23 us
    pallas_call x5, Pallas kernels, call(): pl.pallas_call(kernel, out_shape=tuple((jax.ShapeDtypeStruct(*shape) for...  5.94 us
    ppermute x2, starting transfers between devices, partners(): return (core, near, lax.ppermute(near, 'c', other))  5.68 us
    all_to_all x2, waiting for transfers between devices, swap(): return lax.all_to_all(values, axis, split_axis=0, concat_axis=0, tiled=True)  4.07 us
    ppermute x2, waiting for transfers between devices, partners(): return (core, near, lax.ppermute(near, 'c', other))  2.99 us
  transfers between devices with their start and end apart: 8, of which 5 were waited for; matrix products, arithmetic and copies ran while one was open for 0% of the time, Pallas kernels for 3%

profile of v4, /device:TPU:1, one launch (start us, length us, event | category | flops | bytes accessed | tf_op | source)
XLA Modules:
  0.0 92.1 jit_solution(2130886431175612319)
XLA Ops:
  0.6 0.0 copy-start
  0.7 0.7 copy-done
  1.4 0.8 broadcast_in_dim.3
  2.2 0.0 copy-start.1
  2.2 0.0 copy-start.2
  2.2 0.0 copy-start.5
  2.2 17.3 %all-to-all-start = ((f32[64,16,128]{2,1,0:T(8,128)}), f32[64,16,128]{2,1,0:T(8,128)S(1)}, u32[]{:S(2)}, u32[]{:S(2)}) async-start(f32[64,16,128]{2,1,0:T(8,128)} %broadcast_in_dim.3), calls=%async_computation | async-start | bytes 1048576 | tf_op jit(solution)/shard_map/all_to_all | solution.py:231
  19.5 0.0 copy-done.1
  19.5 3.1 %collective-permute-start.1 = (f32[1,32,2048]{2,1,0:T(8,128)S(1)}, f32[1,32,2048]{2,1,0:T(8,128)S(1)}, u32[]{:S(2)}, u32[]{:S(2)}) collective-permute-start(f32[1,32,2048]{2,1,0:T(8,128)S(1)} %copy-done.1), channel_id=1, source_target_pairs={{0,128},{128,0},{1,129},{129,1},{2,130},{130,2},{3,131},{131,3},{4... | collective-permute-start | bytes 786440 | tf_op jit(solution)/shard_map/ppermute | solution.py:236
  22.7 3.1 %collective-permute-start = (f32[1,32,2048]{2,1,0:T(8,128)S(1)}, f32[1,32,2048]{2,1,0:T(8,128)S(1)}, u32[]{:S(2)}, u32[]{:S(2)}) collective-permute-start(f32[1,32,2048]{2,1,0:T(8,128)S(1)} %copy-done.1), channel_id=1, source_target_pairs={{0,64},{64,0},{1,65},{65,1},{2,66},{66,2},{3,67},{67,3},{4,68},{68... | collective-permute-start | bytes 786440 | tf_op jit(solution)/shard_map/ppermute | solution.py:237
  25.8 2.5 %collective-permute-done.1.f2 = f32[1,32,2048]{2,1,0:T(8,128)S(1)} collective-permute-done((f32[1,32,2048]{2,1,0:T(8,128)S(1)}, f32[1,32,2048]{2,1,0:T(8,128)S(1)}, u32[]{:S(2)}, u32[]{:S(2)}) %collective-permute-start.1) | collective-permute-done | bytes 262176 | tf_op jit(solution)/shard_map/ppermute | solution.py:236
  28.3 3.8 %collective-permute-start.2 = (f32[1,32,2048]{2,1,0:T(8,128)S(1)}, f32[1,32,2048]{2,1,0:T(8,128)S(1)}, u32[]{:S(2)}, u32[]{:S(2)}) collective-permute-start(f32[1,32,2048]{2,1,0:T(8,128)S(1)} %collective-permute-done.1.f2), channel_id=1, source_target_pairs={{0,64},{64,0},{1,65},{65,1},{2,66},{66,2},{3,67},{67,3},{4,68},{68... | collective-permute-start | bytes 786440 | tf_op jit(solution)/shard_map/ppermute | solution.py:238
  32.1 0.0 collective-permute-done.f1
  32.1 1.1 %collective-permute-done.2.f3 = f32[1,32,2048]{2,1,0:T(8,128)S(1)} collective-permute-done((f32[1,32,2048]{2,1,0:T(8,128)S(1)}, f32[1,32,2048]{2,1,0:T(8,128)S(1)}, u32[]{:S(2)}, u32[]{:S(2)}) %collective-permute-start.2) | collective-permute-done | bytes 262176 | tf_op jit(solution)/shard_map/ppermute | solution.py:238
  33.2 0.0 copy-done.2
  33.2 0.0 copy-done.5
  33.2 0.8 lines.1
  34.0 0.0 copy-start.3
  34.0 1.9 %all-to-all-done = f32[64,16,128]{2,1,0:T(8,128)S(1)} async-done(((f32[64,16,128]{2,1,0:T(8,128)}), f32[64,16,128]{2,1,0:T(8,128)S(1)}, u32[]{:S(2)}, u32[]{:S(2)}) %all-to-all-start) | async-done | bytes 524320 | tf_op jit(solution)/shard_map/all_to_all | solution.py:231
  35.9 3.1 %collective-permute-start.4 = (f32[64,2,8,128]{3,2,1,0:T(8,128)S(1)}, f32[64,2,8,128]{3,2,1,0:T(8,128)S(1)}, u32[]{:S(2)}, u32[]{:S(2)}) collective-permute-start(f32[64,2,8,128]{3,2,1,0:T(8,128)S(1)} %bitcast.5), channel_id=1, source_target_pairs={{0,128},{128,0},{1,129},{129,1},{2,130},{130,2},{3,131},{131,3},{4... | collective-permute-start | bytes 1572872 | tf_op jit(solution)/shard_map/ppermute | solution.py:236
  39.0 0.0 copy-done.3
  39.0 1.5 %rows.1 = (f32[32,3,8,128]{3,2,1,0:T(8,128)}, bf16[512,256]{1,0:T(8,128)(2,1)S(1)}, bf16[512,256]{1,0:T(8,128)(2,1)S(1)}) custom-call(bf16[1024,512]{1,0:T(8,128)(2,1)S(1)} %get-tuple-element.20.both_ref, f32[512,128]{1,0:T(8,128)S(1)} %get-tuple-element.21.same_ref, f32[32,8,128]{2,1,0:T(8,128)S(1)} %get-tuple-element.22.decays_ref, ...), custom_call_target="tpu_custom_call" | custom-call | tf_op jit(solution)/shard_map/rows/pallas_call | solution.py:219
  40.5 8.2 %all-to-all-start.1 = ((f32[32,3,8,128]{3,2,1,0:T(8,128)}), f32[32,3,8,128]{3,2,1,0:T(8,128)S(1)}, u32[]{:S(2)}, u32[]{:S(2)}) async-start(f32[32,3,8,128]{3,2,1,0:T(8,128)} %get-tuple-element.24), calls=%async_computation.1 | async-start | bytes 786432 | tf_op jit(solution)/shard_map/all_to_all | solution.py:231
  48.7 4.6 %collective-permute-start.3 = (f32[64,2,8,128]{3,2,1,0:T(8,128)S(1)}, f32[64,2,8,128]{3,2,1,0:T(8,128)S(1)}, u32[]{:S(2)}, u32[]{:S(2)}) collective-permute-start(f32[64,2,8,128]{3,2,1,0:T(8,128)S(1)} %bitcast.7), channel_id=1, source_target_pairs={{0,64},{64,0},{1,65},{65,1},{2,66},{66,2},{3,67},{67,3},{4,68},{68... | collective-permute-start | bytes 1572872 | tf_op jit(solution)/shard_map/ppermute | solution.py:237
  53.3 0.0 collective-permute-done.4.m2
  53.4 1.9 %collective-permute-start.5 = (f32[64,2,8,128]{3,2,1,0:T(8,128)S(1)}, f32[64,2,8,128]{3,2,1,0:T(8,128)S(1)}, u32[]{:S(2)}, u32[]{:S(2)}) collective-permute-start(f32[64,2,8,128]{3,2,1,0:T(8,128)S(1)} %collective-permute-done.4.m2), channel_id=1, source_target_pairs={{0,64},{64,0},{1,65},{65,1},{2,66},{66,2},{3,67},{67,3},{4,68},{68... | collective-permute-start | bytes 1572872 | tf_op jit(solution)/shard_map/ppermute | solution.py:238
  55.3 0.0 collective-permute-done.3.m1
  55.3 1.9 %collective-permute-done.5.m3 = f32[64,2,8,128]{3,2,1,0:T(8,128)S(1)} collective-permute-done((f32[64,2,8,128]{3,2,1,0:T(8,128)S(1)}, f32[64,2,8,128]{3,2,1,0:T(8,128)S(1)}, u32[]{:S(2)}, u32[]{:S(2)}) %collective-permute-start.5) | collective-permute-done | bytes 524320 | tf_op jit(solution)/shard_map/ppermute | solution.py:238
  57.2 0.3 rest.1
  57.5 0.0 copy-start.4
  57.5 2.2 %all-to-all-done.1.x_ref = f32[32,3,8,128]{3,2,1,0:T(8,128)S(1)} async-done(((f32[32,3,8,128]{3,2,1,0:T(8,128)}), f32[32,3,8,128]{3,2,1,0:T(8,128)S(1)}, u32[]{:S(2)}, u32[]{:S(2)}) %all-to-all-start.1) | async-done | bytes 393248 | tf_op jit(solution)/shard_map/all_to_all | solution.py:231
  59.7 0.0 copy-done.4
  59.7 1.8 %middle.1 = f32[128,8,128]{2,1,0:T(8,128)S(1)} custom-call(f32[32,3,8,128]{3,2,1,0:T(8,128)S(1)} %all-to-all-done.1.x_ref, s32[16,128]{1,0:T(8,128)S(1)} %bitcast.10, bf16[512,256]{1,0:T(8,128)(2,1)S(1)} %get-tuple-element.28.h0, bf16[512,256]{1,0:T(8,128)(2,1)S(1)} %get-tuple-element.29.l0, bf16[2,512,384]{2,1,0:T(8,128)(2,1)S(1)} %get-tuple-element.30.h1, ...), custom_call_target="tpu_custom_call" | custom-call | tf_op jit(solution)/shard_map/middle/pallas_call | solution.py:219
  61.5 29.0 %all_to_all.15.x_ref = f32[128,8,128]{2,1,0:T(8,128)S(1)} all-to-all(f32[128,8,128]{2,1,0:T(8,128)S(1)} %middle.1), channel_id=1, replica_groups=mesh['u'=2,'v'=2,'c'=2,'h'=4,'l'=2,'z'=8] {'u','v','c','l','z'}, dimensions={0} | all-to-all | bytes 1048576 | tf_op jit(solution)/shard_map/all_to_all | solution.py:231
  90.5 1.6 %last.1 = (f32[1,32,2048]{2,1,0:T(8,128)}, f32[1,32,2048]{2,1,0:T(8,128)}) custom-call(f32[128,8,128]{2,1,0:T(8,128)S(1)} %all_to_all.15.x_ref, s32[16,128]{1,0:T(8,128)S(1)} %bitcast.9, bf16[512,256]{1,0:T(8,128)(2,1)S(1)} %get-tuple-element.28.h0, bf16[512,256]{1,0:T(8,128)(2,1)S(1)} %get-tuple-element.29.l0, ...), custom_call_target="tpu_custom_call" | custom-call | tf_op jit(solution)/shard_map/last/pallas_call | solution.py:219
  (1 shorter events, 0.0 us)
Async XLA Ops:
  0.6 0.8 copy-start
  2.2 17.3 %copy-start.1 = (f32[1,32,2048]{2,1,0:T(8,128)S(1)}, f32[1,32,2048]{2,1,0:T(8,128)}, u32[]{:S(2)}) copy-start(f32[1,32,2048]{2,1,0:T(8,128)} %f0.1) | copy-start | bytes 786436
  2.2 31.0 %copy-start.2 = (s32[32,2048]{1,0:T(8,128)S(1)}, s32[32,2048]{1,0:T(8,128)}, u32[]{:S(2)}) copy-start(s32[32,2048]{1,0:T(8,128)} %rate_ref.1) | copy-start | bytes 786436
  2.2 31.0 %copy-start.5 = (f32[16]{0:T(128)S(1)}, f32[16]{0:T(128)}, u32[]{:S(2)}) copy-start(f32[16]{0:T(128)} %table_ref.1) | copy-start | bytes 196
  2.2 33.6 %all-to-all-start = ((f32[64,16,128]{2,1,0:T(8,128)}), f32[64,16,128]{2,1,0:T(8,128)S(1)}, u32[]{:S(2)}, u32[]{:S(2)}) async-start(f32[64,16,128]{2,1,0:T(8,128)} %broadcast_in_dim.3), calls=%async_computation | async-start | bytes 1048576 | tf_op jit(solution)/shard_map/all_to_all | solution.py:231
  19.5 8.8 %collective-permute-start.1 = (f32[1,32,2048]{2,1,0:T(8,128)S(1)}, f32[1,32,2048]{2,1,0:T(8,128)S(1)}, u32[]{:S(2)}, u32[]{:S(2)}) collective-permute-start(f32[1,32,2048]{2,1,0:T(8,128)S(1)} %copy-done.1), channel_id=1, source_target_pairs={{0,128},{128,0},{1,129},{129,1},{2,130},{130,2},{3,131},{131,3},{4... | collective-permute-start | bytes 786440 | tf_op jit(solution)/shard_map/ppermute | solution.py:236
  22.7 9.4 %collective-permute-start = (f32[1,32,2048]{2,1,0:T(8,128)S(1)}, f32[1,32,2048]{2,1,0:T(8,128)S(1)}, u32[]{:S(2)}, u32[]{:S(2)}) collective-permute-start(f32[1,32,2048]{2,1,0:T(8,128)S(1)} %copy-done.1), channel_id=1, source_target_pairs={{0,64},{64,0},{1,65},{65,1},{2,66},{66,2},{3,67},{67,3},{4,68},{68... | collective-permute-start | bytes 786440 | tf_op jit(solution)/shard_map/ppermute | solution.py:237
  28.3 4.9 %collective-permute-start.2 = (f32[1,32,2048]{2,1,0:T(8,128)S(1)}, f32[1,32,2048]{2,1,0:T(8,128)S(1)}, u32[]{:S(2)}, u32[]{:S(2)}) collective-permute-start(f32[1,32,2048]{2,1,0:T(8,128)S(1)} %collective-permute-done.1.f2), channel_id=1, source_target_pairs={{0,64},{64,0},{1,65},{65,1},{2,66},{66,2},{3,67},{67,3},{4,68},{68... | collective-permute-start | bytes 786440 | tf_op jit(solution)/shard_map/ppermute | solution.py:238
  34.0 5.0 %copy-start.3 = (s32[2048]{0:T(1024)S(1)}, s32[2048]{0:T(1024)}, u32[]{:S(2)}) copy-start(s32[2048]{0:T(1024)} %param.9) | copy-start | bytes 24580
  35.9 17.5 %collective-permute-start.4 = (f32[64,2,8,128]{3,2,1,0:T(8,128)S(1)}, f32[64,2,8,128]{3,2,1,0:T(8,128)S(1)}, u32[]{:S(2)}, u32[]{:S(2)}) collective-permute-start(f32[64,2,8,128]{3,2,1,0:T(8,128)S(1)} %bitcast.5), channel_id=1, source_target_pairs={{0,128},{128,0},{1,129},{129,1},{2,130},{130,2},{3,131},{131,3},{4... | collective-permute-start | bytes 1572872 | tf_op jit(solution)/shard_map/ppermute | solution.py:236
  40.5 19.2 %all-to-all-start.1 = ((f32[32,3,8,128]{3,2,1,0:T(8,128)}), f32[32,3,8,128]{3,2,1,0:T(8,128)S(1)}, u32[]{:S(2)}, u32[]{:S(2)}) async-start(f32[32,3,8,128]{3,2,1,0:T(8,128)} %get-tuple-element.24), calls=%async_computation.1 | async-start | bytes 786432 | tf_op jit(solution)/shard_map/all_to_all | solution.py:231
  48.7 6.6 %collective-permute-start.3 = (f32[64,2,8,128]{3,2,1,0:T(8,128)S(1)}, f32[64,2,8,128]{3,2,1,0:T(8,128)S(1)}, u32[]{:S(2)}, u32[]{:S(2)}) collective-permute-start(f32[64,2,8,128]{3,2,1,0:T(8,128)S(1)} %bitcast.7), channel_id=1, source_target_pairs={{0,64},{64,0},{1,65},{65,1},{2,66},{66,2},{3,67},{67,3},{4,68},{68... | collective-permute-start | bytes 1572872 | tf_op jit(solution)/shard_map/ppermute | solution.py:237
  53.4 3.8 %collective-permute-start.5 = (f32[64,2,8,128]{3,2,1,0:T(8,128)S(1)}, f32[64,2,8,128]{3,2,1,0:T(8,128)S(1)}, u32[]{:S(2)}, u32[]{:S(2)}) collective-permute-start(f32[64,2,8,128]{3,2,1,0:T(8,128)S(1)} %collective-permute-done.4.m2), channel_id=1, source_target_pairs={{0,64},{64,0},{1,65},{65,1},{2,66},{66,2},{3,67},{67,3},{4,68},{68... | collective-permute-start | bytes 1572872 | tf_op jit(solution)/shard_map/ppermute | solution.py:238
  57.5 2.2 %copy-start.4 = (s32[2048]{0:T(1024)S(1)}, s32[2048]{0:T(1024)}, u32[]{:S(2)}) copy-start(s32[2048]{0:T(1024)} %param.10) | copy-start | bytes 24580

commit v5 on v4

--- a/solution.py
+++ b/solution.py
@@ -14,7 +14,7 @@
 ROWS = ("h", "l", "z")
 TIME = ("u", "v", "c")
 NEAR = ("u", "l", "z")
-SPREAD = ("u", "v", "c", "l", "z")
+SPREAD = ("l", "z", "u", "v", "c")
 
 
 def split(values):
@@ -105,8 +105,12 @@
 
 
 def rows_kernel(
-    both_ref, same_ref, decays_ref, m_ref, class_ref, out_ref, high_ref, low_ref
+    both_ref, same_ref, decays_ref, m_ref, class_ref,
+    out_ref, high_ref, low_ref, first_ref, second_ref,
 ):
+    half = m_ref.shape[0] // 2
+    first_ref[...] = m_ref[:half]
+    second_ref[...] = m_ref[half:]
     for k in range(2):
         high, low = split(m_ref[:, k].reshape(BLOCK, LANES))
         high_ref[:, k * LANES : (k + 1) * LANES] = high
@@ -123,12 +127,16 @@
         out_ref[at, 2] = decays_ref[at]
 
 
-def rest_kernel(m1, m2, m3, high_ref, low_ref):
-    for n, ref in enumerate((m1, m2, m3)):
+def rest_kernel(m1, near1, near2, both1, both2, high_ref, low_ref):
+    for n, refs in enumerate(((m1,), (near1, near2), (both1, both2))):
+        lanes = slice(n * LANES, (n + 1) * LANES)
+        count = BLOCK // len(refs)
         for k in range(2):
-            high, low = split(ref[:, k].reshape(BLOCK, LANES))
-            high_ref[k, :, n * LANES : (n + 1) * LANES] = high
-            low_ref[k, :, n * LANES : (n + 1) * LANES] = low
+            for part, ref in enumerate(refs):
+                rows = slice(part * count, (part + 1) * count)
+                high, low = split(ref[:, k].reshape(count, LANES))
+                high_ref[k, rows, lanes] = high
+                low_ref[k, rows, lanes] = low
 
 
 def middle_kernel(x_ref, class_ref, h0, l0, h1, l1, out_ref, a_ref, r_ref):
@@ -186,17 +194,17 @@
             for i in range(4):
                 block = made[i].reshape(4, 8, LANES)
                 for x in range(4):
-                    out_ref[(x * 2 + core) * 16 + q * 4 + i] = block[x]
+                    out_ref[(q * 4 + i) * 8 + x * 2 + core] = block[x]
 
 
 def last_kernel(x_ref, class_ref, h0, l0, h1, l1, field_ref, adjoint_ref):
     c, v = lax.axis_index("c"), lax.axis_index("v")
+    tiles = x_ref[...].reshape(16, 8, 8, LANES)
     lines = []
     for u in range(2):
         pieces = []
         for k in range(4):
-            first = (u * 4 + k) * 16
-            turned = x_ref[first : first + 16].reshape(LANES, LANES).T
+            turned = tiles[:, u * 4 + k].reshape(LANES, LANES).T
             for b in range(2):
                 at = (u * 2 + b) * BLOCK + k * LANES
                 field_ref[0, :, at : at + LANES] = turned[b * PIECE : (b + 1) * PIECE]
@@ -231,11 +239,21 @@
     return lax.all_to_all(values, axis, split_axis=0, concat_axis=0, tiled=True)
 
 
+OTHER = [(0, 1), (1, 0)]
+
+
 def partners(values):
-    other = [(0, 1), (1, 0)]
-    near = lax.ppermute(values, "v", other)
-    core = lax.ppermute(values, "c", other)
-    return core, near, lax.ppermute(near, "c", other)
+    near = lax.ppermute(values, "v", OTHER)
+    core = lax.ppermute(values, "c", OTHER)
+    return core, near, lax.ppermute(near, "c", OTHER)
+
+
+def from_sides(first, second):
+    count = lax.axis_size("u") * 2
+    up = [(k, (k + 1) % count) for k in range(count)]
+    near = lax.ppermute(first, ("u", "v"), up)
+    far = lax.ppermute(second, ("u", "v"), [(b, a) for a, b in up])
+    return near, far
 
 
 def per_device(forcing, rate_class, rate_table, row_class, col_class, offsets):
@@ -253,14 +271,19 @@
     lines = call(lines_kernel, "lines", shapes, operands, smem=(5,))
     own, *lines = lax.optimization_barrier((own,) + lines)
     own = own.reshape(-1, 2, rows, LANES)
-    rest = partners(own)
+    half = (own.shape[0] // 2,) + own.shape[1:]
 
     shapes = (((32, 3, 8, LANES), F32),) + (((BLOCK, 256), BF16),) * 2
+    shapes += ((half, F32),) * 2
     operands = (*lines, own, row_lines)
-    out, *own = call(rows_kernel, "rows", shapes, operands)
+    out, high, low, first, second = call(rows_kernel, "rows", shapes, operands)
+    core = lax.ppermute(own, "c", OTHER)
+    near = from_sides(first, second)
+    both = [lax.ppermute(part, "c", OTHER) for part in near]
+    own = (high, low)
     out = swap(out, NEAR)
     shapes = (((2, BLOCK, 384), BF16),) * 2
-    rest = call(rest_kernel, "rest", shapes, rest)
+    rest = call(rest_kernel, "rest", shapes, (core, *near, *both))
     out, *rest = lax.optimization_barrier((out,) + rest)
     matrices = (*own, *rest)
     (out,) = call(

time: 92.6 us -> 102 us (1.10)
  starting transfers between devices: 45.2 us -> 51.1 us
  waiting for transfers between devices: 9.54 us -> 13.9 us
  blocking collectives: 29 us -> 27.9 us
    ppermute x6 -> x8, waiting for transfers between devices: 5.47 us -> 12 us  [the longest x1 6.88 us: from_sides(): near = lax.ppermute(first, ('u', 'v'), up)]
    ppermute x6 -> x8, starting transfers between devices: 19.7 us -> 25 us  [the longest x1 4.36 us: from_sides(): far = lax.ppermute(second, ('u', 'v'), [(b, a) for a, b in up])]
    all_to_all x2, waiting for transfers between devices: 4.07 us -> 1.88 us  [swap(): return lax.all_to_all(values, axis, split_axis=0, concat_axis=0, tiled=True)]
    all_to_all x1, blocking collectives: 29 us -> 27.9 us  [swap(): return lax.all_to_all(values, axis, split_axis=0, concat_axis=0, tiled=True)]
  transfers between devices with their start and end apart: 8 -> 10, of which waited for: 5 -> 5; matrix products, arithmetic and copies ran while one was open for 0% -> 0% of each run, Pallas kernels for 3% -> 1%
where the time goes in v5:
time: 102 us
  starting transfers between devices  51.1 us (50%)
  blocking collectives  27.9 us (27%)
  waiting for transfers between devices  13.9 us (14%)
  Pallas kernels  5.92 us (6%)
  local copies, waits for them, and re-layouts  2.28 us (2%)
    all_to_all x1, blocking collectives, swap(): return lax.all_to_all(values, axis, split_axis=0, concat_axis=0, tiled=True)  27.9 us
    all_to_all x2, starting transfers between devices, swap(): return lax.all_to_all(values, axis, split_axis=0, concat_axis=0, tiled=True)  26 us
    ppermute x1, waiting for transfers between devices, from_sides(): near = lax.ppermute(first, ('u', 'v'), up)  6.88 us
    pallas_call x5, Pallas kernels, call(): pl.pallas_call(kernel, out_shape=tuple((jax.ShapeDtypeStruct(*shape) for...  5.92 us
    ppermute x1, starting transfers between devices, from_sides(): far = lax.ppermute(second, ('u', 'v'), [(b, a) for a, b in up])  4.36 us
    ppermute x2, starting transfers between devices, per_device(): both = [lax.ppermute(part, 'c', OTHER) for part in near]  4.32 us
    ppermute x1, starting transfers between devices, per_device(): core = lax.ppermute(own, 'c', OTHER)  4.11 us
    ppermute x1, starting transfers between devices, partners(): return (core, near, lax.ppermute(near, 'c', OTHER))  3.76 us
  transfers between devices with their start and end apart: 10, of which 5 were waited for; matrix products, arithmetic and copies ran while one was open for 0% of the time, Pallas kernels for 1%

profile of v5, /device:TPU:1, one launch (start us, length us, event | category | flops | bytes accessed | tf_op | source)
XLA Modules:
  0.0 101.8 jit_solution(12471443224852679669)
XLA Ops:
  0.6 0.0 copy-start
  0.7 0.7 copy-done
  1.4 0.8 broadcast_in_dim.3
  2.2 0.0 copy-start.1
  2.2 0.0 copy-start.2
  2.2 0.0 copy-start.5
  2.2 17.3 %all-to-all-start = ((f32[64,16,128]{2,1,0:T(8,128)}), f32[64,16,128]{2,1,0:T(8,128)S(1)}, u32[]{:S(2)}, u32[]{:S(2)}) async-start(f32[64,16,128]{2,1,0:T(8,128)} %broadcast_in_dim.3), calls=%async_computation | async-start | bytes 1048576 | tf_op jit(solution)/shard_map/all_to_all | solution.py:239
  19.5 0.0 copy-done.1
  19.5 3.1 %collective-permute-start.1 = (f32[1,32,2048]{2,1,0:T(8,128)S(1)}, f32[1,32,2048]{2,1,0:T(8,128)S(1)}, u32[]{:S(2)}, u32[]{:S(2)}) collective-permute-start(f32[1,32,2048]{2,1,0:T(8,128)S(1)} %copy-done.1), channel_id=1, source_target_pairs={{0,128},{128,0},{1,129},{129,1},{2,130},{130,2},{3,131},{131,3},{4... | collective-permute-start | bytes 786440 | tf_op jit(solution)/shard_map/ppermute | solution.py:246
  22.6 3.1 %collective-permute-start = (f32[1,32,2048]{2,1,0:T(8,128)S(1)}, f32[1,32,2048]{2,1,0:T(8,128)S(1)}, u32[]{:S(2)}, u32[]{:S(2)}) collective-permute-start(f32[1,32,2048]{2,1,0:T(8,128)S(1)} %copy-done.1), channel_id=1, source_target_pairs={{0,64},{64,0},{1,65},{65,1},{2,66},{66,2},{3,67},{67,3},{4,68},{68... | collective-permute-start | bytes 786440 | tf_op jit(solution)/shard_map/ppermute | solution.py:247
  25.8 2.5 %collective-permute-done.1.f2 = f32[1,32,2048]{2,1,0:T(8,128)S(1)} collective-permute-done((f32[1,32,2048]{2,1,0:T(8,128)S(1)}, f32[1,32,2048]{2,1,0:T(8,128)S(1)}, u32[]{:S(2)}, u32[]{:S(2)}) %collective-permute-start.1) | collective-permute-done | bytes 262176 | tf_op jit(solution)/shard_map/ppermute | solution.py:246
  28.3 3.8 %collective-permute-start.2 = (f32[1,32,2048]{2,1,0:T(8,128)S(1)}, f32[1,32,2048]{2,1,0:T(8,128)S(1)}, u32[]{:S(2)}, u32[]{:S(2)}) collective-permute-start(f32[1,32,2048]{2,1,0:T(8,128)S(1)} %collective-permute-done.1.f2), channel_id=1, source_target_pairs={{0,64},{64,0},{1,65},{65,1},{2,66},{66,2},{3,67},{67,3},{4,68},{68... | collective-permute-start | bytes 786440 | tf_op jit(solution)/shard_map/ppermute | solution.py:248
  32.0 0.0 collective-permute-done.f1
  32.0 1.1 %collective-permute-done.2.f3 = f32[1,32,2048]{2,1,0:T(8,128)S(1)} collective-permute-done((f32[1,32,2048]{2,1,0:T(8,128)S(1)}, f32[1,32,2048]{2,1,0:T(8,128)S(1)}, u32[]{:S(2)}, u32[]{:S(2)}) %collective-permute-start.2) | collective-permute-done | bytes 262176 | tf_op jit(solution)/shard_map/ppermute | solution.py:248
  33.2 0.0 copy-done.2
  33.2 0.0 copy-done.5
  33.2 0.8 lines.1
  34.0 0.0 copy-start.3
  34.0 1.9 %all-to-all-done = f32[64,16,128]{2,1,0:T(8,128)S(1)} async-done(((f32[64,16,128]{2,1,0:T(8,128)}), f32[64,16,128]{2,1,0:T(8,128)S(1)}, u32[]{:S(2)}, u32[]{:S(2)}) %all-to-all-start) | async-done | bytes 524320 | tf_op jit(solution)/shard_map/all_to_all | solution.py:239
  35.9 0.0 copy-done.3
  35.9 1.5 %rows.1 = (f32[32,3,8,128]{3,2,1,0:T(8,128)}, bf16[512,256]{1,0:T(8,128)(2,1)S(1)}, bf16[512,256]{1,0:T(8,128)(2,1)S(1)}, f32[32,2,8,128]{3,2,1,0:T(8,128)S(1)}, f32[32,2,8,128]{3,2,1,0:T(8,128)S(1)}) custom-call(bf16[1024,512]{1,0:T(8,128)(2,1)S(1)} %get-tuple-element.22.both_ref, f32[512,128]{1,0:T(8,128)S(1)} %get-tuple-element.23.same_ref, ...), custom_call_target="tpu_custom_call" | custom-call | tf_op jit(solution)/shard_map/rows/pallas_call | solution.py:227
  37.4 8.8 %all-to-all-start.1 = ((f32[32,3,8,128]{3,2,1,0:T(8,128)}), f32[32,3,8,128]{3,2,1,0:T(8,128)S(1)}, u32[]{:S(2)}, u32[]{:S(2)}) async-start(f32[32,3,8,128]{3,2,1,0:T(8,128)} %get-tuple-element.26), calls=%async_computation.1 | async-start | bytes 786432 | tf_op jit(solution)/shard_map/all_to_all | solution.py:239
  46.1 4.1 %collective-permute-start.3 = (f32[64,2,8,128]{3,2,1,0:T(8,128)S(1)}, f32[64,2,8,128]{3,2,1,0:T(8,128)S(1)}, u32[]{:S(2)}, u32[]{:S(2)}) collective-permute-start(f32[64,2,8,128]{3,2,1,0:T(8,128)S(1)} %bitcast.6), channel_id=1, source_target_pairs={{0,64},{64,0},{1,65},{65,1},{2,66},{66,2},{3,67},{67,3},{4,68},{68... | collective-permute-start | bytes 1572872 | tf_op jit(solution)/shard_map/ppermute | solution.py:280
  50.3 2.2 %collective-permute-start.4 = (f32[32,2,8,128]{3,2,1,0:T(8,128)S(1)}, f32[32,2,8,128]{3,2,1,0:T(8,128)S(1)}, u32[]{:S(2)}, u32[]{:S(2)}) collective-permute-start(f32[32,2,8,128]{3,2,1,0:T(8,128)S(1)} %get-tuple-element.27), channel_id=1, source_target_pairs={{0,128},{128,256},{256,384},{384,0},{1,129},{129,257},{257,385},{3... | collective-permute-start | bytes 786440 | tf_op jit(solution)/shard_map/ppermute | solution.py:254
  52.5 4.4 %collective-permute-start.5 = (f32[32,2,8,128]{3,2,1,0:T(8,128)S(1)}, f32[32,2,8,128]{3,2,1,0:T(8,128)S(1)}, u32[]{:S(2)}, u32[]{:S(2)}) collective-permute-start(f32[32,2,8,128]{3,2,1,0:T(8,128)S(1)} %get-tuple-element.28), channel_id=1, source_target_pairs={{128,0},{256,128},{384,256},{0,384},{129,1},{257,129},{385,257},{1... | collective-permute-start | bytes 786440 | tf_op jit(solution)/shard_map/ppermute | solution.py:255
  56.9 6.9 %collective-permute-done.4.near1 = f32[32,2,8,128]{3,2,1,0:T(8,128)S(1)} collective-permute-done((f32[32,2,8,128]{3,2,1,0:T(8,128)S(1)}, f32[32,2,8,128]{3,2,1,0:T(8,128)S(1)}, u32[]{:S(2)}, u32[]{:S(2)}) %collective-permute-start.4) | collective-permute-done | bytes 262176 | tf_op jit(solution)/shard_map/ppermute | solution.py:254
  63.7 2.4 %collective-permute-start.6 = (f32[32,2,8,128]{3,2,1,0:T(8,128)S(1)}, f32[32,2,8,128]{3,2,1,0:T(8,128)S(1)}, u32[]{:S(2)}, u32[]{:S(2)}) collective-permute-start(f32[32,2,8,128]{3,2,1,0:T(8,128)S(1)} %collective-permute-done.4.near1), channel_id=1, source_target_pairs={{0,64},{64,0},{1,65},{65,1},{2,66},{66,2},{3,67},{67,3},{4,68},{68... | collective-permute-start | bytes 786440 | tf_op jit(solution)/shard_map/ppermute | solution.py:282
  66.1 0.0 collective-permute-done.5.near2
  66.2 1.9 %collective-permute-start.7 = (f32[32,2,8,128]{3,2,1,0:T(8,128)S(1)}, f32[32,2,8,128]{3,2,1,0:T(8,128)S(1)}, u32[]{:S(2)}, u32[]{:S(2)}) collective-permute-start(f32[32,2,8,128]{3,2,1,0:T(8,128)S(1)} %collective-permute-done.5.near2), channel_id=1, source_target_pairs={{0,64},{64,0},{1,65},{65,1},{2,66},{66,2},{3,67},{67,3},{4,68},{68... | collective-permute-start | bytes 786440 | tf_op jit(solution)/shard_map/ppermute | solution.py:282
  68.1 0.0 collective-permute-done.3.m1
  68.1 0.0 collective-permute-done.6.both1
  68.1 1.5 %collective-permute-done.7.both2 = f32[32,2,8,128]{3,2,1,0:T(8,128)S(1)} collective-permute-done((f32[32,2,8,128]{3,2,1,0:T(8,128)S(1)}, f32[32,2,8,128]{3,2,1,0:T(8,128)S(1)}, u32[]{:S(2)}, u32[]{:S(2)}) %collective-permute-start.7) | collective-permute-done | bytes 262176 | tf_op jit(solution)/shard_map/ppermute | solution.py:282
  69.6 0.3 rest.1
  69.9 0.0 copy-start.4
  69.9 0.0 all-to-all-done.1.x_ref
  69.9 0.7 copy-done.4
  70.6 1.8 %middle.1 = f32[128,8,128]{2,1,0:T(8,128)S(1)} custom-call(f32[32,3,8,128]{3,2,1,0:T(8,128)S(1)} %all-to-all-done.1.x_ref, s32[16,128]{1,0:T(8,128)S(1)} %bitcast.9, bf16[512,256]{1,0:T(8,128)(2,1)S(1)} %get-tuple-element.32.h0, bf16[512,256]{1,0:T(8,128)(2,1)S(1)} %get-tuple-element.33.l0, bf16[2,512,384]{2,1,0:T(8,128)(2,1)S(1)} %get-tuple-element.34.h1, ...), custom_call_target="tpu_custom_call" | custom-call | tf_op jit(solution)/shard_map/middle/pallas_call | solution.py:227
  72.3 27.9 %all_to_all.15.x_ref = f32[128,8,128]{2,1,0:T(8,128)S(1)} all-to-all(f32[128,8,128]{2,1,0:T(8,128)S(1)} %middle.1), channel_id=1, replica_groups=mesh['u'=2,'v'=2,'c'=2,'h'=4,'l'=2,'z'=8] {'l','z','u','v','c'}, dimensions={0} | all-to-all | bytes 1048576 | tf_op jit(solution)/shard_map/all_to_all | solution.py:239
  100.2 1.6 %last.1 = (f32[1,32,2048]{2,1,0:T(8,128)}, f32[1,32,2048]{2,1,0:T(8,128)}) custom-call(f32[128,8,128]{2,1,0:T(8,128)S(1)} %all_to_all.15.x_ref, s32[16,128]{1,0:T(8,128)S(1)} %bitcast.8, bf16[512,256]{1,0:T(8,128)(2,1)S(1)} %get-tuple-element.32.h0, bf16[512,256]{1,0:T(8,128)(2,1)S(1)} %get-tuple-element.33.l0, ...), custom_call_target="tpu_custom_call" | custom-call | tf_op jit(solution)/shard_map/last/pallas_call | solution.py:227
  (1 shorter events, 0.0 us)
Async XLA Ops:
  0.6 0.8 copy-start
  2.2 17.3 %copy-start.1 = (f32[1,32,2048]{2,1,0:T(8,128)S(1)}, f32[1,32,2048]{2,1,0:T(8,128)}, u32[]{:S(2)}) copy-start(f32[1,32,2048]{2,1,0:T(8,128)} %f0.1) | copy-start | bytes 786436
  2.2 31.0 %copy-start.2 = (s32[32,2048]{1,0:T(8,128)S(1)}, s32[32,2048]{1,0:T(8,128)}, u32[]{:S(2)}) copy-start(s32[32,2048]{1,0:T(8,128)} %rate_ref.1) | copy-start | bytes 786436
  2.2 31.0 %copy-start.5 = (f32[16]{0:T(128)S(1)}, f32[16]{0:T(128)}, u32[]{:S(2)}) copy-start(f32[16]{0:T(128)} %table_ref.1) | copy-start | bytes 196
  2.2 33.6 %all-to-all-start = ((f32[64,16,128]{2,1,0:T(8,128)}), f32[64,16,128]{2,1,0:T(8,128)S(1)}, u32[]{:S(2)}, u32[]{:S(2)}) async-start(f32[64,16,128]{2,1,0:T(8,128)} %broadcast_in_dim.3), calls=%async_computation | async-start | bytes 1048576 | tf_op jit(solution)/shard_map/all_to_all | solution.py:239
  19.5 8.8 %collective-permute-start.1 = (f32[1,32,2048]{2,1,0:T(8,128)S(1)}, f32[1,32,2048]{2,1,0:T(8,128)S(1)}, u32[]{:S(2)}, u32[]{:S(2)}) collective-permute-start(f32[1,32,2048]{2,1,0:T(8,128)S(1)} %copy-done.1), channel_id=1, source_target_pairs={{0,128},{128,0},{1,129},{129,1},{2,130},{130,2},{3,131},{131,3},{4... | collective-permute-start | bytes 786440 | tf_op jit(solution)/shard_map/ppermute | solution.py:246
  22.6 9.4 %collective-permute-start = (f32[1,32,2048]{2,1,0:T(8,128)S(1)}, f32[1,32,2048]{2,1,0:T(8,128)S(1)}, u32[]{:S(2)}, u32[]{:S(2)}) collective-permute-start(f32[1,32,2048]{2,1,0:T(8,128)S(1)} %copy-done.1), channel_id=1, source_target_pairs={{0,64},{64,0},{1,65},{65,1},{2,66},{66,2},{3,67},{67,3},{4,68},{68... | collective-permute-start | bytes 786440 | tf_op jit(solution)/shard_map/ppermute | solution.py:247
  28.3 4.9 %collective-permute-start.2 = (f32[1,32,2048]{2,1,0:T(8,128)S(1)}, f32[1,32,2048]{2,1,0:T(8,128)S(1)}, u32[]{:S(2)}, u32[]{:S(2)}) collective-permute-start(f32[1,32,2048]{2,1,0:T(8,128)S(1)} %collective-permute-done.1.f2), channel_id=1, source_target_pairs={{0,64},{64,0},{1,65},{65,1},{2,66},{66,2},{3,67},{67,3},{4,68},{68... | collective-permute-start | bytes 786440 | tf_op jit(solution)/shard_map/ppermute | solution.py:248
  34.0 1.9 %copy-start.3 = (s32[2048]{0:T(1024)S(1)}, s32[2048]{0:T(1024)}, u32[]{:S(2)}) copy-start(s32[2048]{0:T(1024)} %param.9) | copy-start | bytes 24580
  37.4 32.5 %all-to-all-start.1 = ((f32[32,3,8,128]{3,2,1,0:T(8,128)}), f32[32,3,8,128]{3,2,1,0:T(8,128)S(1)}, u32[]{:S(2)}, u32[]{:S(2)}) async-start(f32[32,3,8,128]{3,2,1,0:T(8,128)} %get-tuple-element.26), calls=%async_computation.1 | async-start | bytes 786432 | tf_op jit(solution)/shard_map/all_to_all | solution.py:239
  46.1 22.0 %collective-permute-start.3 = (f32[64,2,8,128]{3,2,1,0:T(8,128)S(1)}, f32[64,2,8,128]{3,2,1,0:T(8,128)S(1)}, u32[]{:S(2)}, u32[]{:S(2)}) collective-permute-start(f32[64,2,8,128]{3,2,1,0:T(8,128)S(1)} %bitcast.6), channel_id=1, source_target_pairs={{0,64},{64,0},{1,65},{65,1},{2,66},{66,2},{3,67},{67,3},{4,68},{68... | collective-permute-start | bytes 1572872 | tf_op jit(solution)/shard_map/ppermute | solution.py:280
  50.3 13.5 %collective-permute-start.4 = (f32[32,2,8,128]{3,2,1,0:T(8,128)S(1)}, f32[32,2,8,128]{3,2,1,0:T(8,128)S(1)}, u32[]{:S(2)}, u32[]{:S(2)}) collective-permute-start(f32[32,2,8,128]{3,2,1,0:T(8,128)S(1)} %get-tuple-element.27), channel_id=1, source_target_pairs={{0,128},{128,256},{256,384},{384,0},{1,129},{129,257},{257,385},{3... | collective-permute-start | bytes 786440 | tf_op jit(solution)/shard_map/ppermute | solution.py:254
  52.5 13.7 %collective-permute-start.5 = (f32[32,2,8,128]{3,2,1,0:T(8,128)S(1)}, f32[32,2,8,128]{3,2,1,0:T(8,128)S(1)}, u32[]{:S(2)}, u32[]{:S(2)}) collective-permute-start(f32[32,2,8,128]{3,2,1,0:T(8,128)S(1)} %get-tuple-element.28), channel_id=1, source_target_pairs={{128,0},{256,128},{384,256},{0,384},{129,1},{257,129},{385,257},{1... | collective-permute-start | bytes 786440 | tf_op jit(solution)/shard_map/ppermute | solution.py:255
  63.7 4.4 %collective-permute-start.6 = (f32[32,2,8,128]{3,2,1,0:T(8,128)S(1)}, f32[32,2,8,128]{3,2,1,0:T(8,128)S(1)}, u32[]{:S(2)}, u32[]{:S(2)}) collective-permute-start(f32[32,2,8,128]{3,2,1,0:T(8,128)S(1)} %collective-permute-done.4.near1), channel_id=1, source_target_pairs={{0,64},{64,0},{1,65},{65,1},{2,66},{66,2},{3,67},{67,3},{4,68},{68... | collective-permute-start | bytes 786440 | tf_op jit(solution)/shard_map/ppermute | solution.py:282
  66.2 3.4 %collective-permute-start.7 = (f32[32,2,8,128]{3,2,1,0:T(8,128)S(1)}, f32[32,2,8,128]{3,2,1,0:T(8,128)S(1)}, u32[]{:S(2)}, u32[]{:S(2)}) collective-permute-start(f32[32,2,8,128]{3,2,1,0:T(8,128)S(1)} %collective-permute-done.5.near2), channel_id=1, source_target_pairs={{0,64},{64,0},{1,65},{65,1},{2,66},{66,2},{3,67},{67,3},{4,68},{68... | collective-permute-start | bytes 786440 | tf_op jit(solution)/shard_map/ppermute | solution.py:282
  69.9 0.7 copy-start.4

commit v6 on v4

--- a/solution.py
+++ b/solution.py
@@ -12,9 +12,16 @@
 F32 = jnp.float32
 BF16 = jnp.bfloat16
 ROWS = ("h", "l", "z")
-TIME = ("u", "v", "c")
-NEAR = ("u", "l", "z")
-SPREAD = ("u", "v", "c", "l", "z")
+TIME = ("x", "c")
+NEAR = ("x", "l", "z")
+SPREAD = ("x", "c", "l", "z")
+SIDES = ((0, 3), (1, 2))
+
+
+def place_along_x():
+    x = lax.axis_index("x")
+    u = x // 2
+    return u, jnp.where(lax.rem(x, 2) == u, 0, 1)
 
 
 def split(values):
@@ -79,7 +86,7 @@
 
 
 def lines_kernel(f0, f1, f2, f3, rate_ref, table_ref, both_ref, same_ref, decays_ref):
-    quarter = lax.axis_index("v") * 2 + lax.axis_index("c")
+    quarter = place_along_x()[1] * 2 + lax.axis_index("c")
     fields = ((f0, f1), (f2, f3))
     at = [pl.multiple_of(b * BLOCK + quarter * LANES, LANES) for b in range(4)]
     for far in range(2):
@@ -132,7 +139,8 @@
 
 
 def middle_kernel(x_ref, class_ref, h0, l0, h1, l1, out_ref, a_ref, r_ref):
-    c, v, u = lax.axis_index("c"), lax.axis_index("v"), lax.axis_index("u")
+    c = lax.axis_index("c")
+    u, v = place_along_x()
     tiles = x_ref[...].reshape(2, 4, 4, 3, 8, LANES)
     made = exchange_lanes([tiles[:, :, i, :2].reshape(128, LANES) for i in range(4)])
     for tb in range(4):
@@ -161,7 +169,7 @@
     for t in range(8):
         far, late, core = t // 4, (t // 2) % 2, t % 2
         pair = smoothed[far]
-        pair = jnp.where(v == 0, pair[late], pair[1 - late])
+        pair = jnp.where(v == far, pair[late], pair[1 - late])
         here = scaled * jnp.where(c == 0, pair[core], pair[1 - core])
         state = here if state is None else decays * state + here
         field.append(state)
@@ -189,28 +197,34 @@
                     out_ref[(x * 2 + core) * 16 + q * 4 + i] = block[x]
 
 
-def last_kernel(x_ref, class_ref, h0, l0, h1, l1, field_ref, adjoint_ref):
-    c, v = lax.axis_index("c"), lax.axis_index("v")
+def last_kernel(
+    x_ref, class_ref, h0, l0, h1, l1, field_out, adjoint_ref, field_ref, done
+):
+    c = lax.axis_index("c")
+    v = place_along_x()[1]
     lines = []
     for u in range(2):
         pieces = []
         for k in range(4):
-            first = (u * 4 + k) * 16
+            first = ((u * 2 + ((k // 2) ^ u)) * 2 + k % 2) * 16
             turned = x_ref[first : first + 16].reshape(LANES, LANES).T
             for b in range(2):
                 at = (u * 2 + b) * BLOCK + k * LANES
                 field_ref[0, :, at : at + LANES] = turned[b * PIECE : (b + 1) * PIECE]
             pieces.append(turned[2 * PIECE :])
         lines.append(jnp.concatenate(pieces, axis=1))
+    copy = pltpu.make_async_copy(field_ref, field_out, done)
+    copy.start()
     lines = jnp.concatenate(lines, axis=0)
     mask = row_mask(class_ref, 4)
     solved = lines + solve(own_first(lines, v, c), mask, (h0, l0, h1, l1), True)
     for b in range(4):
         piece = solved[b * PIECE : (b + 1) * PIECE]
         adjoint_ref[0, :, b * BLOCK : (b + 1) * BLOCK] = piece
-
-
-def call(kernel, name, shapes, operands, smem=(), scratch=()):
+    copy.wait()
+
+
+def call(kernel, name, shapes, operands, smem=(), scratch=(), loose=()):
     vmem = pl.BlockSpec(memory_space=pltpu.VMEM)
     places = [
         pl.BlockSpec(memory_space=pltpu.SMEM) if k in smem else vmem
@@ -220,20 +234,26 @@
         kernel,
         out_shape=tuple(jax.ShapeDtypeStruct(*shape) for shape in shapes),
         in_specs=places,
-        out_specs=(vmem,) * len(shapes),
-        scratch_shapes=[pltpu.VMEM(shape, F32) for shape in scratch],
+        out_specs=tuple(
+            pl.BlockSpec(memory_space=pl.ANY) if k in loose else vmem
+            for k in range(len(shapes))
+        ),
+        scratch_shapes=[pltpu.VMEM(shape, F32) for shape in scratch]
+        + [pltpu.SemaphoreType.DMA] * len(loose),
         compiler_params=pltpu.CompilerParams(vmem_limit_bytes=40 * 1024 * 1024),
         name=name,
     )(*operands)
 
 
-def swap(values, axis):
-    return lax.all_to_all(values, axis, split_axis=0, concat_axis=0, tiled=True)
+def swap(values, axis, groups=None):
+    return lax.all_to_all(
+        values, axis, split_axis=0, concat_axis=0, axis_index_groups=groups, tiled=True
+    )
 
 
 def partners(values):
+    near = lax.ppermute(values, "x", [(k, k ^ 1) for k in range(4)])
     other = [(0, 1), (1, 0)]
-    near = lax.ppermute(values, "v", other)
     core = lax.ppermute(values, "c", other)
     return core, near, lax.ppermute(near, "c", other)
 
@@ -242,7 +262,7 @@
     row_lines = row_class.reshape(-1, LANES)
     col_lines = col_class.reshape(-1, LANES)
 
-    quarter = lax.axis_index("v") * 2 + lax.axis_index("c")
+    quarter = place_along_x()[1] * 2 + lax.axis_index("c")
     rows = offsets.shape[1]
     piece = lax.dynamic_slice(offsets, (0, 0, quarter * LANES), (2, rows, LANES))
     piece = piece.reshape(2 * rows, LANES)
@@ -258,7 +278,9 @@
     shapes = (((32, 3, 8, LANES), F32),) + (((BLOCK, 256), BF16),) * 2
     operands = (*lines, own, row_lines)
     out, *own = call(rows_kernel, "rows", shapes, operands)
-    out = swap(out, NEAR)
+    count = lax.axis_size(("l", "z"))
+    groups = [[x * count + k for x in side for k in range(count)] for side in SIDES]
+    out = swap(out, NEAR, groups)
     shapes = (((2, BLOCK, 384), BF16),) * 2
     rest = call(rest_kernel, "rest", shapes, rest)
     out, *rest = lax.optimization_barrier((out,) + rest)
@@ -272,14 +294,16 @@
     )
     out = swap(out, SPREAD)
     shapes = ((forcing.shape, F32),) * 2
-    return call(last_kernel, "last", shapes, (out, row_lines) + matrices)
+    operands = (out, row_lines) + matrices
+    scratch = (forcing.shape,)
+    return call(last_kernel, "last", shapes, operands, scratch=scratch, loose=(0,))
 
 
 def solution(mesh):
     devices = mesh.devices
     tm, row = devices.shape
     fine = Mesh(
-        devices.reshape(tm // 4, 2, 2, row // 16, 2, 8), ("u", "v", "c", "h", "l", "z")
+        devices.reshape(tm // 2, 2, row // 16, 2, 8), ("x", "c", "h", "l", "z")
     )
     field = P(TIME, ROWS, None)
     return jax.shard_map(

time: 92.6 us -> 92.2 us (level)
  no operation moved by 1% of the time
where the time goes in v6:
time: 92.2 us; the launch traced here: 91.7 us
  starting transfers between devices  44.5 us (48%)
  blocking collectives  29 us (31%)
  waiting for transfers between devices  9.24 us (10%)
  Pallas kernels  6.46 us (7%)
  local copies, waits for them, and re-layouts  1.61 us (2%)
    all_to_all x1, blocking collectives, swap(): lax.all_to_all(values, axis, split_axis=0, concat_axis=0, axis_index_grou...  29 us
    all_to_all x2, starting transfers between devices, swap(): lax.all_to_all(values, axis, split_axis=0, concat_axis=0, axis_index_grou...  24.9 us
    ppermute x2, starting transfers between devices, partners(): core = lax.ppermute(values, 'c', other)  7.76 us
    pallas_call x5, Pallas kernels, call(): pl.pallas_call(kernel, out_shape=tuple((jax.ShapeDtypeStruct(*shape) for...  6.46 us
    ppermute x2, starting transfers between devices, partners(): near = lax.ppermute(values, 'x', [(k, k ^ 1) for k in range(4)])  6.23 us
    ppermute x2, starting transfers between devices, partners(): return (core, near, lax.ppermute(near, 'c', other))  5.68 us
    all_to_all x2, waiting for transfers between devices, swap(): lax.all_to_all(values, axis, split_axis=0, concat_axis=0, axis_index_grou...  3.77 us
    ppermute x2, waiting for transfers between devices, partners(): return (core, near, lax.ppermute(near, 'c', other))  2.99 us
  transfers between devices with their start and end apart: 8, of which 5 were waited for; matrix products, arithmetic and copies ran while one was open for 0% of the time, Pallas kernels for 3%

profile of v6, /device:TPU:1, one launch (start us, length us, event | category | flops | bytes accessed | tf_op | source)
XLA Modules:
  0.0 91.7 jit_solution(11578921852465626323)
XLA Ops:
  0.6 0.0 copy-start
  0.7 0.7 copy-done
  1.4 0.8 broadcast_in_dim.3
  2.2 0.0 copy-start.1
  2.2 0.0 copy-start.2
  2.2 0.0 copy-start.5
  2.2 17.3 %all-to-all-start = ((f32[64,16,128]{2,1,0:T(8,128)}), f32[64,16,128]{2,1,0:T(8,128)S(1)}, u32[]{:S(2)}, u32[]{:S(2)}) async-start(f32[64,16,128]{2,1,0:T(8,128)} %broadcast_in_dim.3), calls=%async_computation | async-start | bytes 1048576 | tf_op jit(solution)/shard_map/all_to_all | solution.py:249
  19.5 0.0 copy-done.1
  19.5 3.1 %collective-permute-start.1 = (f32[1,32,2048]{2,1,0:T(8,128)S(1)}, f32[1,32,2048]{2,1,0:T(8,128)S(1)}, u32[]{:S(2)}, u32[]{:S(2)}) collective-permute-start(f32[1,32,2048]{2,1,0:T(8,128)S(1)} %copy-done.1), channel_id=1, source_target_pairs={{0,128},{128,0},{256,384},{384,256},{1,129},{129,1},{257,385},{385... | collective-permute-start | bytes 786440 | tf_op jit(solution)/shard_map/ppermute | solution.py:255
  22.7 3.1 %collective-permute-start = (f32[1,32,2048]{2,1,0:T(8,128)S(1)}, f32[1,32,2048]{2,1,0:T(8,128)S(1)}, u32[]{:S(2)}, u32[]{:S(2)}) collective-permute-start(f32[1,32,2048]{2,1,0:T(8,128)S(1)} %copy-done.1), channel_id=1, source_target_pairs={{0,64},{64,0},{1,65},{65,1},{2,66},{66,2},{3,67},{67,3},{4,68},{68... | collective-permute-start | bytes 786440 | tf_op jit(solution)/shard_map/ppermute | solution.py:257
  25.8 2.5 %collective-permute-done.1.f2 = f32[1,32,2048]{2,1,0:T(8,128)S(1)} collective-permute-done((f32[1,32,2048]{2,1,0:T(8,128)S(1)}, f32[1,32,2048]{2,1,0:T(8,128)S(1)}, u32[]{:S(2)}, u32[]{:S(2)}) %collective-permute-start.1) | collective-permute-done | bytes 262176 | tf_op jit(solution)/shard_map/ppermute | solution.py:255
  28.3 3.8 %collective-permute-start.2 = (f32[1,32,2048]{2,1,0:T(8,128)S(1)}, f32[1,32,2048]{2,1,0:T(8,128)S(1)}, u32[]{:S(2)}, u32[]{:S(2)}) collective-permute-start(f32[1,32,2048]{2,1,0:T(8,128)S(1)} %collective-permute-done.1.f2), channel_id=1, source_target_pairs={{0,64},{64,0},{1,65},{65,1},{2,66},{66,2},{3,67},{67,3},{4,68},{68... | collective-permute-start | bytes 786440 | tf_op jit(solution)/shard_map/ppermute | solution.py:258
  32.1 0.0 collective-permute-done.f1
  32.1 1.1 %collective-permute-done.2.f3 = f32[1,32,2048]{2,1,0:T(8,128)S(1)} collective-permute-done((f32[1,32,2048]{2,1,0:T(8,128)S(1)}, f32[1,32,2048]{2,1,0:T(8,128)S(1)}, u32[]{:S(2)}, u32[]{:S(2)}) %collective-permute-start.2) | collective-permute-done | bytes 262176 | tf_op jit(solution)/shard_map/ppermute | solution.py:258
  33.2 0.0 copy-done.2
  33.2 0.0 copy-done.5
  33.2 0.8 lines.1
  34.0 0.0 copy-start.3
  34.0 1.9 %all-to-all-done = f32[64,16,128]{2,1,0:T(8,128)S(1)} async-done(((f32[64,16,128]{2,1,0:T(8,128)}), f32[64,16,128]{2,1,0:T(8,128)S(1)}, u32[]{:S(2)}, u32[]{:S(2)}) %all-to-all-start) | async-done | bytes 524320 | tf_op jit(solution)/shard_map/all_to_all | solution.py:249
  35.9 3.1 %collective-permute-start.4 = (f32[64,2,8,128]{3,2,1,0:T(8,128)S(1)}, f32[64,2,8,128]{3,2,1,0:T(8,128)S(1)}, u32[]{:S(2)}, u32[]{:S(2)}) collective-permute-start(f32[64,2,8,128]{3,2,1,0:T(8,128)S(1)} %bitcast.5), channel_id=1, source_target_pairs={{0,128},{128,0},{256,384},{384,256},{1,129},{129,1},{257,385},{385... | collective-permute-start | bytes 1572872 | tf_op jit(solution)/shard_map/ppermute | solution.py:255
  39.0 0.0 copy-done.3
  39.0 1.5 %rows.1 = (f32[32,3,8,128]{3,2,1,0:T(8,128)}, bf16[512,256]{1,0:T(8,128)(2,1)S(1)}, bf16[512,256]{1,0:T(8,128)(2,1)S(1)}) custom-call(bf16[1024,512]{1,0:T(8,128)(2,1)S(1)} %get-tuple-element.20.both_ref, f32[512,128]{1,0:T(8,128)S(1)} %get-tuple-element.21.same_ref, f32[32,8,128]{2,1,0:T(8,128)S(1)} %get-tuple-element.22.decays_ref, ...), custom_call_target="tpu_custom_call" | custom-call | tf_op jit(solution)/shard_map/rows/pallas_call | solution.py:233
  40.5 7.6 %all-to-all-start.1 = ((f32[32,3,8,128]{3,2,1,0:T(8,128)}), f32[32,3,8,128]{3,2,1,0:T(8,128)S(1)}, u32[]{:S(2)}, u32[]{:S(2)}) async-start(f32[32,3,8,128]{3,2,1,0:T(8,128)} %get-tuple-element.24), calls=%async_computation.1 | async-start | bytes 786432 | tf_op jit(solution)/shard_map/all_to_all | solution.py:249
  48.1 4.6 %collective-permute-start.3 = (f32[64,2,8,128]{3,2,1,0:T(8,128)S(1)}, f32[64,2,8,128]{3,2,1,0:T(8,128)S(1)}, u32[]{:S(2)}, u32[]{:S(2)}) collective-permute-start(f32[64,2,8,128]{3,2,1,0:T(8,128)S(1)} %bitcast.7), channel_id=1, source_target_pairs={{0,64},{64,0},{1,65},{65,1},{2,66},{66,2},{3,67},{67,3},{4,68},{68... | collective-permute-start | bytes 1572872 | tf_op jit(solution)/shard_map/ppermute | solution.py:257
  52.7 0.0 collective-permute-done.4.m2
  52.7 1.9 %collective-permute-start.5 = (f32[64,2,8,128]{3,2,1,0:T(8,128)S(1)}, f32[64,2,8,128]{3,2,1,0:T(8,128)S(1)}, u32[]{:S(2)}, u32[]{:S(2)}) collective-permute-start(f32[64,2,8,128]{3,2,1,0:T(8,128)S(1)} %collective-permute-done.4.m2), channel_id=1, source_target_pairs={{0,64},{64,0},{1,65},{65,1},{2,66},{66,2},{3,67},{67,3},{4,68},{68... | collective-permute-start | bytes 1572872 | tf_op jit(solution)/shard_map/ppermute | solution.py:258
  54.6 0.0 collective-permute-done.3.m1
  54.7 1.9 %collective-permute-done.5.m3 = f32[64,2,8,128]{3,2,1,0:T(8,128)S(1)} collective-permute-done((f32[64,2,8,128]{3,2,1,0:T(8,128)S(1)}, f32[64,2,8,128]{3,2,1,0:T(8,128)S(1)}, u32[]{:S(2)}, u32[]{:S(2)}) %collective-permute-start.5) | collective-permute-done | bytes 524320 | tf_op jit(solution)/shard_map/ppermute | solution.py:258
  56.5 0.3 rest.1
  56.9 0.0 copy-start.4
  56.9 1.9 %all-to-all-done.1.x_ref = f32[32,3,8,128]{3,2,1,0:T(8,128)S(1)} async-done(((f32[32,3,8,128]{3,2,1,0:T(8,128)}), f32[32,3,8,128]{3,2,1,0:T(8,128)S(1)}, u32[]{:S(2)}, u32[]{:S(2)}) %all-to-all-start.1) | async-done | bytes 393248 | tf_op jit(solution)/shard_map/all_to_all | solution.py:249
  58.8 0.0 copy-done.4
  58.8 1.8 %middle.1 = f32[128,8,128]{2,1,0:T(8,128)S(1)} custom-call(f32[32,3,8,128]{3,2,1,0:T(8,128)S(1)} %all-to-all-done.1.x_ref, s32[16,128]{1,0:T(8,128)S(1)} %bitcast.10, bf16[512,256]{1,0:T(8,128)(2,1)S(1)} %get-tuple-element.28.h0, bf16[512,256]{1,0:T(8,128)(2,1)S(1)} %get-tuple-element.29.l0, bf16[2,512,384]{2,1,0:T(8,128)(2,1)S(1)} %get-tuple-element.30.h1, ...), custom_call_target="tpu_custom_call" | custom-call | tf_op jit(solution)/shard_map/middle/pallas_call | solution.py:233
  60.5 29.0 %all_to_all.15.x_ref = f32[128,8,128]{2,1,0:T(8,128)S(1)} all-to-all(f32[128,8,128]{2,1,0:T(8,128)S(1)} %middle.1), channel_id=1, replica_groups=mesh['x'=4,'c'=2,'h'=4,'l'=2,'z'=8] {'x','c','l','z'}, dimensions={0} | all-to-all | bytes 1048576 | tf_op jit(solution)/shard_map/all_to_all | solution.py:249
  89.5 2.1 %last.1 = (f32[1,32,2048]{2,1,0:T(8,128)}, f32[1,32,2048]{2,1,0:T(8,128)}) custom-call(f32[128,8,128]{2,1,0:T(8,128)S(1)} %all_to_all.15.x_ref, s32[16,128]{1,0:T(8,128)S(1)} %bitcast.9, bf16[512,256]{1,0:T(8,128)(2,1)S(1)} %get-tuple-element.28.h0, bf16[512,256]{1,0:T(8,128)(2,1)S(1)} %get-tuple-element.29.l0, ...), custom_call_target="tpu_custom_call" | custom-call | tf_op jit(solution)/shard_map/last/pallas_call | solution.py:233
  (1 shorter events, 0.0 us)
Async XLA Ops:
  0.6 0.8 copy-start
  2.2 17.3 %copy-start.1 = (f32[1,32,2048]{2,1,0:T(8,128)S(1)}, f32[1,32,2048]{2,1,0:T(8,128)}, u32[]{:S(2)}) copy-start(f32[1,32,2048]{2,1,0:T(8,128)} %f0.1) | copy-start | bytes 786436
  2.2 31.0 %copy-start.2 = (s32[32,2048]{1,0:T(8,128)S(1)}, s32[32,2048]{1,0:T(8,128)}, u32[]{:S(2)}) copy-start(s32[32,2048]{1,0:T(8,128)} %rate_ref.1) | copy-start | bytes 786436
  2.2 31.0 %copy-start.5 = (f32[16]{0:T(128)S(1)}, f32[16]{0:T(128)}, u32[]{:S(2)}) copy-start(f32[16]{0:T(128)} %table_ref.1) | copy-start | bytes 196
  2.2 33.6 %all-to-all-start = ((f32[64,16,128]{2,1,0:T(8,128)}), f32[64,16,128]{2,1,0:T(8,128)S(1)}, u32[]{:S(2)}, u32[]{:S(2)}) async-start(f32[64,16,128]{2,1,0:T(8,128)} %broadcast_in_dim.3), calls=%async_computation | async-start | bytes 1048576 | tf_op jit(solution)/shard_map/all_to_all | solution.py:249
  19.5 8.8 %collective-permute-start.1 = (f32[1,32,2048]{2,1,0:T(8,128)S(1)}, f32[1,32,2048]{2,1,0:T(8,128)S(1)}, u32[]{:S(2)}, u32[]{:S(2)}) collective-permute-start(f32[1,32,2048]{2,1,0:T(8,128)S(1)} %copy-done.1), channel_id=1, source_target_pairs={{0,128},{128,0},{256,384},{384,256},{1,129},{129,1},{257,385},{385... | collective-permute-start | bytes 786440 | tf_op jit(solution)/shard_map/ppermute | solution.py:255
  22.7 9.4 %collective-permute-start = (f32[1,32,2048]{2,1,0:T(8,128)S(1)}, f32[1,32,2048]{2,1,0:T(8,128)S(1)}, u32[]{:S(2)}, u32[]{:S(2)}) collective-permute-start(f32[1,32,2048]{2,1,0:T(8,128)S(1)} %copy-done.1), channel_id=1, source_target_pairs={{0,64},{64,0},{1,65},{65,1},{2,66},{66,2},{3,67},{67,3},{4,68},{68... | collective-permute-start | bytes 786440 | tf_op jit(solution)/shard_map/ppermute | solution.py:257
  28.3 4.9 %collective-permute-start.2 = (f32[1,32,2048]{2,1,0:T(8,128)S(1)}, f32[1,32,2048]{2,1,0:T(8,128)S(1)}, u32[]{:S(2)}, u32[]{:S(2)}) collective-permute-start(f32[1,32,2048]{2,1,0:T(8,128)S(1)} %collective-permute-done.1.f2), channel_id=1, source_target_pairs={{0,64},{64,0},{1,65},{65,1},{2,66},{66,2},{3,67},{67,3},{4,68},{68... | collective-permute-start | bytes 786440 | tf_op jit(solution)/shard_map/ppermute | solution.py:258
  34.0 5.0 %copy-start.3 = (s32[2048]{0:T(1024)S(1)}, s32[2048]{0:T(1024)}, u32[]{:S(2)}) copy-start(s32[2048]{0:T(1024)} %param.9) | copy-start | bytes 24580
  35.9 16.8 %collective-permute-start.4 = (f32[64,2,8,128]{3,2,1,0:T(8,128)S(1)}, f32[64,2,8,128]{3,2,1,0:T(8,128)S(1)}, u32[]{:S(2)}, u32[]{:S(2)}) collective-permute-start(f32[64,2,8,128]{3,2,1,0:T(8,128)S(1)} %bitcast.5), channel_id=1, source_target_pairs={{0,128},{128,0},{256,384},{384,256},{1,129},{129,1},{257,385},{385... | collective-permute-start | bytes 1572872 | tf_op jit(solution)/shard_map/ppermute | solution.py:255
  40.5 18.3 %all-to-all-start.1 = ((f32[32,3,8,128]{3,2,1,0:T(8,128)}), f32[32,3,8,128]{3,2,1,0:T(8,128)S(1)}, u32[]{:S(2)}, u32[]{:S(2)}) async-start(f32[32,3,8,128]{3,2,1,0:T(8,128)} %get-tuple-element.24), calls=%async_computation.1 | async-start | bytes 786432 | tf_op jit(solution)/shard_map/all_to_all | solution.py:249
  48.1 6.6 %collective-permute-start.3 = (f32[64,2,8,128]{3,2,1,0:T(8,128)S(1)}, f32[64,2,8,128]{3,2,1,0:T(8,128)S(1)}, u32[]{:S(2)}, u32[]{:S(2)}) collective-permute-start(f32[64,2,8,128]{3,2,1,0:T(8,128)S(1)} %bitcast.7), channel_id=1, source_target_pairs={{0,64},{64,0},{1,65},{65,1},{2,66},{66,2},{3,67},{67,3},{4,68},{68... | collective-permute-start | bytes 1572872 | tf_op jit(solution)/shard_map/ppermute | solution.py:257
  52.7 3.8 %collective-permute-start.5 = (f32[64,2,8,128]{3,2,1,0:T(8,128)S(1)}, f32[64,2,8,128]{3,2,1,0:T(8,128)S(1)}, u32[]{:S(2)}, u32[]{:S(2)}) collective-permute-start(f32[64,2,8,128]{3,2,1,0:T(8,128)S(1)} %collective-permute-done.4.m2), channel_id=1, source_target_pairs={{0,64},{64,0},{1,65},{65,1},{2,66},{66,2},{3,67},{67,3},{4,68},{68... | collective-permute-start | bytes 1572872 | tf_op jit(solution)/shard_map/ppermute | solution.py:258
  56.9 1.9 %copy-start.4 = (s32[2048]{0:T(1024)S(1)}, s32[2048]{0:T(1024)}, u32[]{:S(2)}) copy-start(s32[2048]{0:T(1024)} %param.10) | copy-start | bytes 24580

commit v7 on v6

--- a/solution.py
+++ b/solution.py
@@ -197,9 +197,7 @@
                     out_ref[(x * 2 + core) * 16 + q * 4 + i] = block[x]
 
 
-def last_kernel(
-    x_ref, class_ref, h0, l0, h1, l1, field_out, adjoint_ref, field_ref, done
-):
+def last_kernel(x_ref, class_ref, h0, l0, h1, l1, field_ref, adjoint_ref):
     c = lax.axis_index("c")
     v = place_along_x()[1]
     lines = []
@@ -213,18 +211,15 @@
                 field_ref[0, :, at : at + LANES] = turned[b * PIECE : (b + 1) * PIECE]
             pieces.append(turned[2 * PIECE :])
         lines.append(jnp.concatenate(pieces, axis=1))
-    copy = pltpu.make_async_copy(field_ref, field_out, done)
-    copy.start()
     lines = jnp.concatenate(lines, axis=0)
     mask = row_mask(class_ref, 4)
     solved = lines + solve(own_first(lines, v, c), mask, (h0, l0, h1, l1), True)
     for b in range(4):
         piece = solved[b * PIECE : (b + 1) * PIECE]
         adjoint_ref[0, :, b * BLOCK : (b + 1) * BLOCK] = piece
-    copy.wait()
-
-
-def call(kernel, name, shapes, operands, smem=(), scratch=(), loose=()):
+
+
+def call(kernel, name, shapes, operands, smem=(), scratch=()):
     vmem = pl.BlockSpec(memory_space=pltpu.VMEM)
     places = [
         pl.BlockSpec(memory_space=pltpu.SMEM) if k in smem else vmem
@@ -234,12 +229,8 @@
         kernel,
         out_shape=tuple(jax.ShapeDtypeStruct(*shape) for shape in shapes),
         in_specs=places,
-        out_specs=tuple(
-            pl.BlockSpec(memory_space=pl.ANY) if k in loose else vmem
-            for k in range(len(shapes))
-        ),
-        scratch_shapes=[pltpu.VMEM(shape, F32) for shape in scratch]
-        + [pltpu.SemaphoreType.DMA] * len(loose),
+        out_specs=(vmem,) * len(shapes),
+        scratch_shapes=[pltpu.VMEM(shape, F32) for shape in scratch],
         compiler_params=pltpu.CompilerParams(vmem_limit_bytes=40 * 1024 * 1024),
         name=name,
     )(*operands)
@@ -294,9 +285,7 @@
     )
     out = swap(out, SPREAD)
     shapes = ((forcing.shape, F32),) * 2
-    operands = (out, row_lines) + matrices
-    scratch = (forcing.shape,)
-    return call(last_kernel, "last", shapes, operands, scratch=scratch, loose=(0,))
+    return call(last_kernel, "last", shapes, (out, row_lines) + matrices)
 
 
 def solution(mesh):

time: 92.2 us -> 91.7 us (level)
  no operation moved by 1% of the time
where the time goes in v7:
time: 91.7 us; the launch traced here: 91.1 us
  starting transfers between devices  44.5 us (49%)
  blocking collectives  29 us (32%)
  waiting for transfers between devices  9.24 us (10%)
  Pallas kernels  5.94 us (6%)
  local copies, waits for them, and re-layouts  1.61 us (2%)
    all_to_all x1, blocking collectives, swap(): lax.all_to_all(values, axis, split_axis=0, concat_axis=0, axis_index_grou...  29 us
    all_to_all x2, starting transfers between devices, swap(): lax.all_to_all(values, axis, split_axis=0, concat_axis=0, axis_index_grou...  24.9 us
    ppermute x2, starting transfers between devices, partners(): core = lax.ppermute(values, 'c', other)  7.76 us
    ppermute x2, starting transfers between devices, partners(): near = lax.ppermute(values, 'x', [(k, k ^ 1) for k in range(4)])  6.23 us
    pallas_call x5, Pallas kernels, call(): pl.pallas_call(kernel, out_shape=tuple((jax.ShapeDtypeStruct(*shape) for...  5.94 us
    ppermute x2, starting transfers between devices, partners(): return (core, near, lax.ppermute(near, 'c', other))  5.68 us
    all_to_all x2, waiting for transfers between devices, swap(): lax.all_to_all(values, axis, split_axis=0, concat_axis=0, axis_index_grou...  3.77 us
    ppermute x2, waiting for transfers between devices, partners(): return (core, near, lax.ppermute(near, 'c', other))  2.99 us
  transfers between devices with their start and end apart: 8, of which 5 were waited for; matrix products, arithmetic and copies ran while one was open for 0% of the time, Pallas kernels for 3%

profile of v7, /device:TPU:1, one launch (start us, length us, event | category | flops | bytes accessed | tf_op | source)
XLA Modules:
  0.0 91.1 jit_solution(4838908057056473826)
XLA Ops:
  0.6 0.0 copy-start
  0.7 0.7 copy-done
  1.4 0.8 broadcast_in_dim.3
  2.2 0.0 copy-start.1
  2.2 0.0 copy-start.2
  2.2 0.0 copy-start.5
  2.2 17.3 %all-to-all-start = ((f32[64,16,128]{2,1,0:T(8,128)}), f32[64,16,128]{2,1,0:T(8,128)S(1)}, u32[]{:S(2)}, u32[]{:S(2)}) async-start(f32[64,16,128]{2,1,0:T(8,128)} %broadcast_in_dim.3), calls=%async_computation | async-start | bytes 1048576 | tf_op jit(solution)/shard_map/all_to_all | solution.py:240
  19.5 0.0 copy-done.1
  19.5 3.1 %collective-permute-start.1 = (f32[1,32,2048]{2,1,0:T(8,128)S(1)}, f32[1,32,2048]{2,1,0:T(8,128)S(1)}, u32[]{:S(2)}, u32[]{:S(2)}) collective-permute-start(f32[1,32,2048]{2,1,0:T(8,128)S(1)} %copy-done.1), channel_id=1, source_target_pairs={{0,128},{128,0},{256,384},{384,256},{1,129},{129,1},{257,385},{385... | collective-permute-start | bytes 786440 | tf_op jit(solution)/shard_map/ppermute | solution.py:246
  22.7 3.1 %collective-permute-start = (f32[1,32,2048]{2,1,0:T(8,128)S(1)}, f32[1,32,2048]{2,1,0:T(8,128)S(1)}, u32[]{:S(2)}, u32[]{:S(2)}) collective-permute-start(f32[1,32,2048]{2,1,0:T(8,128)S(1)} %copy-done.1), channel_id=1, source_target_pairs={{0,64},{64,0},{1,65},{65,1},{2,66},{66,2},{3,67},{67,3},{4,68},{68... | collective-permute-start | bytes 786440 | tf_op jit(solution)/shard_map/ppermute | solution.py:248
  25.8 2.5 %collective-permute-done.1.f2 = f32[1,32,2048]{2,1,0:T(8,128)S(1)} collective-permute-done((f32[1,32,2048]{2,1,0:T(8,128)S(1)}, f32[1,32,2048]{2,1,0:T(8,128)S(1)}, u32[]{:S(2)}, u32[]{:S(2)}) %collective-permute-start.1) | collective-permute-done | bytes 262176 | tf_op jit(solution)/shard_map/ppermute | solution.py:246
  28.3 3.8 %collective-permute-start.2 = (f32[1,32,2048]{2,1,0:T(8,128)S(1)}, f32[1,32,2048]{2,1,0:T(8,128)S(1)}, u32[]{:S(2)}, u32[]{:S(2)}) collective-permute-start(f32[1,32,2048]{2,1,0:T(8,128)S(1)} %collective-permute-done.1.f2), channel_id=1, source_target_pairs={{0,64},{64,0},{1,65},{65,1},{2,66},{66,2},{3,67},{67,3},{4,68},{68... | collective-permute-start | bytes 786440 | tf_op jit(solution)/shard_map/ppermute | solution.py:249
  32.1 0.0 collective-permute-done.f1
  32.1 1.1 %collective-permute-done.2.f3 = f32[1,32,2048]{2,1,0:T(8,128)S(1)} collective-permute-done((f32[1,32,2048]{2,1,0:T(8,128)S(1)}, f32[1,32,2048]{2,1,0:T(8,128)S(1)}, u32[]{:S(2)}, u32[]{:S(2)}) %collective-permute-start.2) | collective-permute-done | bytes 262176 | tf_op jit(solution)/shard_map/ppermute | solution.py:249
  33.2 0.0 copy-done.2
  33.2 0.0 copy-done.5
  33.2 0.8 lines.1
  34.0 0.0 copy-start.3
  34.0 1.9 %all-to-all-done = f32[64,16,128]{2,1,0:T(8,128)S(1)} async-done(((f32[64,16,128]{2,1,0:T(8,128)}), f32[64,16,128]{2,1,0:T(8,128)S(1)}, u32[]{:S(2)}, u32[]{:S(2)}) %all-to-all-start) | async-done | bytes 524320 | tf_op jit(solution)/shard_map/all_to_all | solution.py:240
  35.9 3.1 %collective-permute-start.4 = (f32[64,2,8,128]{3,2,1,0:T(8,128)S(1)}, f32[64,2,8,128]{3,2,1,0:T(8,128)S(1)}, u32[]{:S(2)}, u32[]{:S(2)}) collective-permute-start(f32[64,2,8,128]{3,2,1,0:T(8,128)S(1)} %bitcast.5), channel_id=1, source_target_pairs={{0,128},{128,0},{256,384},{384,256},{1,129},{129,1},{257,385},{385... | collective-permute-start | bytes 1572872 | tf_op jit(solution)/shard_map/ppermute | solution.py:246
  39.0 0.0 copy-done.3
  39.0 1.5 %rows.1 = (f32[32,3,8,128]{3,2,1,0:T(8,128)}, bf16[512,256]{1,0:T(8,128)(2,1)S(1)}, bf16[512,256]{1,0:T(8,128)(2,1)S(1)}) custom-call(bf16[1024,512]{1,0:T(8,128)(2,1)S(1)} %get-tuple-element.20.both_ref, f32[512,128]{1,0:T(8,128)S(1)} %get-tuple-element.21.same_ref, f32[32,8,128]{2,1,0:T(8,128)S(1)} %get-tuple-element.22.decays_ref, ...), custom_call_target="tpu_custom_call" | custom-call | tf_op jit(solution)/shard_map/rows/pallas_call | solution.py:228
  40.5 7.6 %all-to-all-start.1 = ((f32[32,3,8,128]{3,2,1,0:T(8,128)}), f32[32,3,8,128]{3,2,1,0:T(8,128)S(1)}, u32[]{:S(2)}, u32[]{:S(2)}) async-start(f32[32,3,8,128]{3,2,1,0:T(8,128)} %get-tuple-element.24), calls=%async_computation.1 | async-start | bytes 786432 | tf_op jit(solution)/shard_map/all_to_all | solution.py:240
  48.1 4.6 %collective-permute-start.3 = (f32[64,2,8,128]{3,2,1,0:T(8,128)S(1)}, f32[64,2,8,128]{3,2,1,0:T(8,128)S(1)}, u32[]{:S(2)}, u32[]{:S(2)}) collective-permute-start(f32[64,2,8,128]{3,2,1,0:T(8,128)S(1)} %bitcast.7), channel_id=1, source_target_pairs={{0,64},{64,0},{1,65},{65,1},{2,66},{66,2},{3,67},{67,3},{4,68},{68... | collective-permute-start | bytes 1572872 | tf_op jit(solution)/shard_map/ppermute | solution.py:248
  52.7 0.0 collective-permute-done.4.m2
  52.7 1.9 %collective-permute-start.5 = (f32[64,2,8,128]{3,2,1,0:T(8,128)S(1)}, f32[64,2,8,128]{3,2,1,0:T(8,128)S(1)}, u32[]{:S(2)}, u32[]{:S(2)}) collective-permute-start(f32[64,2,8,128]{3,2,1,0:T(8,128)S(1)} %collective-permute-done.4.m2), channel_id=1, source_target_pairs={{0,64},{64,0},{1,65},{65,1},{2,66},{66,2},{3,67},{67,3},{4,68},{68... | collective-permute-start | bytes 1572872 | tf_op jit(solution)/shard_map/ppermute | solution.py:249
  54.6 0.0 collective-permute-done.3.m1
  54.7 1.9 %collective-permute-done.5.m3 = f32[64,2,8,128]{3,2,1,0:T(8,128)S(1)} collective-permute-done((f32[64,2,8,128]{3,2,1,0:T(8,128)S(1)}, f32[64,2,8,128]{3,2,1,0:T(8,128)S(1)}, u32[]{:S(2)}, u32[]{:S(2)}) %collective-permute-start.5) | collective-permute-done | bytes 524320 | tf_op jit(solution)/shard_map/ppermute | solution.py:249
  56.5 0.3 rest.1
  56.9 0.0 copy-start.4
  56.9 1.9 %all-to-all-done.1.x_ref = f32[32,3,8,128]{3,2,1,0:T(8,128)S(1)} async-done(((f32[32,3,8,128]{3,2,1,0:T(8,128)}), f32[32,3,8,128]{3,2,1,0:T(8,128)S(1)}, u32[]{:S(2)}, u32[]{:S(2)}) %all-to-all-start.1) | async-done | bytes 393248 | tf_op jit(solution)/shard_map/all_to_all | solution.py:240
  58.8 0.0 copy-done.4
  58.8 1.8 %middle.1 = f32[128,8,128]{2,1,0:T(8,128)S(1)} custom-call(f32[32,3,8,128]{3,2,1,0:T(8,128)S(1)} %all-to-all-done.1.x_ref, s32[16,128]{1,0:T(8,128)S(1)} %bitcast.10, bf16[512,256]{1,0:T(8,128)(2,1)S(1)} %get-tuple-element.28.h0, bf16[512,256]{1,0:T(8,128)(2,1)S(1)} %get-tuple-element.29.l0, bf16[2,512,384]{2,1,0:T(8,128)(2,1)S(1)} %get-tuple-element.30.h1, ...), custom_call_target="tpu_custom_call" | custom-call | tf_op jit(solution)/shard_map/middle/pallas_call | solution.py:228
  60.5 29.0 %all_to_all.15.x_ref = f32[128,8,128]{2,1,0:T(8,128)S(1)} all-to-all(f32[128,8,128]{2,1,0:T(8,128)S(1)} %middle.1), channel_id=1, replica_groups=mesh['x'=4,'c'=2,'h'=4,'l'=2,'z'=8] {'x','c','l','z'}, dimensions={0} | all-to-all | bytes 1048576 | tf_op jit(solution)/shard_map/all_to_all | solution.py:240
  89.5 1.6 %last.1 = (f32[1,32,2048]{2,1,0:T(8,128)}, f32[1,32,2048]{2,1,0:T(8,128)}) custom-call(f32[128,8,128]{2,1,0:T(8,128)S(1)} %all_to_all.15.x_ref, s32[16,128]{1,0:T(8,128)S(1)} %bitcast.9, bf16[512,256]{1,0:T(8,128)(2,1)S(1)} %get-tuple-element.28.h0, bf16[512,256]{1,0:T(8,128)(2,1)S(1)} %get-tuple-element.29.l0, ...), custom_call_target="tpu_custom_call" | custom-call | tf_op jit(solution)/shard_map/last/pallas_call | solution.py:228
  (1 shorter events, 0.0 us)
Async XLA Ops:
  0.6 0.8 copy-start
  2.2 17.3 %copy-start.1 = (f32[1,32,2048]{2,1,0:T(8,128)S(1)}, f32[1,32,2048]{2,1,0:T(8,128)}, u32[]{:S(2)}) copy-start(f32[1,32,2048]{2,1,0:T(8,128)} %f0.1) | copy-start | bytes 786436
  2.2 31.0 %copy-start.2 = (s32[32,2048]{1,0:T(8,128)S(1)}, s32[32,2048]{1,0:T(8,128)}, u32[]{:S(2)}) copy-start(s32[32,2048]{1,0:T(8,128)} %rate_ref.1) | copy-start | bytes 786436
  2.2 31.0 %copy-start.5 = (f32[16]{0:T(128)S(1)}, f32[16]{0:T(128)}, u32[]{:S(2)}) copy-start(f32[16]{0:T(128)} %table_ref.1) | copy-start | bytes 196
  2.2 33.6 %all-to-all-start = ((f32[64,16,128]{2,1,0:T(8,128)}), f32[64,16,128]{2,1,0:T(8,128)S(1)}, u32[]{:S(2)}, u32[]{:S(2)}) async-start(f32[64,16,128]{2,1,0:T(8,128)} %broadcast_in_dim.3), calls=%async_computation | async-start | bytes 1048576 | tf_op jit(solution)/shard_map/all_to_all | solution.py:240
  19.5 8.8 %collective-permute-start.1 = (f32[1,32,2048]{2,1,0:T(8,128)S(1)}, f32[1,32,2048]{2,1,0:T(8,128)S(1)}, u32[]{:S(2)}, u32[]{:S(2)}) collective-permute-start(f32[1,32,2048]{2,1,0:T(8,128)S(1)} %copy-done.1), channel_id=1, source_target_pairs={{0,128},{128,0},{256,384},{384,256},{1,129},{129,1},{257,385},{385... | collective-permute-start | bytes 786440 | tf_op jit(solution)/shard_map/ppermute | solution.py:246
  22.7 9.4 %collective-permute-start = (f32[1,32,2048]{2,1,0:T(8,128)S(1)}, f32[1,32,2048]{2,1,0:T(8,128)S(1)}, u32[]{:S(2)}, u32[]{:S(2)}) collective-permute-start(f32[1,32,2048]{2,1,0:T(8,128)S(1)} %copy-done.1), channel_id=1, source_target_pairs={{0,64},{64,0},{1,65},{65,1},{2,66},{66,2},{3,67},{67,3},{4,68},{68... | collective-permute-start | bytes 786440 | tf_op jit(solution)/shard_map/ppermute | solution.py:248
  28.3 4.9 %collective-permute-start.2 = (f32[1,32,2048]{2,1,0:T(8,128)S(1)}, f32[1,32,2048]{2,1,0:T(8,128)S(1)}, u32[]{:S(2)}, u32[]{:S(2)}) collective-permute-start(f32[1,32,2048]{2,1,0:T(8,128)S(1)} %collective-permute-done.1.f2), channel_id=1, source_target_pairs={{0,64},{64,0},{1,65},{65,1},{2,66},{66,2},{3,67},{67,3},{4,68},{68... | collective-permute-start | bytes 786440 | tf_op jit(solution)/shard_map/ppermute | solution.py:249
  34.0 5.0 %copy-start.3 = (s32[2048]{0:T(1024)S(1)}, s32[2048]{0:T(1024)}, u32[]{:S(2)}) copy-start(s32[2048]{0:T(1024)} %param.9) | copy-start | bytes 24580
  35.9 16.8 %collective-permute-start.4 = (f32[64,2,8,128]{3,2,1,0:T(8,128)S(1)}, f32[64,2,8,128]{3,2,1,0:T(8,128)S(1)}, u32[]{:S(2)}, u32[]{:S(2)}) collective-permute-start(f32[64,2,8,128]{3,2,1,0:T(8,128)S(1)} %bitcast.5), channel_id=1, source_target_pairs={{0,128},{128,0},{256,384},{384,256},{1,129},{129,1},{257,385},{385... | collective-permute-start | bytes 1572872 | tf_op jit(solution)/shard_map/ppermute | solution.py:246
  40.5 18.3 %all-to-all-start.1 = ((f32[32,3,8,128]{3,2,1,0:T(8,128)}), f32[32,3,8,128]{3,2,1,0:T(8,128)S(1)}, u32[]{:S(2)}, u32[]{:S(2)}) async-start(f32[32,3,8,128]{3,2,1,0:T(8,128)} %get-tuple-element.24), calls=%async_computation.1 | async-start | bytes 786432 | tf_op jit(solution)/shard_map/all_to_all | solution.py:240
  48.1 6.6 %collective-permute-start.3 = (f32[64,2,8,128]{3,2,1,0:T(8,128)S(1)}, f32[64,2,8,128]{3,2,1,0:T(8,128)S(1)}, u32[]{:S(2)}, u32[]{:S(2)}) collective-permute-start(f32[64,2,8,128]{3,2,1,0:T(8,128)S(1)} %bitcast.7), channel_id=1, source_target_pairs={{0,64},{64,0},{1,65},{65,1},{2,66},{66,2},{3,67},{67,3},{4,68},{68... | collective-permute-start | bytes 1572872 | tf_op jit(solution)/shard_map/ppermute | solution.py:248
  52.7 3.8 %collective-permute-start.5 = (f32[64,2,8,128]{3,2,1,0:T(8,128)S(1)}, f32[64,2,8,128]{3,2,1,0:T(8,128)S(1)}, u32[]{:S(2)}, u32[]{:S(2)}) collective-permute-start(f32[64,2,8,128]{3,2,1,0:T(8,128)S(1)} %collective-permute-done.4.m2), channel_id=1, source_target_pairs={{0,64},{64,0},{1,65},{65,1},{2,66},{66,2},{3,67},{67,3},{4,68},{68... | collective-permute-start | bytes 1572872 | tf_op jit(solution)/shard_map/ppermute | solution.py:249
  56.9 1.9 %copy-start.4 = (s32[2048]{0:T(1024)S(1)}, s32[2048]{0:T(1024)}, u32[]{:S(2)}) copy-start(s32[2048]{0:T(1024)} %param.10) | copy-start | bytes 24580

commit v8 on v7

--- a/solution.py
+++ b/solution.py
@@ -19,9 +19,10 @@
 
 
 def place_along_x():
-    x = lax.axis_index("x")
+    x, odd = lax.axis_index("x"), lax.rem(lax.axis_index("h"), 2)
     u = x // 2
-    return u, jnp.where(lax.rem(x, 2) == u, 0, 1)
+    side = jnp.where(lax.rem(x, 2) == u, 0, 1)
+    return u, jnp.where(side == odd, 0, 1), side, odd
 
 
 def split(values):
@@ -83,6 +84,17 @@
     line = class_ref[pl.ds(place // 4, 1), :]
     marks = class_marks(line, lax.rem(place, 4) * PIECE, PIECE)
     return jnp.concatenate([marks] * copies, axis=0) > 0.5
+
+
+def pieces_kernel(m_ref, out_ref):
+    c, side = lax.axis_index("c"), place_along_x()[2]
+    count = lax.axis_size(("l", "z"))
+    pieces = []
+    for v in (side, 1 - side):
+        at = pl.multiple_of((v * 2 + c) * LANES, LANES)
+        pieces.append(m_ref[:, :, pl.ds(at, LANES)].reshape(out_ref.shape[1:]))
+    for device in range(out_ref.shape[0]):
+        out_ref[device] = pieces[(device // count) % 2]
 
 
 def lines_kernel(f0, f1, f2, f3, rate_ref, table_ref, both_ref, same_ref, decays_ref):
@@ -112,8 +124,12 @@
 
 
 def rows_kernel(
-    both_ref, same_ref, decays_ref, m_ref, class_ref, out_ref, high_ref, low_ref
+    both_ref, same_ref, decays_ref, m_ref, class_ref,
+    out_ref, high_ref, low_ref, first_ref, second_ref,
 ):
+    half = m_ref.shape[0] // 2
+    first_ref[...] = m_ref[:half]
+    second_ref[...] = m_ref[half:]
     for k in range(2):
         high, low = split(m_ref[:, k].reshape(BLOCK, LANES))
         high_ref[:, k * LANES : (k + 1) * LANES] = high
@@ -130,17 +146,21 @@
         out_ref[at, 2] = decays_ref[at]
 
 
-def rest_kernel(m1, m2, m3, high_ref, low_ref):
-    for n, ref in enumerate((m1, m2, m3)):
+def rest_kernel(m1, near1, near2, both1, both2, high_ref, low_ref):
+    for n, refs in enumerate(((m1,), (near1, near2), (both1, both2))):
+        lanes = slice(n * LANES, (n + 1) * LANES)
+        count = BLOCK // len(refs)
         for k in range(2):
-            high, low = split(ref[:, k].reshape(BLOCK, LANES))
-            high_ref[k, :, n * LANES : (n + 1) * LANES] = high
-            low_ref[k, :, n * LANES : (n + 1) * LANES] = low
+            for part, ref in enumerate(refs):
+                rows = slice(part * count, (part + 1) * count)
+                high, low = split(ref[:, k].reshape(count, LANES))
+                high_ref[k, rows, lanes] = high
+                low_ref[k, rows, lanes] = low
 
 
 def middle_kernel(x_ref, class_ref, h0, l0, h1, l1, out_ref, a_ref, r_ref):
     c = lax.axis_index("c")
-    u, v = place_along_x()
+    u, v, side, _ = place_along_x()
     tiles = x_ref[...].reshape(2, 4, 4, 3, 8, LANES)
     made = exchange_lanes([tiles[:, :, i, :2].reshape(128, LANES) for i in range(4)])
     for tb in range(4):
@@ -169,7 +189,7 @@
     for t in range(8):
         far, late, core = t // 4, (t // 2) % 2, t % 2
         pair = smoothed[far]
-        pair = jnp.where(v == far, pair[late], pair[1 - late])
+        pair = jnp.where(side == far, pair[late], pair[1 - late])
         here = scaled * jnp.where(c == 0, pair[core], pair[1 - core])
         state = here if state is None else decays * state + here
         field.append(state)
@@ -199,13 +219,15 @@
 
 def last_kernel(x_ref, class_ref, h0, l0, h1, l1, field_ref, adjoint_ref):
     c = lax.axis_index("c")
-    v = place_along_x()[1]
+    _, v, _, odd = place_along_x()
     lines = []
     for u in range(2):
         pieces = []
         for k in range(4):
-            first = ((u * 2 + ((k // 2) ^ u)) * 2 + k % 2) * 16
-            turned = x_ref[first : first + 16].reshape(LANES, LANES).T
+            turn = (k // 2) ^ u
+            x = u * 2 + jnp.where(odd == 0, turn, 1 - turn)
+            first = pl.multiple_of((x * 2 + k % 2) * 16, 16)
+            turned = x_ref[pl.ds(first, 16)].reshape(LANES, LANES).T
             for b in range(2):
                 at = (u * 2 + b) * BLOCK + k * LANES
                 field_ref[0, :, at : at + LANES] = turned[b * PIECE : (b + 1) * PIECE]
@@ -242,33 +264,45 @@
     )
 
 
-def partners(values):
-    near = lax.ppermute(values, "x", [(k, k ^ 1) for k in range(4)])
-    other = [(0, 1), (1, 0)]
-    core = lax.ppermute(values, "c", other)
-    return core, near, lax.ppermute(near, "c", other)
+def from_core(values):
+    return lax.ppermute(values, "c", [(0, 1), (1, 0)])
+
+
+def from_near(values):
+    return lax.ppermute(values, "x", [(k, k ^ 1) for k in range(4)])
+
+
+def from_next(values):
+    count = lax.axis_size("h") * 2
+    pairs = [(k, (k + 1) % count) for k in range(1, count, 2)]
+    return lax.ppermute(values, ("h", "l"), pairs + [(b, a) for a, b in pairs])
 
 
 def per_device(forcing, rate_class, rate_table, row_class, col_class, offsets):
     row_lines = row_class.reshape(-1, LANES)
     col_lines = col_class.reshape(-1, LANES)
 
-    quarter = place_along_x()[1] * 2 + lax.axis_index("c")
     rows = offsets.shape[1]
-    piece = lax.dynamic_slice(offsets, (0, 0, quarter * LANES), (2, rows, LANES))
-    piece = piece.reshape(2 * rows, LANES)
-    own = swap(jnp.broadcast_to(piece, (BLOCK // rows, 2 * rows, LANES)), ROWS)
+    shape = (BLOCK // rows, 2 * rows, LANES)
+    (own,) = call(pieces_kernel, "pieces", ((shape, F32),), (offsets,))
+    own = swap(own, ROWS)
 
     shapes = (((1024, BLOCK), BF16), ((512, LANES), F32), ((32, 8, LANES), F32))
-    operands = (forcing,) + partners(forcing) + (rate_class, rate_table)
+    near = from_near(forcing)
+    fields = (forcing, from_core(forcing), near, from_core(near))
+    operands = fields + (rate_class, rate_table)
     lines = call(lines_kernel, "lines", shapes, operands, smem=(5,))
     own, *lines = lax.optimization_barrier((own,) + lines)
     own = own.reshape(-1, 2, rows, LANES)
-    rest = partners(own)
+    half = (own.shape[0] // 2,) + own.shape[1:]
 
     shapes = (((32, 3, 8, LANES), F32),) + (((BLOCK, 256), BF16),) * 2
+    shapes += ((half, F32),) * 2
     operands = (*lines, own, row_lines)
-    out, *own = call(rows_kernel, "rows", shapes, operands)
+    out, high, low, first, second = call(rows_kernel, "rows", shapes, operands)
+    near = (from_near(first), from_next(second))
+    rest = (from_core(own), *near, *map(from_core, near))
+    own = (high, low)
     count = lax.axis_size(("l", "z"))
     groups = [[x * count + k for x in side for k in range(count)] for side in SIDES]
     out = swap(out, NEAR, groups)

time: 91.7 us -> 102 us (1.11)
  starting transfers between devices: 44.5 us -> 50.8 us
  waiting for transfers between devices: 9.24 us -> 11.3 us
  blocking collectives: 29 us -> 30.1 us
    ppermute x6 -> x8, starting transfers between devices: 19.7 us -> 25.1 us  [the longest x5 16.6 us: from_core(): return lax.ppermute(values, 'c', [(0, 1), (1, 0)])]
    ppermute x6 -> x8, waiting for transfers between devices: 5.47 us -> 9.43 us  [the longest x2 6.98 us: from_near(): return lax.ppermute(values, 'x', [(k, k ^ 1) for k in range(4)])]
    all_to_all x2, waiting for transfers between devices: 3.77 us -> 1.87 us  [swap(): lax.all_to_all(values, axis, split_axis=0, concat_axis=0, axis_index_grou...]
    all_to_all x1, blocking collectives: 29 us -> 30.1 us  [swap(): lax.all_to_all(values, axis, split_axis=0, concat_axis=0, axis_index_grou...]
    pallas_call x5 -> x6, Pallas kernels: 5.94 us -> 6.77 us  [call(): pl.pallas_call(kernel, out_shape=tuple((jax.ShapeDtypeStruct(*shape) for...]
  transfers between devices with their start and end apart: 8 -> 10, of which waited for: 5 -> 6; matrix products, arithmetic and copies ran while one was open for 0% -> 0% of each run, Pallas kernels for 3% -> 1%
where the time goes in v8:
time: 102 us; the launch traced here: 101 us
  starting transfers between devices  50.8 us (50%)
  blocking collectives  30.1 us (30%)
  waiting for transfers between devices  11.3 us (11%)
  Pallas kernels  6.77 us (7%)
  local copies, waits for them, and re-layouts  1.45 us (1%)
    all_to_all x1, blocking collectives, swap(): lax.all_to_all(values, axis, split_axis=0, concat_axis=0, axis_index_grou...  30.1 us
    all_to_all x2, starting transfers between devices, swap(): lax.all_to_all(values, axis, split_axis=0, concat_axis=0, axis_index_grou...  25.8 us
    ppermute x5, starting transfers between devices, from_core(): return lax.ppermute(values, 'c', [(0, 1), (1, 0)])  16.6 us
    ppermute x2, waiting for transfers between devices, from_near(): return lax.ppermute(values, 'x', [(k, k ^ 1) for k in range(4)])  6.98 us
    pallas_call x6, Pallas kernels, call(): pl.pallas_call(kernel, out_shape=tuple((jax.ShapeDtypeStruct(*shape) for...  6.77 us
    ppermute x2, starting transfers between devices, from_near(): return lax.ppermute(values, 'x', [(k, k ^ 1) for k in range(4)])  5.04 us
    ppermute x1, starting transfers between devices, from_next(): return lax.ppermute(values, ('h', 'l'), pairs + [(b, a) for a, b in pairs])  3.38 us
    ppermute x5, waiting for transfers between devices, from_core(): return lax.ppermute(values, 'c', [(0, 1), (1, 0)])  2.26 us
  transfers between devices with their start and end apart: 10, of which 6 were waited for; matrix products, arithmetic and copies ran while one was open for 0% of the time, Pallas kernels for 1%

profile of v8, /device:TPU:1, one launch (start us, length us, event | category | flops | bytes accessed | tf_op | source)
XLA Modules:
  0.0 101.2 jit_solution(13167040548994861729)
XLA Ops:
  0.6 0.0 copy-start.3
  0.6 0.7 copy-done.3
  1.4 0.8 pieces.1
  2.2 0.0 copy-start
  2.2 0.0 copy-start.1
  2.2 0.0 copy-start.5
  2.2 17.3 %all-to-all-start = ((f32[64,16,128]{2,1,0:T(8,128)}), f32[64,16,128]{2,1,0:T(8,128)S(1)}, u32[]{:S(2)}, u32[]{:S(2)}) async-start(f32[64,16,128]{2,1,0:T(8,128)} %pieces.1), calls=%async_computation | async-start | bytes 1048576 | tf_op jit(solution)/shard_map/all_to_all | solution.py:262
  19.5 0.0 copy-done
  19.5 3.1 %collective-permute-start.1 = (f32[1,32,2048]{2,1,0:T(8,128)S(1)}, f32[1,32,2048]{2,1,0:T(8,128)S(1)}, u32[]{:S(2)}, u32[]{:S(2)}) collective-permute-start(f32[1,32,2048]{2,1,0:T(8,128)S(1)} %copy-done), channel_id=1, source_target_pairs={{0,128},{128,0},{256,384},{384,256},{1,129},{129,1},{257,385},{385... | collective-permute-start | bytes 786440 | tf_op jit(solution)/shard_map/ppermute | solution.py:272
  22.6 3.1 %collective-permute-start = (f32[1,32,2048]{2,1,0:T(8,128)S(1)}, f32[1,32,2048]{2,1,0:T(8,128)S(1)}, u32[]{:S(2)}, u32[]{:S(2)}) collective-permute-start(f32[1,32,2048]{2,1,0:T(8,128)S(1)} %copy-done), channel_id=1, source_target_pairs={{0,64},{64,0},{1,65},{65,1},{2,66},{66,2},{3,67},{67,3},{4,68},{68... | collective-permute-start | bytes 786440 | tf_op jit(solution)/shard_map/ppermute | solution.py:268
  25.8 2.5 %collective-permute-done.1.f2 = f32[1,32,2048]{2,1,0:T(8,128)S(1)} collective-permute-done((f32[1,32,2048]{2,1,0:T(8,128)S(1)}, f32[1,32,2048]{2,1,0:T(8,128)S(1)}, u32[]{:S(2)}, u32[]{:S(2)}) %collective-permute-start.1) | collective-permute-done | bytes 262176 | tf_op jit(solution)/shard_map/ppermute | solution.py:272
  28.3 3.8 %collective-permute-start.2 = (f32[1,32,2048]{2,1,0:T(8,128)S(1)}, f32[1,32,2048]{2,1,0:T(8,128)S(1)}, u32[]{:S(2)}, u32[]{:S(2)}) collective-permute-start(f32[1,32,2048]{2,1,0:T(8,128)S(1)} %collective-permute-done.1.f2), channel_id=1, source_target_pairs={{0,64},{64,0},{1,65},{65,1},{2,66},{66,2},{3,67},{67,3},{4,68},{68... | collective-permute-start | bytes 786440 | tf_op jit(solution)/shard_map/ppermute | solution.py:268
  32.0 0.0 collective-permute-done.f1
  32.0 1.1 %collective-permute-done.2.f3 = f32[1,32,2048]{2,1,0:T(8,128)S(1)} collective-permute-done((f32[1,32,2048]{2,1,0:T(8,128)S(1)}, f32[1,32,2048]{2,1,0:T(8,128)S(1)}, u32[]{:S(2)}, u32[]{:S(2)}) %collective-permute-start.2) | collective-permute-done | bytes 262176 | tf_op jit(solution)/shard_map/ppermute | solution.py:268
  33.2 0.0 copy-done.1
  33.2 0.0 copy-done.5
  33.2 0.8 lines.1
  34.0 0.0 copy-start.2
  34.0 1.9 %all-to-all-done = f32[64,16,128]{2,1,0:T(8,128)S(1)} async-done(((f32[64,16,128]{2,1,0:T(8,128)}), f32[64,16,128]{2,1,0:T(8,128)S(1)}, u32[]{:S(2)}, u32[]{:S(2)}) %all-to-all-start) | async-done | bytes 524320 | tf_op jit(solution)/shard_map/all_to_all | solution.py:262
  35.8 0.0 copy-done.2
  35.8 1.5 %rows.1 = (f32[32,3,8,128]{3,2,1,0:T(8,128)}, bf16[512,256]{1,0:T(8,128)(2,1)S(1)}, bf16[512,256]{1,0:T(8,128)(2,1)S(1)}, f32[32,2,8,128]{3,2,1,0:T(8,128)S(1)}, f32[32,2,8,128]{3,2,1,0:T(8,128)S(1)}) custom-call(bf16[1024,512]{1,0:T(8,128)(2,1)S(1)} %get-tuple-element.22.both_ref, f32[512,128]{1,0:T(8,128)S(1)} %get-tuple-element.23.same_ref, ...), custom_call_target="tpu_custom_call" | custom-call | tf_op jit(solution)/shard_map/rows/pallas_call | solution.py:250
  37.4 8.5 %all-to-all-start.1 = ((f32[32,3,8,128]{3,2,1,0:T(8,128)}), f32[32,3,8,128]{3,2,1,0:T(8,128)S(1)}, u32[]{:S(2)}, u32[]{:S(2)}) async-start(f32[32,3,8,128]{3,2,1,0:T(8,128)} %get-tuple-element.26), calls=%async_computation.1 | async-start | bytes 786432 | tf_op jit(solution)/shard_map/all_to_all | solution.py:262
  45.9 4.1 %collective-permute-start.3 = (f32[64,2,8,128]{3,2,1,0:T(8,128)S(1)}, f32[64,2,8,128]{3,2,1,0:T(8,128)S(1)}, u32[]{:S(2)}, u32[]{:S(2)}) collective-permute-start(f32[64,2,8,128]{3,2,1,0:T(8,128)S(1)} %bitcast.4), channel_id=1, source_target_pairs={{0,64},{64,0},{1,65},{65,1},{2,66},{66,2},{3,67},{67,3},{4,68},{68... | collective-permute-start | bytes 1572872 | tf_op jit(solution)/shard_map/ppermute | solution.py:268
  50.0 1.9 %collective-permute-start.4 = (f32[32,2,8,128]{3,2,1,0:T(8,128)S(1)}, f32[32,2,8,128]{3,2,1,0:T(8,128)S(1)}, u32[]{:S(2)}, u32[]{:S(2)}) collective-permute-start(f32[32,2,8,128]{3,2,1,0:T(8,128)S(1)} %get-tuple-element.27), channel_id=1, source_target_pairs={{0,128},{128,0},{256,384},{384,256},{1,129},{129,1},{257,385},{385... | collective-permute-start | bytes 786440 | tf_op jit(solution)/shard_map/ppermute | solution.py:272
  51.9 3.4 %collective-permute-start.5 = (f32[32,2,8,128]{3,2,1,0:T(8,128)S(1)}, f32[32,2,8,128]{3,2,1,0:T(8,128)S(1)}, u32[]{:S(2)}, u32[]{:S(2)}) collective-permute-start(f32[32,2,8,128]{3,2,1,0:T(8,128)S(1)} %get-tuple-element.28), channel_id=1, source_target_pairs={{8,16},{24,32},{40,48},{56,0},{16,8},{32,24},{48,40},{0,56},{9,17}... | collective-permute-start | bytes 786440 | tf_op jit(solution)/shard_map/ppermute | solution.py:278
  55.3 4.5 %collective-permute-done.4.near1 = f32[32,2,8,128]{3,2,1,0:T(8,128)S(1)} collective-permute-done((f32[32,2,8,128]{3,2,1,0:T(8,128)S(1)}, f32[32,2,8,128]{3,2,1,0:T(8,128)S(1)}, u32[]{:S(2)}, u32[]{:S(2)}) %collective-permute-start.4) | collective-permute-done | bytes 262176 | tf_op jit(solution)/shard_map/ppermute | solution.py:272
  59.8 2.7 %collective-permute-start.6 = (f32[32,2,8,128]{3,2,1,0:T(8,128)S(1)}, f32[32,2,8,128]{3,2,1,0:T(8,128)S(1)}, u32[]{:S(2)}, u32[]{:S(2)}) collective-permute-start(f32[32,2,8,128]{3,2,1,0:T(8,128)S(1)} %collective-permute-done.4.near1), channel_id=1, source_target_pairs={{0,64},{64,0},{1,65},{65,1},{2,66},{66,2},{3,67},{67,3},{4,68},{68... | collective-permute-start | bytes 786440 | tf_op jit(solution)/shard_map/ppermute | solution.py:268
  62.5 0.2 collective-permute-done.5.near2
  62.7 2.9 %collective-permute-start.7 = (f32[32,2,8,128]{3,2,1,0:T(8,128)S(1)}, f32[32,2,8,128]{3,2,1,0:T(8,128)S(1)}, u32[]{:S(2)}, u32[]{:S(2)}) collective-permute-start(f32[32,2,8,128]{3,2,1,0:T(8,128)S(1)} %collective-permute-done.5.near2), channel_id=1, source_target_pairs={{0,64},{64,0},{1,65},{65,1},{2,66},{66,2},{3,67},{67,3},{4,68},{68... | collective-permute-start | bytes 786440 | tf_op jit(solution)/shard_map/ppermute | solution.py:268
  65.6 0.0 collective-permute-done.3.m1
  65.6 0.0 collective-permute-done.6.both1
  65.7 1.1 %collective-permute-done.7.both2 = f32[32,2,8,128]{3,2,1,0:T(8,128)S(1)} collective-permute-done((f32[32,2,8,128]{3,2,1,0:T(8,128)S(1)}, f32[32,2,8,128]{3,2,1,0:T(8,128)S(1)}, u32[]{:S(2)}, u32[]{:S(2)}) %collective-permute-start.7) | collective-permute-done | bytes 262176 | tf_op jit(solution)/shard_map/ppermute | solution.py:268
  66.8 0.3 rest.1
  67.1 0.0 copy-start.4
  67.1 0.0 all-to-all-done.1.x_ref
  67.1 0.7 copy-done.4
  67.8 1.8 %middle.1 = f32[128,8,128]{2,1,0:T(8,128)S(1)} custom-call(f32[32,3,8,128]{3,2,1,0:T(8,128)S(1)} %all-to-all-done.1.x_ref, s32[16,128]{1,0:T(8,128)S(1)} %bitcast.7, bf16[512,256]{1,0:T(8,128)(2,1)S(1)} %get-tuple-element.32.h0, bf16[512,256]{1,0:T(8,128)(2,1)S(1)} %get-tuple-element.33.l0, bf16[2,512,384]{2,1,0:T(8,128)(2,1)S(1)} %get-tuple-element.34.h1, ...), custom_call_target="tpu_custom_call" | custom-call | tf_op jit(solution)/shard_map/middle/pallas_call | solution.py:250
  69.5 30.1 %all_to_all.15.x_ref = f32[128,8,128]{2,1,0:T(8,128)S(1)} all-to-all(f32[128,8,128]{2,1,0:T(8,128)S(1)} %middle.1), channel_id=1, replica_groups=mesh['x'=4,'c'=2,'h'=4,'l'=2,'z'=8] {'x','c','l','z'}, dimensions={0} | all-to-all | bytes 1048576 | tf_op jit(solution)/shard_map/all_to_all | solution.py:262
  99.6 1.6 %last.1 = (f32[1,32,2048]{2,1,0:T(8,128)}, f32[1,32,2048]{2,1,0:T(8,128)}) custom-call(f32[128,8,128]{2,1,0:T(8,128)S(1)} %all_to_all.15.x_ref, s32[16,128]{1,0:T(8,128)S(1)} %bitcast.6, bf16[512,256]{1,0:T(8,128)(2,1)S(1)} %get-tuple-element.32.h0, bf16[512,256]{1,0:T(8,128)(2,1)S(1)} %get-tuple-element.33.l0, ...), custom_call_target="tpu_custom_call" | custom-call | tf_op jit(solution)/shard_map/last/pallas_call | solution.py:250
Async XLA Ops:
  0.6 0.8 copy-start.3
  2.2 17.3 %copy-start = (f32[1,32,2048]{2,1,0:T(8,128)S(1)}, f32[1,32,2048]{2,1,0:T(8,128)}, u32[]{:S(2)}) copy-start(f32[1,32,2048]{2,1,0:T(8,128)} %f0.1) | copy-start | bytes 786436
  2.2 31.0 %copy-start.1 = (s32[32,2048]{1,0:T(8,128)S(1)}, s32[32,2048]{1,0:T(8,128)}, u32[]{:S(2)}) copy-start(s32[32,2048]{1,0:T(8,128)} %rate_ref.1) | copy-start | bytes 786436
  2.2 31.0 %copy-start.5 = (f32[16]{0:T(128)S(1)}, f32[16]{0:T(128)}, u32[]{:S(2)}) copy-start(f32[16]{0:T(128)} %table_ref.1) | copy-start | bytes 196
  2.2 33.6 %all-to-all-start = ((f32[64,16,128]{2,1,0:T(8,128)}), f32[64,16,128]{2,1,0:T(8,128)S(1)}, u32[]{:S(2)}, u32[]{:S(2)}) async-start(f32[64,16,128]{2,1,0:T(8,128)} %pieces.1), calls=%async_computation | async-start | bytes 1048576 | tf_op jit(solution)/shard_map/all_to_all | solution.py:262
  19.5 8.8 %collective-permute-start.1 = (f32[1,32,2048]{2,1,0:T(8,128)S(1)}, f32[1,32,2048]{2,1,0:T(8,128)S(1)}, u32[]{:S(2)}, u32[]{:S(2)}) collective-permute-start(f32[1,32,2048]{2,1,0:T(8,128)S(1)} %copy-done), channel_id=1, source_target_pairs={{0,128},{128,0},{256,384},{384,256},{1,129},{129,1},{257,385},{385... | collective-permute-start | bytes 786440 | tf_op jit(solution)/shard_map/ppermute | solution.py:272
  22.6 9.4 %collective-permute-start = (f32[1,32,2048]{2,1,0:T(8,128)S(1)}, f32[1,32,2048]{2,1,0:T(8,128)S(1)}, u32[]{:S(2)}, u32[]{:S(2)}) collective-permute-start(f32[1,32,2048]{2,1,0:T(8,128)S(1)} %copy-done), channel_id=1, source_target_pairs={{0,64},{64,0},{1,65},{65,1},{2,66},{66,2},{3,67},{67,3},{4,68},{68... | collective-permute-start | bytes 786440 | tf_op jit(solution)/shard_map/ppermute | solution.py:268
  28.3 4.9 %collective-permute-start.2 = (f32[1,32,2048]{2,1,0:T(8,128)S(1)}, f32[1,32,2048]{2,1,0:T(8,128)S(1)}, u32[]{:S(2)}, u32[]{:S(2)}) collective-permute-start(f32[1,32,2048]{2,1,0:T(8,128)S(1)} %collective-permute-done.1.f2), channel_id=1, source_target_pairs={{0,64},{64,0},{1,65},{65,1},{2,66},{66,2},{3,67},{67,3},{4,68},{68... | collective-permute-start | bytes 786440 | tf_op jit(solution)/shard_map/ppermute | solution.py:268
  34.0 1.9 %copy-start.2 = (s32[2048]{0:T(1024)S(1)}, s32[2048]{0:T(1024)}, u32[]{:S(2)}) copy-start(s32[2048]{0:T(1024)} %param.9) | copy-start | bytes 24580
  37.4 29.7 %all-to-all-start.1 = ((f32[32,3,8,128]{3,2,1,0:T(8,128)}), f32[32,3,8,128]{3,2,1,0:T(8,128)S(1)}, u32[]{:S(2)}, u32[]{:S(2)}) async-start(f32[32,3,8,128]{3,2,1,0:T(8,128)} %get-tuple-element.26), calls=%async_computation.1 | async-start | bytes 786432 | tf_op jit(solution)/shard_map/all_to_all | solution.py:262
  45.9 19.8 %collective-permute-start.3 = (f32[64,2,8,128]{3,2,1,0:T(8,128)S(1)}, f32[64,2,8,128]{3,2,1,0:T(8,128)S(1)}, u32[]{:S(2)}, u32[]{:S(2)}) collective-permute-start(f32[64,2,8,128]{3,2,1,0:T(8,128)S(1)} %bitcast.4), channel_id=1, source_target_pairs={{0,64},{64,0},{1,65},{65,1},{2,66},{66,2},{3,67},{67,3},{4,68},{68... | collective-permute-start | bytes 1572872 | tf_op jit(solution)/shard_map/ppermute | solution.py:268
  50.0 9.8 %collective-permute-start.4 = (f32[32,2,8,128]{3,2,1,0:T(8,128)S(1)}, f32[32,2,8,128]{3,2,1,0:T(8,128)S(1)}, u32[]{:S(2)}, u32[]{:S(2)}) collective-permute-start(f32[32,2,8,128]{3,2,1,0:T(8,128)S(1)} %get-tuple-element.27), channel_id=1, source_target_pairs={{0,128},{128,0},{256,384},{384,256},{1,129},{129,1},{257,385},{385... | collective-permute-start | bytes 786440 | tf_op jit(solution)/shard_map/ppermute | solution.py:272
  51.9 10.8 %collective-permute-start.5 = (f32[32,2,8,128]{3,2,1,0:T(8,128)S(1)}, f32[32,2,8,128]{3,2,1,0:T(8,128)S(1)}, u32[]{:S(2)}, u32[]{:S(2)}) collective-permute-start(f32[32,2,8,128]{3,2,1,0:T(8,128)S(1)} %get-tuple-element.28), channel_id=1, source_target_pairs={{8,16},{24,32},{40,48},{56,0},{16,8},{32,24},{48,40},{0,56},{9,17}... | collective-permute-start | bytes 786440 | tf_op jit(solution)/shard_map/ppermute | solution.py:278
  59.8 5.9 %collective-permute-start.6 = (f32[32,2,8,128]{3,2,1,0:T(8,128)S(1)}, f32[32,2,8,128]{3,2,1,0:T(8,128)S(1)}, u32[]{:S(2)}, u32[]{:S(2)}) collective-permute-start(f32[32,2,8,128]{3,2,1,0:T(8,128)S(1)} %collective-permute-done.4.near1), channel_id=1, source_target_pairs={{0,64},{64,0},{1,65},{65,1},{2,66},{66,2},{3,67},{67,3},{4,68},{68... | collective-permute-start | bytes 786440 | tf_op jit(solution)/shard_map/ppermute | solution.py:268
  62.7 4.1 %collective-permute-start.7 = (f32[32,2,8,128]{3,2,1,0:T(8,128)S(1)}, f32[32,2,8,128]{3,2,1,0:T(8,128)S(1)}, u32[]{:S(2)}, u32[]{:S(2)}) collective-permute-start(f32[32,2,8,128]{3,2,1,0:T(8,128)S(1)} %collective-permute-done.5.near2), channel_id=1, source_target_pairs={{0,64},{64,0},{1,65},{65,1},{2,66},{66,2},{3,67},{67,3},{4,68},{68... | collective-permute-start | bytes 786440 | tf_op jit(solution)/shard_map/ppermute | solution.py:268
  67.1 0.7 copy-start.4

commit v9 on v7

--- a/solution.py
+++ b/solution.py
@@ -14,7 +14,8 @@
 ROWS = ("h", "l", "z")
 TIME = ("x", "c")
 NEAR = ("x", "l", "z")
-SPREAD = ("x", "c", "l", "z")
+SPREAD = ("l", "z", "x", "c")
+SHARDS = ("l", "h", "z")
 SIDES = ((0, 3), (1, 2))
 
 
@@ -115,7 +116,7 @@
     both_ref, same_ref, decays_ref, m_ref, class_ref, out_ref, high_ref, low_ref
 ):
     for k in range(2):
-        high, low = split(m_ref[:, k].reshape(BLOCK, LANES))
+        high, low = split(in_rows(m_ref, k))
         high_ref[:, k * LANES : (k + 1) * LANES] = high
         low_ref[:, k * LANES : (k + 1) * LANES] = low
     solved = product(both_ref[...], high_ref[...], low_ref[...], False)
@@ -130,10 +131,17 @@
         out_ref[at, 2] = decays_ref[at]
 
 
+def in_rows(ref, k):
+    outer, inner, run = (lax.axis_size(name) for name in SHARDS)
+    starts = [(a * inner + b) * run for b in range(inner) for a in range(outer)]
+    pieces = [ref[at : at + run, k].reshape(-1, LANES) for at in starts]
+    return jnp.concatenate(pieces, axis=0)
+
+
 def rest_kernel(m1, m2, m3, high_ref, low_ref):
     for n, ref in enumerate((m1, m2, m3)):
         for k in range(2):
-            high, low = split(ref[:, k].reshape(BLOCK, LANES))
+            high, low = split(in_rows(ref, k))
             high_ref[k, :, n * LANES : (n + 1) * LANES] = high
             low_ref[k, :, n * LANES : (n + 1) * LANES] = low
 
@@ -194,18 +202,19 @@
             for i in range(4):
                 block = made[i].reshape(4, 8, LANES)
                 for x in range(4):
-                    out_ref[(x * 2 + core) * 16 + q * 4 + i] = block[x]
+                    out_ref[(q * 4 + i) * 8 + x * 2 + core] = block[x]
 
 
 def last_kernel(x_ref, class_ref, h0, l0, h1, l1, field_ref, adjoint_ref):
     c = lax.axis_index("c")
     v = place_along_x()[1]
+    tiles = x_ref[...].reshape(16, 8, 8, LANES)
     lines = []
     for u in range(2):
         pieces = []
         for k in range(4):
-            first = ((u * 2 + ((k // 2) ^ u)) * 2 + k % 2) * 16
-            turned = x_ref[first : first + 16].reshape(LANES, LANES).T
+            source = (u * 2 + ((k // 2) ^ u)) * 2 + k % 2
+            turned = tiles[:, source].reshape(LANES, LANES).T
             for b in range(2):
                 at = (u * 2 + b) * BLOCK + k * LANES
                 field_ref[0, :, at : at + LANES] = turned[b * PIECE : (b + 1) * PIECE]
@@ -257,7 +266,7 @@
     rows = offsets.shape[1]
     piece = lax.dynamic_slice(offsets, (0, 0, quarter * LANES), (2, rows, LANES))
     piece = piece.reshape(2 * rows, LANES)
-    own = swap(jnp.broadcast_to(piece, (BLOCK // rows, 2 * rows, LANES)), ROWS)
+    own = swap(jnp.broadcast_to(piece, (BLOCK // rows, 2 * rows, LANES)), SHARDS)
 
     shapes = (((1024, BLOCK), BF16), ((512, LANES), F32), ((32, 8, LANES), F32))
     operands = (forcing,) + partners(forcing) + (rate_class, rate_table)

time: 91.7 us -> 91.9 us (level)
  waiting for transfers between devices: 9.24 us -> 10.4 us
    all_to_all x2, starting transfers between devices: 24.9 us -> 21.4 us  [swap(): lax.all_to_all(values, axis, split_axis=0, concat_axis=0, axis_index_grou...]
    ppermute x2, starting transfers between devices: 5.68 us -> 8.51 us  [partners(): return (core, near, lax.ppermute(near, 'c', other))]
    all_to_all x2, waiting for transfers between devices: 3.77 us -> 5.25 us  [swap(): lax.all_to_all(values, axis, split_axis=0, concat_axis=0, axis_index_grou...]
    all_to_all x1, blocking collectives: 29 us -> 28.1 us  [swap(): lax.all_to_all(values, axis, split_axis=0, concat_axis=0, axis_index_grou...]
  transfers between devices with their start and end apart: 8 -> 8, of which waited for: 5 -> 4; matrix products, arithmetic and copies ran while one was open for 0% -> 0% of each run, Pallas kernels for 3% -> 3%
where the time goes in v9:
time: 91.9 us; the launch traced here: 91.3 us
  starting transfers between devices  43.9 us (48%)
  blocking collectives  28.1 us (31%)
  waiting for transfers between devices  10.4 us (11%)
  Pallas kernels  5.95 us (6%)
  local copies, waits for them, and re-layouts  2.28 us (2%)
    all_to_all x1, blocking collectives, swap(): lax.all_to_all(values, axis, split_axis=0, concat_axis=0, axis_index_grou...  28.1 us
    all_to_all x2, starting transfers between devices, swap(): lax.all_to_all(values, axis, split_axis=0, concat_axis=0, axis_index_grou...  21.4 us
    ppermute x2, starting transfers between devices, partners(): return (core, near, lax.ppermute(near, 'c', other))  8.51 us
    ppermute x2, starting transfers between devices, partners(): core = lax.ppermute(values, 'c', other)  7.76 us
    ppermute x2, starting transfers between devices, partners(): near = lax.ppermute(values, 'x', [(k, k ^ 1) for k in range(4)])  6.23 us
    pallas_call x5, Pallas kernels, call(): pl.pallas_call(kernel, out_shape=tuple((jax.ShapeDtypeStruct(*shape) for...  5.95 us
    all_to_all x2, waiting for transfers between devices, swap(): lax.all_to_all(values, axis, split_axis=0, concat_axis=0, axis_index_grou...  5.25 us
    ppermute x2, waiting for transfers between devices, partners(): return (core, near, lax.ppermute(near, 'c', other))  2.63 us
  transfers between devices with their start and end apart: 8, of which 4 were waited for; matrix products, arithmetic and copies ran while one was open for 0% of the time, Pallas kernels for 3%

profile of v9, /device:TPU:1, one launch (start us, length us, event | category | flops | bytes accessed | tf_op | source)
XLA Modules:
  0.0 91.3 jit_solution(4505069389433486917)
XLA Ops:
  0.6 0.0 copy-start
  0.7 0.7 copy-done
  1.4 0.8 broadcast_in_dim.3
  2.2 0.0 copy-start.1
  2.2 0.0 copy-start.2
  2.2 0.0 copy-start.5
  2.2 17.3 %all-to-all-start = ((f32[64,16,128]{2,1,0:T(8,128)}), f32[64,16,128]{2,1,0:T(8,128)S(1)}, u32[]{:S(2)}, u32[]{:S(2)}) async-start(f32[64,16,128]{2,1,0:T(8,128)} %broadcast_in_dim.3), calls=%async_computation | async-start | bytes 1048576 | tf_op jit(solution)/shard_map/all_to_all | solution.py:249
  19.5 0.0 copy-done.1
  19.5 3.1 %collective-permute-start.1 = (f32[1,32,2048]{2,1,0:T(8,128)S(1)}, f32[1,32,2048]{2,1,0:T(8,128)S(1)}, u32[]{:S(2)}, u32[]{:S(2)}) collective-permute-start(f32[1,32,2048]{2,1,0:T(8,128)S(1)} %copy-done.1), channel_id=1, source_target_pairs={{0,128},{128,0},{256,384},{384,256},{1,129},{129,1},{257,385},{385... | collective-permute-start | bytes 786440 | tf_op jit(solution)/shard_map/ppermute | solution.py:255
  22.7 3.1 %collective-permute-start = (f32[1,32,2048]{2,1,0:T(8,128)S(1)}, f32[1,32,2048]{2,1,0:T(8,128)S(1)}, u32[]{:S(2)}, u32[]{:S(2)}) collective-permute-start(f32[1,32,2048]{2,1,0:T(8,128)S(1)} %copy-done.1), channel_id=1, source_target_pairs={{0,64},{64,0},{1,65},{65,1},{2,66},{66,2},{3,67},{67,3},{4,68},{68... | collective-permute-start | bytes 786440 | tf_op jit(solution)/shard_map/ppermute | solution.py:257
  25.8 2.5 %collective-permute-done.1.f2 = f32[1,32,2048]{2,1,0:T(8,128)S(1)} collective-permute-done((f32[1,32,2048]{2,1,0:T(8,128)S(1)}, f32[1,32,2048]{2,1,0:T(8,128)S(1)}, u32[]{:S(2)}, u32[]{:S(2)}) %collective-permute-start.1) | collective-permute-done | bytes 262176 | tf_op jit(solution)/shard_map/ppermute | solution.py:255
  28.3 3.8 %collective-permute-start.2 = (f32[1,32,2048]{2,1,0:T(8,128)S(1)}, f32[1,32,2048]{2,1,0:T(8,128)S(1)}, u32[]{:S(2)}, u32[]{:S(2)}) collective-permute-start(f32[1,32,2048]{2,1,0:T(8,128)S(1)} %collective-permute-done.1.f2), channel_id=1, source_target_pairs={{0,64},{64,0},{1,65},{65,1},{2,66},{66,2},{3,67},{67,3},{4,68},{68... | collective-permute-start | bytes 786440 | tf_op jit(solution)/shard_map/ppermute | solution.py:258
  32.1 0.0 collective-permute-done.f1
  32.1 1.1 %collective-permute-done.2.f3 = f32[1,32,2048]{2,1,0:T(8,128)S(1)} collective-permute-done((f32[1,32,2048]{2,1,0:T(8,128)S(1)}, f32[1,32,2048]{2,1,0:T(8,128)S(1)}, u32[]{:S(2)}, u32[]{:S(2)}) %collective-permute-start.2) | collective-permute-done | bytes 262176 | tf_op jit(solution)/shard_map/ppermute | solution.py:258
  33.2 0.0 copy-done.2
  33.2 0.0 copy-done.5
  33.2 0.8 lines.1
  34.0 0.0 copy-start.3
  34.0 5.2 %all-to-all-done = f32[64,16,128]{2,1,0:T(8,128)S(1)} async-done(((f32[64,16,128]{2,1,0:T(8,128)}), f32[64,16,128]{2,1,0:T(8,128)S(1)}, u32[]{:S(2)}, u32[]{:S(2)}) %all-to-all-start) | async-done | bytes 524320 | tf_op jit(solution)/shard_map/all_to_all | solution.py:249
  39.2 3.1 %collective-permute-start.4 = (f32[64,2,8,128]{3,2,1,0:T(8,128)S(1)}, f32[64,2,8,128]{3,2,1,0:T(8,128)S(1)}, u32[]{:S(2)}, u32[]{:S(2)}) collective-permute-start(f32[64,2,8,128]{3,2,1,0:T(8,128)S(1)} %bitcast.5), channel_id=1, source_target_pairs={{0,128},{128,0},{256,384},{384,256},{1,129},{129,1},{257,385},{385... | collective-permute-start | bytes 1572872 | tf_op jit(solution)/shard_map/ppermute | solution.py:255
  42.4 0.0 copy-done.3
  42.4 1.5 %rows.1 = (f32[32,3,8,128]{3,2,1,0:T(8,128)}, bf16[512,256]{1,0:T(8,128)(2,1)S(1)}, bf16[512,256]{1,0:T(8,128)(2,1)S(1)}) custom-call(bf16[1024,512]{1,0:T(8,128)(2,1)S(1)} %get-tuple-element.20.both_ref, f32[512,128]{1,0:T(8,128)S(1)} %get-tuple-element.21.same_ref, f32[32,8,128]{2,1,0:T(8,128)S(1)} %get-tuple-element.22.decays_ref, ...), custom_call_target="tpu_custom_call" | custom-call | tf_op jit(solution)/shard_map/rows/pallas_call | solution.py:237
  43.8 4.1 %all-to-all-start.1 = ((f32[32,3,8,128]{3,2,1,0:T(8,128)}), f32[32,3,8,128]{3,2,1,0:T(8,128)S(1)}, u32[]{:S(2)}, u32[]{:S(2)}) async-start(f32[32,3,8,128]{3,2,1,0:T(8,128)} %get-tuple-element.24), calls=%async_computation.1 | async-start | bytes 786432 | tf_op jit(solution)/shard_map/all_to_all | solution.py:249
  48.0 4.6 %collective-permute-start.3 = (f32[64,2,8,128]{3,2,1,0:T(8,128)S(1)}, f32[64,2,8,128]{3,2,1,0:T(8,128)S(1)}, u32[]{:S(2)}, u32[]{:S(2)}) collective-permute-start(f32[64,2,8,128]{3,2,1,0:T(8,128)S(1)} %bitcast.7), channel_id=1, source_target_pairs={{0,64},{64,0},{1,65},{65,1},{2,66},{66,2},{3,67},{67,3},{4,68},{68... | collective-permute-start | bytes 1572872 | tf_op jit(solution)/shard_map/ppermute | solution.py:257
  52.6 0.0 collective-permute-done.4.m2
  52.6 4.7 %collective-permute-start.5 = (f32[64,2,8,128]{3,2,1,0:T(8,128)S(1)}, f32[64,2,8,128]{3,2,1,0:T(8,128)S(1)}, u32[]{:S(2)}, u32[]{:S(2)}) collective-permute-start(f32[64,2,8,128]{3,2,1,0:T(8,128)S(1)} %collective-permute-done.4.m2), channel_id=1, source_target_pairs={{0,64},{64,0},{1,65},{65,1},{2,66},{66,2},{3,67},{67,3},{4,68},{68... | collective-permute-start | bytes 1572872 | tf_op jit(solution)/shard_map/ppermute | solution.py:258
  57.4 0.0 collective-permute-done.3.m1
  57.4 1.5 %collective-permute-done.5.m3 = f32[64,2,8,128]{3,2,1,0:T(8,128)S(1)} collective-permute-done((f32[64,2,8,128]{3,2,1,0:T(8,128)S(1)}, f32[64,2,8,128]{3,2,1,0:T(8,128)S(1)}, u32[]{:S(2)}, u32[]{:S(2)}) %collective-permute-start.5) | collective-permute-done | bytes 524320 | tf_op jit(solution)/shard_map/ppermute | solution.py:258
  58.9 0.3 rest.1
  59.2 0.0 copy-start.4
  59.2 0.0 all-to-all-done.1.x_ref
  59.2 0.7 copy-done.4
  59.9 1.8 %middle.1 = f32[128,8,128]{2,1,0:T(8,128)S(1)} custom-call(f32[32,3,8,128]{3,2,1,0:T(8,128)S(1)} %all-to-all-done.1.x_ref, s32[16,128]{1,0:T(8,128)S(1)} %bitcast.10, bf16[512,256]{1,0:T(8,128)(2,1)S(1)} %get-tuple-element.28.h0, bf16[512,256]{1,0:T(8,128)(2,1)S(1)} %get-tuple-element.29.l0, bf16[2,512,384]{2,1,0:T(8,128)(2,1)S(1)} %get-tuple-element.30.h1, ...), custom_call_target="tpu_custom_call" | custom-call | tf_op jit(solution)/shard_map/middle/pallas_call | solution.py:237
  61.7 28.1 %all_to_all.15.x_ref = f32[128,8,128]{2,1,0:T(8,128)S(1)} all-to-all(f32[128,8,128]{2,1,0:T(8,128)S(1)} %middle.1), channel_id=1, replica_groups=mesh['x'=4,'c'=2,'h'=4,'l'=2,'z'=8] {'l','z','x','c'}, dimensions={0} | all-to-all | bytes 1048576 | tf_op jit(solution)/shard_map/all_to_all | solution.py:249
  89.7 1.6 %last.1 = (f32[1,32,2048]{2,1,0:T(8,128)}, f32[1,32,2048]{2,1,0:T(8,128)}) custom-call(f32[128,8,128]{2,1,0:T(8,128)S(1)} %all_to_all.15.x_ref, s32[16,128]{1,0:T(8,128)S(1)} %bitcast.9, bf16[512,256]{1,0:T(8,128)(2,1)S(1)} %get-tuple-element.28.h0, bf16[512,256]{1,0:T(8,128)(2,1)S(1)} %get-tuple-element.29.l0, ...), custom_call_target="tpu_custom_call" | custom-call | tf_op jit(solution)/shard_map/last/pallas_call | solution.py:237
  (1 shorter events, 0.0 us)
Async XLA Ops:
  0.6 0.8 copy-start
  2.2 17.3 %copy-start.1 = (f32[1,32,2048]{2,1,0:T(8,128)S(1)}, f32[1,32,2048]{2,1,0:T(8,128)}, u32[]{:S(2)}) copy-start(f32[1,32,2048]{2,1,0:T(8,128)} %f0.1) | copy-start | bytes 786436
  2.2 31.0 %copy-start.2 = (s32[32,2048]{1,0:T(8,128)S(1)}, s32[32,2048]{1,0:T(8,128)}, u32[]{:S(2)}) copy-start(s32[32,2048]{1,0:T(8,128)} %rate_ref.1) | copy-start | bytes 786436
  2.2 31.0 %copy-start.5 = (f32[16]{0:T(128)S(1)}, f32[16]{0:T(128)}, u32[]{:S(2)}) copy-start(f32[16]{0:T(128)} %table_ref.1) | copy-start | bytes 196
  2.2 37.0 %all-to-all-start = ((f32[64,16,128]{2,1,0:T(8,128)}), f32[64,16,128]{2,1,0:T(8,128)S(1)}, u32[]{:S(2)}, u32[]{:S(2)}) async-start(f32[64,16,128]{2,1,0:T(8,128)} %broadcast_in_dim.3), calls=%async_computation | async-start | bytes 1048576 | tf_op jit(solution)/shard_map/all_to_all | solution.py:249
  19.5 8.8 %collective-permute-start.1 = (f32[1,32,2048]{2,1,0:T(8,128)S(1)}, f32[1,32,2048]{2,1,0:T(8,128)S(1)}, u32[]{:S(2)}, u32[]{:S(2)}) collective-permute-start(f32[1,32,2048]{2,1,0:T(8,128)S(1)} %copy-done.1), channel_id=1, source_target_pairs={{0,128},{128,0},{256,384},{384,256},{1,129},{129,1},{257,385},{385... | collective-permute-start | bytes 786440 | tf_op jit(solution)/shard_map/ppermute | solution.py:255
  22.7 9.4 %collective-permute-start = (f32[1,32,2048]{2,1,0:T(8,128)S(1)}, f32[1,32,2048]{2,1,0:T(8,128)S(1)}, u32[]{:S(2)}, u32[]{:S(2)}) collective-permute-start(f32[1,32,2048]{2,1,0:T(8,128)S(1)} %copy-done.1), channel_id=1, source_target_pairs={{0,64},{64,0},{1,65},{65,1},{2,66},{66,2},{3,67},{67,3},{4,68},{68... | collective-permute-start | bytes 786440 | tf_op jit(solution)/shard_map/ppermute | solution.py:257
  28.3 4.9 %collective-permute-start.2 = (f32[1,32,2048]{2,1,0:T(8,128)S(1)}, f32[1,32,2048]{2,1,0:T(8,128)S(1)}, u32[]{:S(2)}, u32[]{:S(2)}) collective-permute-start(f32[1,32,2048]{2,1,0:T(8,128)S(1)} %collective-permute-done.1.f2), channel_id=1, source_target_pairs={{0,64},{64,0},{1,65},{65,1},{2,66},{66,2},{3,67},{67,3},{4,68},{68... | collective-permute-start | bytes 786440 | tf_op jit(solution)/shard_map/ppermute | solution.py:258
  34.0 8.4 %copy-start.3 = (s32[2048]{0:T(1024)S(1)}, s32[2048]{0:T(1024)}, u32[]{:S(2)}) copy-start(s32[2048]{0:T(1024)} %param.9) | copy-start | bytes 24580
  39.2 13.4 %collective-permute-start.4 = (f32[64,2,8,128]{3,2,1,0:T(8,128)S(1)}, f32[64,2,8,128]{3,2,1,0:T(8,128)S(1)}, u32[]{:S(2)}, u32[]{:S(2)}) collective-permute-start(f32[64,2,8,128]{3,2,1,0:T(8,128)S(1)} %bitcast.5), channel_id=1, source_target_pairs={{0,128},{128,0},{256,384},{384,256},{1,129},{129,1},{257,385},{385... | collective-permute-start | bytes 1572872 | tf_op jit(solution)/shard_map/ppermute | solution.py:255
  43.8 15.4 %all-to-all-start.1 = ((f32[32,3,8,128]{3,2,1,0:T(8,128)}), f32[32,3,8,128]{3,2,1,0:T(8,128)S(1)}, u32[]{:S(2)}, u32[]{:S(2)}) async-start(f32[32,3,8,128]{3,2,1,0:T(8,128)} %get-tuple-element.24), calls=%async_computation.1 | async-start | bytes 786432 | tf_op jit(solution)/shard_map/all_to_all | solution.py:249
  48.0 9.4 %collective-permute-start.3 = (f32[64,2,8,128]{3,2,1,0:T(8,128)S(1)}, f32[64,2,8,128]{3,2,1,0:T(8,128)S(1)}, u32[]{:S(2)}, u32[]{:S(2)}) collective-permute-start(f32[64,2,8,128]{3,2,1,0:T(8,128)S(1)} %bitcast.7), channel_id=1, source_target_pairs={{0,64},{64,0},{1,65},{65,1},{2,66},{66,2},{3,67},{67,3},{4,68},{68... | collective-permute-start | bytes 1572872 | tf_op jit(solution)/shard_map/ppermute | solution.py:257
  52.6 6.3 %collective-permute-start.5 = (f32[64,2,8,128]{3,2,1,0:T(8,128)S(1)}, f32[64,2,8,128]{3,2,1,0:T(8,128)S(1)}, u32[]{:S(2)}, u32[]{:S(2)}) collective-permute-start(f32[64,2,8,128]{3,2,1,0:T(8,128)S(1)} %collective-permute-done.4.m2), channel_id=1, source_target_pairs={{0,64},{64,0},{1,65},{65,1},{2,66},{66,2},{3,67},{67,3},{4,68},{68... | collective-permute-start | bytes 1572872 | tf_op jit(solution)/shard_map/ppermute | solution.py:258
  59.2 0.7 copy-start.4

commit v10 on v9

--- a/solution.py
+++ b/solution.py
@@ -14,8 +14,8 @@
 ROWS = ("h", "l", "z")
 TIME = ("x", "c")
 NEAR = ("x", "l", "z")
-SPREAD = ("l", "z", "x", "c")
-SHARDS = ("l", "h", "z")
+SPREAD = ("z", "l", "x", "c")
+SHARDS = ("z", "l", "h")
 SIDES = ((0, 3), (1, 2))
 
 
@@ -131,10 +131,19 @@
         out_ref[at, 2] = decays_ref[at]
 
 
+def places(order, outer):
+    step, steps = 1, {}
+    for name in reversed(order):
+        steps[name] = step
+        step *= lax.axis_size(name)
+    found = [0]
+    for name in outer:
+        found = [at + k * steps[name] for at in found for k in range(lax.axis_size(name))]
+    return found
+
+
 def in_rows(ref, k):
-    outer, inner, run = (lax.axis_size(name) for name in SHARDS)
-    starts = [(a * inner + b) * run for b in range(inner) for a in range(outer)]
-    pieces = [ref[at : at + run, k].reshape(-1, LANES) for at in starts]
+    pieces = [ref[at, k] for at in places(SHARDS, ROWS)]
     return jnp.concatenate(pieces, axis=0)
 
 
@@ -190,6 +199,8 @@
     adjoint = back + solve(own_first(back, v, c), mask, matrices, True)
     field = jnp.concatenate(field, axis=0).reshape(4, 4, 8, BLOCK)
     adjoint = adjoint.reshape(4, 4, 8, BLOCK)
+    sources = places(SPREAD, ("l", "z"))
+    times = places(SPREAD, TIME)
     for core in range(2):
         for q in range(4):
             lanes = slice(q * LANES, (q + 1) * LANES)
@@ -202,19 +213,21 @@
             for i in range(4):
                 block = made[i].reshape(4, 8, LANES)
                 for x in range(4):
-                    out_ref[(q * 4 + i) * 8 + x * 2 + core] = block[x]
+                    out_ref[sources[q * 4 + i] + times[x * 2 + core]] = block[x]
 
 
 def last_kernel(x_ref, class_ref, h0, l0, h1, l1, field_ref, adjoint_ref):
     c = lax.axis_index("c")
     v = place_along_x()[1]
-    tiles = x_ref[...].reshape(16, 8, 8, LANES)
+    sources = places(SPREAD, ("l", "z"))
+    times = places(SPREAD, TIME)
     lines = []
     for u in range(2):
         pieces = []
         for k in range(4):
             source = (u * 2 + ((k // 2) ^ u)) * 2 + k % 2
-            turned = tiles[:, source].reshape(LANES, LANES).T
+            tiles = [x_ref[at + times[source]] for at in sources]
+            turned = jnp.concatenate(tiles, axis=0).T
             for b in range(2):
                 at = (u * 2 + b) * BLOCK + k * LANES
                 field_ref[0, :, at : at + LANES] = turned[b * PIECE : (b + 1) * PIECE]

time: 91.9 us -> 91.1 us (level)
  transfers between devices with their start and end apart: 8 -> 8, of which waited for: 4 -> 5; matrix products, arithmetic and copies ran while one was open for 0% -> 0% of each run, Pallas kernels for 3% -> 3%
where the time goes in v10:
time: 91.1 us; the launch traced here: 90.5 us
  starting transfers between devices  43.9 us (48%)
  blocking collectives  28.1 us (31%)
  waiting for transfers between devices  9.61 us (11%)
  Pallas kernels  5.94 us (7%)
  local copies, waits for them, and re-layouts  2.11 us (2%)
    all_to_all x1, blocking collectives, swap(): lax.all_to_all(values, axis, split_axis=0, concat_axis=0, axis_index_grou...  28.1 us
    all_to_all x2, starting transfers between devices, swap(): lax.all_to_all(values, axis, split_axis=0, concat_axis=0, axis_index_grou...  22.1 us
    ppermute x2, starting transfers between devices, partners(): core = lax.ppermute(values, 'c', other)  7.84 us
    ppermute x2, starting transfers between devices, partners(): return (core, near, lax.ppermute(near, 'c', other))  7.71 us
    ppermute x2, starting transfers between devices, partners(): near = lax.ppermute(values, 'x', [(k, k ^ 1) for k in range(4)])  6.23 us
    pallas_call x5, Pallas kernels, call(): pl.pallas_call(kernel, out_shape=tuple((jax.ShapeDtypeStruct(*shape) for...  5.94 us
    all_to_all x2, waiting for transfers between devices, swap(): lax.all_to_all(values, axis, split_axis=0, concat_axis=0, axis_index_grou...  4.5 us
    ppermute x2, waiting for transfers between devices, partners(): return (core, near, lax.ppermute(near, 'c', other))  2.63 us
  transfers between devices with their start and end apart: 8, of which 5 were waited for; matrix products, arithmetic and copies ran while one was open for 0% of the time, Pallas kernels for 3%

profile of v10, /device:TPU:1, one launch (start us, length us, event | category | flops | bytes accessed | tf_op | source)
XLA Modules:
  0.0 90.5 jit_solution(3774319936903613412)
XLA Ops:
  0.6 0.0 copy-start
  0.7 0.7 copy-done
  1.4 0.8 broadcast_in_dim.3
  2.2 0.0 copy-start.1
  2.2 0.0 copy-start.2
  2.2 0.0 copy-start.5
  2.2 17.3 %all-to-all-start = ((f32[64,16,128]{2,1,0:T(8,128)}), f32[64,16,128]{2,1,0:T(8,128)S(1)}, u32[]{:S(2)}, u32[]{:S(2)}) async-start(f32[64,16,128]{2,1,0:T(8,128)} %broadcast_in_dim.3), calls=%async_computation | async-start | bytes 1048576 | tf_op jit(solution)/shard_map/all_to_all | solution.py:262
  19.5 0.0 copy-done.1
  19.5 3.1 %collective-permute-start.1 = (f32[1,32,2048]{2,1,0:T(8,128)S(1)}, f32[1,32,2048]{2,1,0:T(8,128)S(1)}, u32[]{:S(2)}, u32[]{:S(2)}) collective-permute-start(f32[1,32,2048]{2,1,0:T(8,128)S(1)} %copy-done.1), channel_id=1, source_target_pairs={{0,128},{128,0},{256,384},{384,256},{1,129},{129,1},{257,385},{385... | collective-permute-start | bytes 786440 | tf_op jit(solution)/shard_map/ppermute | solution.py:268
  22.7 3.1 %collective-permute-start = (f32[1,32,2048]{2,1,0:T(8,128)S(1)}, f32[1,32,2048]{2,1,0:T(8,128)S(1)}, u32[]{:S(2)}, u32[]{:S(2)}) collective-permute-start(f32[1,32,2048]{2,1,0:T(8,128)S(1)} %copy-done.1), channel_id=1, source_target_pairs={{0,64},{64,0},{1,65},{65,1},{2,66},{66,2},{3,67},{67,3},{4,68},{68... | collective-permute-start | bytes 786440 | tf_op jit(solution)/shard_map/ppermute | solution.py:270
  25.8 2.5 %collective-permute-done.1.f2 = f32[1,32,2048]{2,1,0:T(8,128)S(1)} collective-permute-done((f32[1,32,2048]{2,1,0:T(8,128)S(1)}, f32[1,32,2048]{2,1,0:T(8,128)S(1)}, u32[]{:S(2)}, u32[]{:S(2)}) %collective-permute-start.1) | collective-permute-done | bytes 262176 | tf_op jit(solution)/shard_map/ppermute | solution.py:268
  28.3 3.8 %collective-permute-start.2 = (f32[1,32,2048]{2,1,0:T(8,128)S(1)}, f32[1,32,2048]{2,1,0:T(8,128)S(1)}, u32[]{:S(2)}, u32[]{:S(2)}) collective-permute-start(f32[1,32,2048]{2,1,0:T(8,128)S(1)} %collective-permute-done.1.f2), channel_id=1, source_target_pairs={{0,64},{64,0},{1,65},{65,1},{2,66},{66,2},{3,67},{67,3},{4,68},{68... | collective-permute-start | bytes 786440 | tf_op jit(solution)/shard_map/ppermute | solution.py:271
  32.1 0.0 collective-permute-done.f1
  32.1 1.1 %collective-permute-done.2.f3 = f32[1,32,2048]{2,1,0:T(8,128)S(1)} collective-permute-done((f32[1,32,2048]{2,1,0:T(8,128)S(1)}, f32[1,32,2048]{2,1,0:T(8,128)S(1)}, u32[]{:S(2)}, u32[]{:S(2)}) %collective-permute-start.2) | collective-permute-done | bytes 262176 | tf_op jit(solution)/shard_map/ppermute | solution.py:271
  33.2 0.0 copy-done.2
  33.2 0.0 copy-done.5
  33.2 0.8 lines.1
  34.0 0.0 copy-start.3
  34.0 4.3 %all-to-all-done = f32[64,16,128]{2,1,0:T(8,128)S(1)} async-done(((f32[64,16,128]{2,1,0:T(8,128)}), f32[64,16,128]{2,1,0:T(8,128)S(1)}, u32[]{:S(2)}, u32[]{:S(2)}) %all-to-all-start) | async-done | bytes 524320 | tf_op jit(solution)/shard_map/all_to_all | solution.py:262
  38.3 3.1 %collective-permute-start.4 = (f32[64,2,8,128]{3,2,1,0:T(8,128)S(1)}, f32[64,2,8,128]{3,2,1,0:T(8,128)S(1)}, u32[]{:S(2)}, u32[]{:S(2)}) collective-permute-start(f32[64,2,8,128]{3,2,1,0:T(8,128)S(1)} %bitcast.5), channel_id=1, source_target_pairs={{0,128},{128,0},{256,384},{384,256},{1,129},{129,1},{257,385},{385... | collective-permute-start | bytes 1572872 | tf_op jit(solution)/shard_map/ppermute | solution.py:268
  41.4 0.0 copy-done.3
  41.4 1.5 %rows.1 = (f32[32,3,8,128]{3,2,1,0:T(8,128)}, bf16[512,256]{1,0:T(8,128)(2,1)S(1)}, bf16[512,256]{1,0:T(8,128)(2,1)S(1)}) custom-call(bf16[1024,512]{1,0:T(8,128)(2,1)S(1)} %get-tuple-element.20.both_ref, f32[512,128]{1,0:T(8,128)S(1)} %get-tuple-element.21.same_ref, f32[32,8,128]{2,1,0:T(8,128)S(1)} %get-tuple-element.22.decays_ref, ...), custom_call_target="tpu_custom_call" | custom-call | tf_op jit(solution)/shard_map/rows/pallas_call | solution.py:250
  42.9 4.8 %all-to-all-start.1 = ((f32[32,3,8,128]{3,2,1,0:T(8,128)}), f32[32,3,8,128]{3,2,1,0:T(8,128)S(1)}, u32[]{:S(2)}, u32[]{:S(2)}) async-start(f32[32,3,8,128]{3,2,1,0:T(8,128)} %get-tuple-element.24), calls=%async_computation.1 | async-start | bytes 786432 | tf_op jit(solution)/shard_map/all_to_all | solution.py:262
  47.8 4.7 %collective-permute-start.3 = (f32[64,2,8,128]{3,2,1,0:T(8,128)S(1)}, f32[64,2,8,128]{3,2,1,0:T(8,128)S(1)}, u32[]{:S(2)}, u32[]{:S(2)}) collective-permute-start(f32[64,2,8,128]{3,2,1,0:T(8,128)S(1)} %bitcast.7), channel_id=1, source_target_pairs={{0,64},{64,0},{1,65},{65,1},{2,66},{66,2},{3,67},{67,3},{4,68},{68... | collective-permute-start | bytes 1572872 | tf_op jit(solution)/shard_map/ppermute | solution.py:270
  52.5 0.0 collective-permute-done.4.m2
  52.5 4.0 %collective-permute-start.5 = (f32[64,2,8,128]{3,2,1,0:T(8,128)S(1)}, f32[64,2,8,128]{3,2,1,0:T(8,128)S(1)}, u32[]{:S(2)}, u32[]{:S(2)}) collective-permute-start(f32[64,2,8,128]{3,2,1,0:T(8,128)S(1)} %collective-permute-done.4.m2), channel_id=1, source_target_pairs={{0,64},{64,0},{1,65},{65,1},{2,66},{66,2},{3,67},{67,3},{4,68},{68... | collective-permute-start | bytes 1572872 | tf_op jit(solution)/shard_map/ppermute | solution.py:271
  56.4 0.0 collective-permute-done.3.m1
  56.5 1.5 %collective-permute-done.5.m3 = f32[64,2,8,128]{3,2,1,0:T(8,128)S(1)} collective-permute-done((f32[64,2,8,128]{3,2,1,0:T(8,128)S(1)}, f32[64,2,8,128]{3,2,1,0:T(8,128)S(1)}, u32[]{:S(2)}, u32[]{:S(2)}) %collective-permute-start.5) | collective-permute-done | bytes 524320 | tf_op jit(solution)/shard_map/ppermute | solution.py:271
  58.0 0.3 rest.1
  58.3 0.0 copy-start.4
  58.3 0.2 all-to-all-done.1.x_ref
  58.5 0.5 copy-done.4
  59.0 1.7 %middle.1 = f32[128,8,128]{2,1,0:T(8,128)S(1)} custom-call(f32[32,3,8,128]{3,2,1,0:T(8,128)S(1)} %all-to-all-done.1.x_ref, s32[16,128]{1,0:T(8,128)S(1)} %bitcast.10, bf16[512,256]{1,0:T(8,128)(2,1)S(1)} %get-tuple-element.28.h0, bf16[512,256]{1,0:T(8,128)(2,1)S(1)} %get-tuple-element.29.l0, bf16[2,512,384]{2,1,0:T(8,128)(2,1)S(1)} %get-tuple-element.30.h1, ...), custom_call_target="tpu_custom_call" | custom-call | tf_op jit(solution)/shard_map/middle/pallas_call | solution.py:250
  60.7 28.1 %all_to_all.15.x_ref = f32[128,8,128]{2,1,0:T(8,128)S(1)} all-to-all(f32[128,8,128]{2,1,0:T(8,128)S(1)} %middle.1), channel_id=1, replica_groups=mesh['x'=4,'c'=2,'h'=4,'l'=2,'z'=8] {'z','l','x','c'}, dimensions={0} | all-to-all | bytes 1048576 | tf_op jit(solution)/shard_map/all_to_all | solution.py:262
  88.9 1.6 %last.1 = (f32[1,32,2048]{2,1,0:T(8,128)}, f32[1,32,2048]{2,1,0:T(8,128)}) custom-call(f32[128,8,128]{2,1,0:T(8,128)S(1)} %all_to_all.15.x_ref, s32[16,128]{1,0:T(8,128)S(1)} %bitcast.9, bf16[512,256]{1,0:T(8,128)(2,1)S(1)} %get-tuple-element.28.h0, bf16[512,256]{1,0:T(8,128)(2,1)S(1)} %get-tuple-element.29.l0, ...), custom_call_target="tpu_custom_call" | custom-call | tf_op jit(solution)/shard_map/last/pallas_call | solution.py:250
  (1 shorter events, 0.0 us)
Async XLA Ops:
  0.6 0.8 copy-start
  2.2 17.3 %copy-start.1 = (f32[1,32,2048]{2,1,0:T(8,128)S(1)}, f32[1,32,2048]{2,1,0:T(8,128)}, u32[]{:S(2)}) copy-start(f32[1,32,2048]{2,1,0:T(8,128)} %f0.1) | copy-start | bytes 786436
  2.2 31.0 %copy-start.2 = (s32[32,2048]{1,0:T(8,128)S(1)}, s32[32,2048]{1,0:T(8,128)}, u32[]{:S(2)}) copy-start(s32[32,2048]{1,0:T(8,128)} %rate_ref.1) | copy-start | bytes 786436
  2.2 31.0 %copy-start.5 = (f32[16]{0:T(128)S(1)}, f32[16]{0:T(128)}, u32[]{:S(2)}) copy-start(f32[16]{0:T(128)} %table_ref.1) | copy-start | bytes 196
  2.2 36.1 %all-to-all-start = ((f32[64,16,128]{2,1,0:T(8,128)}), f32[64,16,128]{2,1,0:T(8,128)S(1)}, u32[]{:S(2)}, u32[]{:S(2)}) async-start(f32[64,16,128]{2,1,0:T(8,128)} %broadcast_in_dim.3), calls=%async_computation | async-start | bytes 1048576 | tf_op jit(solution)/shard_map/all_to_all | solution.py:262
  19.5 8.8 %collective-permute-start.1 = (f32[1,32,2048]{2,1,0:T(8,128)S(1)}, f32[1,32,2048]{2,1,0:T(8,128)S(1)}, u32[]{:S(2)}, u32[]{:S(2)}) collective-permute-start(f32[1,32,2048]{2,1,0:T(8,128)S(1)} %copy-done.1), channel_id=1, source_target_pairs={{0,128},{128,0},{256,384},{384,256},{1,129},{129,1},{257,385},{385... | collective-permute-start | bytes 786440 | tf_op jit(solution)/shard_map/ppermute | solution.py:268
  22.7 9.4 %collective-permute-start = (f32[1,32,2048]{2,1,0:T(8,128)S(1)}, f32[1,32,2048]{2,1,0:T(8,128)S(1)}, u32[]{:S(2)}, u32[]{:S(2)}) collective-permute-start(f32[1,32,2048]{2,1,0:T(8,128)S(1)} %copy-done.1), channel_id=1, source_target_pairs={{0,64},{64,0},{1,65},{65,1},{2,66},{66,2},{3,67},{67,3},{4,68},{68... | collective-permute-start | bytes 786440 | tf_op jit(solution)/shard_map/ppermute | solution.py:270
  28.3 4.9 %collective-permute-start.2 = (f32[1,32,2048]{2,1,0:T(8,128)S(1)}, f32[1,32,2048]{2,1,0:T(8,128)S(1)}, u32[]{:S(2)}, u32[]{:S(2)}) collective-permute-start(f32[1,32,2048]{2,1,0:T(8,128)S(1)} %collective-permute-done.1.f2), channel_id=1, source_target_pairs={{0,64},{64,0},{1,65},{65,1},{2,66},{66,2},{3,67},{67,3},{4,68},{68... | collective-permute-start | bytes 786440 | tf_op jit(solution)/shard_map/ppermute | solution.py:271
  34.0 7.4 %copy-start.3 = (s32[2048]{0:T(1024)S(1)}, s32[2048]{0:T(1024)}, u32[]{:S(2)}) copy-start(s32[2048]{0:T(1024)} %param.9) | copy-start | bytes 24580
  38.3 14.2 %collective-permute-start.4 = (f32[64,2,8,128]{3,2,1,0:T(8,128)S(1)}, f32[64,2,8,128]{3,2,1,0:T(8,128)S(1)}, u32[]{:S(2)}, u32[]{:S(2)}) collective-permute-start(f32[64,2,8,128]{3,2,1,0:T(8,128)S(1)} %bitcast.5), channel_id=1, source_target_pairs={{0,128},{128,0},{256,384},{384,256},{1,129},{129,1},{257,385},{385... | collective-permute-start | bytes 1572872 | tf_op jit(solution)/shard_map/ppermute | solution.py:268
  42.9 15.6 %all-to-all-start.1 = ((f32[32,3,8,128]{3,2,1,0:T(8,128)}), f32[32,3,8,128]{3,2,1,0:T(8,128)S(1)}, u32[]{:S(2)}, u32[]{:S(2)}) async-start(f32[32,3,8,128]{3,2,1,0:T(8,128)} %get-tuple-element.24), calls=%async_computation.1 | async-start | bytes 786432 | tf_op jit(solution)/shard_map/all_to_all | solution.py:262
  47.8 8.7 %collective-permute-start.3 = (f32[64,2,8,128]{3,2,1,0:T(8,128)S(1)}, f32[64,2,8,128]{3,2,1,0:T(8,128)S(1)}, u32[]{:S(2)}, u32[]{:S(2)}) collective-permute-start(f32[64,2,8,128]{3,2,1,0:T(8,128)S(1)} %bitcast.7), channel_id=1, source_target_pairs={{0,64},{64,0},{1,65},{65,1},{2,66},{66,2},{3,67},{67,3},{4,68},{68... | collective-permute-start | bytes 1572872 | tf_op jit(solution)/shard_map/ppermute | solution.py:270
  52.5 5.5 %collective-permute-start.5 = (f32[64,2,8,128]{3,2,1,0:T(8,128)S(1)}, f32[64,2,8,128]{3,2,1,0:T(8,128)S(1)}, u32[]{:S(2)}, u32[]{:S(2)}) collective-permute-start(f32[64,2,8,128]{3,2,1,0:T(8,128)S(1)} %collective-permute-done.4.m2), channel_id=1, source_target_pairs={{0,64},{64,0},{1,65},{65,1},{2,66},{66,2},{3,67},{67,3},{4,68},{68... | collective-permute-start | bytes 1572872 | tf_op jit(solution)/shard_map/ppermute | solution.py:271
  58.3 0.7 copy-start.4

commit v11 on v10

--- a/solution.py
+++ b/solution.py
@@ -17,6 +17,11 @@
 SPREAD = ("z", "l", "x", "c")
 SHARDS = ("z", "l", "h")
 SIDES = ((0, 3), (1, 2))
+
+
+def near_place(side, line):
+    l, z = divmod(line, 8)
+    return (z * 2 + l) * 2 + side
 
 
 def place_along_x():
@@ -123,12 +128,13 @@
     solved = jnp.where(row_mask(class_ref, 16), solved[:, :LANES], solved[:, LANES:])
     solved = solved + same_ref[...]
     for pair in range(2):
-        at = slice(pair * 16, (pair + 1) * 16)
         for far in range(2):
             first = (far * 2 + pair) * LANES
-            turned = solved[first : first + LANES].T
-            out_ref[at, far] = turned.reshape(16, 8, LANES)
-        out_ref[at, 2] = decays_ref[at]
+            turned = solved[first : first + LANES].T.reshape(16, 8, LANES)
+            for line in range(16):
+                out_ref[near_place(pair, line), far] = turned[line]
+        for line in range(16):
+            out_ref[near_place(pair, line), 2] = decays_ref[pair * 16 + line]
 
 
 def places(order, outer):
@@ -158,13 +164,20 @@
 def middle_kernel(x_ref, class_ref, h0, l0, h1, l1, out_ref, a_ref, r_ref):
     c = lax.axis_index("c")
     u, v = place_along_x()
-    tiles = x_ref[...].reshape(2, 4, 4, 3, 8, LANES)
-    made = exchange_lanes([tiles[:, :, i, :2].reshape(128, LANES) for i in range(4)])
+    tiles = []
+    for i in range(4):
+        found = [near_place(side, q * 4 + i) for side in range(2) for q in range(4)]
+        tiles.append(jnp.concatenate([x_ref[at, :2] for at in found], axis=0))
+    made = exchange_lanes([tile.reshape(128, LANES) for tile in tiles])
     for tb in range(4):
         block = made[tb].reshape(2, 4, 2, 8, LANES)
         for q in range(4):
             a_ref[:, :, tb, :, q * LANES : (q + 1) * LANES] = block[:, q]
-    made = exchange_lanes([tiles[0, :, i, 2].reshape(32, LANES) for i in range(4)])
+    tiles = []
+    for i in range(4):
+        found = [near_place(0, q * 4 + i) for q in range(4)]
+        tiles.append(jnp.concatenate([x_ref[at, 2] for at in found], axis=0))
+    made = exchange_lanes(tiles)
     for b in range(2):
         block = made[b].reshape(4, 8, LANES)
         for q in range(4):
@@ -292,7 +305,10 @@
     operands = (*lines, own, row_lines)
     out, *own = call(rows_kernel, "rows", shapes, operands)
     count = lax.axis_size(("l", "z"))
-    groups = [[x * count + k for x in side for k in range(count)] for side in SIDES]
+    groups = []
+    for side in SIDES:
+        lines = [l * 8 + z for z in range(8) for l in range(2)]
+        groups.append([x * count + line for line in lines for x in side])
     out = swap(out, NEAR, groups)
     shapes = (((2, BLOCK, 384), BF16),) * 2
     rest = call(rest_kernel, "rest", shapes, rest)

time: 91.1 us -> 91 us (level)
  waiting for transfers between devices: 9.61 us -> 11 us
    all_to_all x2, waiting for transfers between devices: 4.5 us -> 5.93 us  [swap(): lax.all_to_all(values, axis, split_axis=0, concat_axis=0, axis_index_grou...]
    all_to_all x1, blocking collectives: 28.1 us -> 27.2 us  [swap(): lax.all_to_all(values, axis, split_axis=0, concat_axis=0, axis_index_grou...]
where the time goes in v11:
time: 91 us; the launch traced here: 90.4 us
  starting transfers between devices  43.9 us (48%)
  blocking collectives  27.2 us (30%)
  waiting for transfers between devices  11 us (12%)
  Pallas kernels  5.94 us (7%)
  local copies, waits for them, and re-layouts  1.61 us (2%)
    all_to_all x1, blocking collectives, swap(): lax.all_to_all(values, axis, split_axis=0, concat_axis=0, axis_index_grou...  27.2 us
    all_to_all x2, starting transfers between devices, swap(): lax.all_to_all(values, axis, split_axis=0, concat_axis=0, axis_index_grou...  22.1 us
    ppermute x2, starting transfers between devices, partners(): core = lax.ppermute(values, 'c', other)  7.84 us
    ppermute x2, starting transfers between devices, partners(): return (core, near, lax.ppermute(near, 'c', other))  7.71 us
    ppermute x2, starting transfers between devices, partners(): near = lax.ppermute(values, 'x', [(k, k ^ 1) for k in range(4)])  6.23 us
    pallas_call x5, Pallas kernels, call(): pl.pallas_call(kernel, out_shape=tuple((jax.ShapeDtypeStruct(*shape) for...  5.94 us
    all_to_all x2, waiting for transfers between devices, swap(): lax.all_to_all(values, axis, split_axis=0, concat_axis=0, axis_index_grou...  5.93 us
    ppermute x2, waiting for transfers between devices, partners(): return (core, near, lax.ppermute(near, 'c', other))  2.63 us
  transfers between devices with their start and end apart: 8, of which 5 were waited for; matrix products, arithmetic and copies ran while one was open for 0% of the time, Pallas kernels for 3%

profile of v11, /device:TPU:1, one launch (start us, length us, event | category | flops | bytes accessed | tf_op | source)
XLA Modules:
  0.0 90.4 jit_solution(13574093321974467936)
XLA Ops:
  0.6 0.0 copy-start
  0.7 0.7 copy-done
  1.4 0.8 broadcast_in_dim.3
  2.2 0.0 copy-start.1
  2.2 0.0 copy-start.2
  2.2 0.0 copy-start.5
  2.2 17.3 %all-to-all-start = ((f32[64,16,128]{2,1,0:T(8,128)}), f32[64,16,128]{2,1,0:T(8,128)S(1)}, u32[]{:S(2)}, u32[]{:S(2)}) async-start(f32[64,16,128]{2,1,0:T(8,128)} %broadcast_in_dim.3), calls=%async_computation | async-start | bytes 1048576 | tf_op jit(solution)/shard_map/all_to_all | solution.py:275
  19.5 0.0 copy-done.1
  19.5 3.1 %collective-permute-start.1 = (f32[1,32,2048]{2,1,0:T(8,128)S(1)}, f32[1,32,2048]{2,1,0:T(8,128)S(1)}, u32[]{:S(2)}, u32[]{:S(2)}) collective-permute-start(f32[1,32,2048]{2,1,0:T(8,128)S(1)} %copy-done.1), channel_id=1, source_target_pairs={{0,128},{128,0},{256,384},{384,256},{1,129},{129,1},{257,385},{385... | collective-permute-start | bytes 786440 | tf_op jit(solution)/shard_map/ppermute | solution.py:281
  22.7 3.1 %collective-permute-start = (f32[1,32,2048]{2,1,0:T(8,128)S(1)}, f32[1,32,2048]{2,1,0:T(8,128)S(1)}, u32[]{:S(2)}, u32[]{:S(2)}) collective-permute-start(f32[1,32,2048]{2,1,0:T(8,128)S(1)} %copy-done.1), channel_id=1, source_target_pairs={{0,64},{64,0},{1,65},{65,1},{2,66},{66,2},{3,67},{67,3},{4,68},{68... | collective-permute-start | bytes 786440 | tf_op jit(solution)/shard_map/ppermute | solution.py:283
  25.8 2.5 %collective-permute-done.1.f2 = f32[1,32,2048]{2,1,0:T(8,128)S(1)} collective-permute-done((f32[1,32,2048]{2,1,0:T(8,128)S(1)}, f32[1,32,2048]{2,1,0:T(8,128)S(1)}, u32[]{:S(2)}, u32[]{:S(2)}) %collective-permute-start.1) | collective-permute-done | bytes 262176 | tf_op jit(solution)/shard_map/ppermute | solution.py:281
  28.3 3.8 %collective-permute-start.2 = (f32[1,32,2048]{2,1,0:T(8,128)S(1)}, f32[1,32,2048]{2,1,0:T(8,128)S(1)}, u32[]{:S(2)}, u32[]{:S(2)}) collective-permute-start(f32[1,32,2048]{2,1,0:T(8,128)S(1)} %collective-permute-done.1.f2), channel_id=1, source_target_pairs={{0,64},{64,0},{1,65},{65,1},{2,66},{66,2},{3,67},{67,3},{4,68},{68... | collective-permute-start | bytes 786440 | tf_op jit(solution)/shard_map/ppermute | solution.py:284
  32.1 0.0 collective-permute-done.f1
  32.1 1.1 %collective-permute-done.2.f3 = f32[1,32,2048]{2,1,0:T(8,128)S(1)} collective-permute-done((f32[1,32,2048]{2,1,0:T(8,128)S(1)}, f32[1,32,2048]{2,1,0:T(8,128)S(1)}, u32[]{:S(2)}, u32[]{:S(2)}) %collective-permute-start.2) | collective-permute-done | bytes 262176 | tf_op jit(solution)/shard_map/ppermute | solution.py:284
  33.2 0.0 copy-done.2
  33.2 0.0 copy-done.5
  33.2 0.8 lines.1
  34.0 0.0 copy-start.3
  34.0 4.3 %all-to-all-done = f32[64,16,128]{2,1,0:T(8,128)S(1)} async-done(((f32[64,16,128]{2,1,0:T(8,128)}), f32[64,16,128]{2,1,0:T(8,128)S(1)}, u32[]{:S(2)}, u32[]{:S(2)}) %all-to-all-start) | async-done | bytes 524320 | tf_op jit(solution)/shard_map/all_to_all | solution.py:275
  38.3 3.1 %collective-permute-start.4 = (f32[64,2,8,128]{3,2,1,0:T(8,128)S(1)}, f32[64,2,8,128]{3,2,1,0:T(8,128)S(1)}, u32[]{:S(2)}, u32[]{:S(2)}) collective-permute-start(f32[64,2,8,128]{3,2,1,0:T(8,128)S(1)} %bitcast.5), channel_id=1, source_target_pairs={{0,128},{128,0},{256,384},{384,256},{1,129},{129,1},{257,385},{385... | collective-permute-start | bytes 1572872 | tf_op jit(solution)/shard_map/ppermute | solution.py:281
  41.4 0.0 copy-done.3
  41.4 1.5 %rows.1 = (f32[32,3,8,128]{3,2,1,0:T(8,128)}, bf16[512,256]{1,0:T(8,128)(2,1)S(1)}, bf16[512,256]{1,0:T(8,128)(2,1)S(1)}) custom-call(bf16[1024,512]{1,0:T(8,128)(2,1)S(1)} %get-tuple-element.20.both_ref, f32[512,128]{1,0:T(8,128)S(1)} %get-tuple-element.21.same_ref, f32[32,8,128]{2,1,0:T(8,128)S(1)} %get-tuple-element.22.decays_ref, ...), custom_call_target="tpu_custom_call" | custom-call | tf_op jit(solution)/shard_map/rows/pallas_call | solution.py:263
  42.9 4.8 %all-to-all-start.1 = ((f32[32,3,8,128]{3,2,1,0:T(8,128)}), f32[32,3,8,128]{3,2,1,0:T(8,128)S(1)}, u32[]{:S(2)}, u32[]{:S(2)}) async-start(f32[32,3,8,128]{3,2,1,0:T(8,128)} %get-tuple-element.24), calls=%async_computation.1 | async-start | bytes 786432 | tf_op jit(solution)/shard_map/all_to_all | solution.py:275
  47.8 4.7 %collective-permute-start.3 = (f32[64,2,8,128]{3,2,1,0:T(8,128)S(1)}, f32[64,2,8,128]{3,2,1,0:T(8,128)S(1)}, u32[]{:S(2)}, u32[]{:S(2)}) collective-permute-start(f32[64,2,8,128]{3,2,1,0:T(8,128)S(1)} %bitcast.7), channel_id=1, source_target_pairs={{0,64},{64,0},{1,65},{65,1},{2,66},{66,2},{3,67},{67,3},{4,68},{68... | collective-permute-start | bytes 1572872 | tf_op jit(solution)/shard_map/ppermute | solution.py:283
  52.5 0.0 collective-permute-done.4.m2
  52.5 3.9 %collective-permute-start.5 = (f32[64,2,8,128]{3,2,1,0:T(8,128)S(1)}, f32[64,2,8,128]{3,2,1,0:T(8,128)S(1)}, u32[]{:S(2)}, u32[]{:S(2)}) collective-permute-start(f32[64,2,8,128]{3,2,1,0:T(8,128)S(1)} %collective-permute-done.4.m2), channel_id=1, source_target_pairs={{0,64},{64,0},{1,65},{65,1},{2,66},{66,2},{3,67},{67,3},{4,68},{68... | collective-permute-start | bytes 1572872 | tf_op jit(solution)/shard_map/ppermute | solution.py:284
  56.4 0.0 collective-permute-done.3.m1
  56.5 1.5 %collective-permute-done.5.m3 = f32[64,2,8,128]{3,2,1,0:T(8,128)S(1)} collective-permute-done((f32[64,2,8,128]{3,2,1,0:T(8,128)S(1)}, f32[64,2,8,128]{3,2,1,0:T(8,128)S(1)}, u32[]{:S(2)}, u32[]{:S(2)}) %collective-permute-start.5) | collective-permute-done | bytes 524320 | tf_op jit(solution)/shard_map/ppermute | solution.py:284
  58.0 0.3 rest.1
  58.3 0.0 copy-start.4
  58.3 1.6 %all-to-all-done.1.x_ref = f32[32,3,8,128]{3,2,1,0:T(8,128)S(1)} async-done(((f32[32,3,8,128]{3,2,1,0:T(8,128)}), f32[32,3,8,128]{3,2,1,0:T(8,128)S(1)}, u32[]{:S(2)}, u32[]{:S(2)}) %all-to-all-start.1) | async-done | bytes 393248 | tf_op jit(solution)/shard_map/all_to_all | solution.py:275
  59.9 0.0 copy-done.4
  59.9 1.8 %middle.1 = f32[128,8,128]{2,1,0:T(8,128)S(1)} custom-call(f32[32,3,8,128]{3,2,1,0:T(8,128)S(1)} %all-to-all-done.1.x_ref, s32[16,128]{1,0:T(8,128)S(1)} %bitcast.10, bf16[512,256]{1,0:T(8,128)(2,1)S(1)} %get-tuple-element.28.h0, bf16[512,256]{1,0:T(8,128)(2,1)S(1)} %get-tuple-element.29.l0, bf16[2,512,384]{2,1,0:T(8,128)(2,1)S(1)} %get-tuple-element.30.h1, ...), custom_call_target="tpu_custom_call" | custom-call | tf_op jit(solution)/shard_map/middle/pallas_call | solution.py:263
  61.7 27.2 %all_to_all.15.x_ref = f32[128,8,128]{2,1,0:T(8,128)S(1)} all-to-all(f32[128,8,128]{2,1,0:T(8,128)S(1)} %middle.1), channel_id=1, replica_groups=mesh['x'=4,'c'=2,'h'=4,'l'=2,'z'=8] {'z','l','x','c'}, dimensions={0} | all-to-all | bytes 1048576 | tf_op jit(solution)/shard_map/all_to_all | solution.py:275
  88.8 1.6 %last.1 = (f32[1,32,2048]{2,1,0:T(8,128)}, f32[1,32,2048]{2,1,0:T(8,128)}) custom-call(f32[128,8,128]{2,1,0:T(8,128)S(1)} %all_to_all.15.x_ref, s32[16,128]{1,0:T(8,128)S(1)} %bitcast.9, bf16[512,256]{1,0:T(8,128)(2,1)S(1)} %get-tuple-element.28.h0, bf16[512,256]{1,0:T(8,128)(2,1)S(1)} %get-tuple-element.29.l0, ...), custom_call_target="tpu_custom_call" | custom-call | tf_op jit(solution)/shard_map/last/pallas_call | solution.py:263
  (1 shorter events, 0.0 us)
Async XLA Ops:
  0.6 0.8 copy-start
  2.2 17.3 %copy-start.1 = (f32[1,32,2048]{2,1,0:T(8,128)S(1)}, f32[1,32,2048]{2,1,0:T(8,128)}, u32[]{:S(2)}) copy-start(f32[1,32,2048]{2,1,0:T(8,128)} %f0.1) | copy-start | bytes 786436
  2.2 31.0 %copy-start.2 = (s32[32,2048]{1,0:T(8,128)S(1)}, s32[32,2048]{1,0:T(8,128)}, u32[]{:S(2)}) copy-start(s32[32,2048]{1,0:T(8,128)} %rate_ref.1) | copy-start | bytes 786436
  2.2 31.0 %copy-start.5 = (f32[16]{0:T(128)S(1)}, f32[16]{0:T(128)}, u32[]{:S(2)}) copy-start(f32[16]{0:T(128)} %table_ref.1) | copy-start | bytes 196
  2.2 36.1 %all-to-all-start = ((f32[64,16,128]{2,1,0:T(8,128)}), f32[64,16,128]{2,1,0:T(8,128)S(1)}, u32[]{:S(2)}, u32[]{:S(2)}) async-start(f32[64,16,128]{2,1,0:T(8,128)} %broadcast_in_dim.3), calls=%async_computation | async-start | bytes 1048576 | tf_op jit(solution)/shard_map/all_to_all | solution.py:275
  19.5 8.8 %collective-permute-start.1 = (f32[1,32,2048]{2,1,0:T(8,128)S(1)}, f32[1,32,2048]{2,1,0:T(8,128)S(1)}, u32[]{:S(2)}, u32[]{:S(2)}) collective-permute-start(f32[1,32,2048]{2,1,0:T(8,128)S(1)} %copy-done.1), channel_id=1, source_target_pairs={{0,128},{128,0},{256,384},{384,256},{1,129},{129,1},{257,385},{385... | collective-permute-start | bytes 786440 | tf_op jit(solution)/shard_map/ppermute | solution.py:281
  22.7 9.4 %collective-permute-start = (f32[1,32,2048]{2,1,0:T(8,128)S(1)}, f32[1,32,2048]{2,1,0:T(8,128)S(1)}, u32[]{:S(2)}, u32[]{:S(2)}) collective-permute-start(f32[1,32,2048]{2,1,0:T(8,128)S(1)} %copy-done.1), channel_id=1, source_target_pairs={{0,64},{64,0},{1,65},{65,1},{2,66},{66,2},{3,67},{67,3},{4,68},{68... | collective-permute-start | bytes 786440 | tf_op jit(solution)/shard_map/ppermute | solution.py:283
  28.3 4.9 %collective-permute-start.2 = (f32[1,32,2048]{2,1,0:T(8,128)S(1)}, f32[1,32,2048]{2,1,0:T(8,128)S(1)}, u32[]{:S(2)}, u32[]{:S(2)}) collective-permute-start(f32[1,32,2048]{2,1,0:T(8,128)S(1)} %collective-permute-done.1.f2), channel_id=1, source_target_pairs={{0,64},{64,0},{1,65},{65,1},{2,66},{66,2},{3,67},{67,3},{4,68},{68... | collective-permute-start | bytes 786440 | tf_op jit(solution)/shard_map/ppermute | solution.py:284
  34.0 7.4 %copy-start.3 = (s32[2048]{0:T(1024)S(1)}, s32[2048]{0:T(1024)}, u32[]{:S(2)}) copy-start(s32[2048]{0:T(1024)} %param.9) | copy-start | bytes 24580
  38.3 14.2 %collective-permute-start.4 = (f32[64,2,8,128]{3,2,1,0:T(8,128)S(1)}, f32[64,2,8,128]{3,2,1,0:T(8,128)S(1)}, u32[]{:S(2)}, u32[]{:S(2)}) collective-permute-start(f32[64,2,8,128]{3,2,1,0:T(8,128)S(1)} %bitcast.5), channel_id=1, source_target_pairs={{0,128},{128,0},{256,384},{384,256},{1,129},{129,1},{257,385},{385... | collective-permute-start | bytes 1572872 | tf_op jit(solution)/shard_map/ppermute | solution.py:281
  42.9 17.0 %all-to-all-start.1 = ((f32[32,3,8,128]{3,2,1,0:T(8,128)}), f32[32,3,8,128]{3,2,1,0:T(8,128)S(1)}, u32[]{:S(2)}, u32[]{:S(2)}) async-start(f32[32,3,8,128]{3,2,1,0:T(8,128)} %get-tuple-element.24), calls=%async_computation.1 | async-start | bytes 786432 | tf_op jit(solution)/shard_map/all_to_all | solution.py:275
  47.8 8.7 %collective-permute-start.3 = (f32[64,2,8,128]{3,2,1,0:T(8,128)S(1)}, f32[64,2,8,128]{3,2,1,0:T(8,128)S(1)}, u32[]{:S(2)}, u32[]{:S(2)}) collective-permute-start(f32[64,2,8,128]{3,2,1,0:T(8,128)S(1)} %bitcast.7), channel_id=1, source_target_pairs={{0,64},{64,0},{1,65},{65,1},{2,66},{66,2},{3,67},{67,3},{4,68},{68... | collective-permute-start | bytes 1572872 | tf_op jit(solution)/shard_map/ppermute | solution.py:283
  52.5 5.5 %collective-permute-start.5 = (f32[64,2,8,128]{3,2,1,0:T(8,128)S(1)}, f32[64,2,8,128]{3,2,1,0:T(8,128)S(1)}, u32[]{:S(2)}, u32[]{:S(2)}) collective-permute-start(f32[64,2,8,128]{3,2,1,0:T(8,128)S(1)} %collective-permute-done.4.m2), channel_id=1, source_target_pairs={{0,64},{64,0},{1,65},{65,1},{2,66},{66,2},{3,67},{67,3},{4,68},{68... | collective-permute-start | bytes 1572872 | tf_op jit(solution)/shard_map/ppermute | solution.py:284
  58.3 1.6 %copy-start.4 = (s32[2048]{0:T(1024)S(1)}, s32[2048]{0:T(1024)}, u32[]{:S(2)}) copy-start(s32[2048]{0:T(1024)} %param.10) | copy-start | bytes 24580
